TPU v7x, 32 devices: a whole 2x2x4 slice. The times are simulated.
32 devices in a mesh: rows: 8 (over y, x, core), band: 4 (over z).
Axes of the slice: x: 2, y: 2, z: 4, core: 2. Of those that a mesh axis runs over, the one named last changes fastest.
Arguments:
- pan_image: float32 [384, 12288], P('rows', 'band'), may hold values from -1 to 17
- vnir_bands: float32 [8, 96, 3072], P('band', 'rows'), may hold values from -13 to 13
- swir_bands: float32 [8, 32, 1024], P('band', 'rows'), may hold values from -12 to 12
Outputs:
- joined_vnir: float32 [8, 384, 12288], P(None, 'rows', 'band')
- joined_swir: float32 [8, 96, 3072], P(None, 'rows', 'band')
All inputs are finite; a program needn't handle non-finite values.
Results may differ from a plain program's by a relative error of at most 0.00023.
Values sent between devices are 32-bit elements; how exact they have to be, the bound alone decides.
No kernel may reach another device: no remote copies, remote signals or barrier semaphores. Data moves between devices by JAX's collectives and lax.ppermute only.
A program may use at most 192 MiB of HBM per device.

v0:
```python
import math

import jax
import jax.numpy as jnp
import numpy as np
from jax import lax
from jax.sharding import PartitionSpec as P

BANDS = 8
RATIO_V = 4
RATIO_S = 3
TAPS_V = 17
TAPS_S = 13


NYQUIST_GAIN = 0.29


def with_halo(block, sides, width):
    for axis, dim in sides:
        count = lax.axis_size(axis)
        forward = [(i, i + 1) for i in range(count - 1)]
        backward = [(target, source) for source, target in forward]
        low = lax.ppermute(
            lax.slice_in_dim(block, block.shape[dim] - width, None, axis=dim), axis, forward
        )
        high = lax.ppermute(lax.slice_in_dim(block, 0, width, axis=dim), axis, backward)
        block = jnp.concatenate([low, block, high], axis=dim)
    return block


def gauss_taps(upscale, kernel_len):
    spread = upscale * math.sqrt(-2.0 * math.log(NYQUIST_GAIN)) / math.pi
    radius = kernel_len // 2
    offsets = np.arange(-radius, radius + 1) * 1.0
    values = np.exp(-(offsets**2) / (2.0 * spread**2))
    return values / values.sum()


def cubic_weight(distance):
    distance = abs(distance)
    if distance <= 1.0:
        return 1.5 * distance**3 - 2.5 * distance**2 + 1.0
    if distance < 2.0:
        return -0.5 * distance**3 + 2.5 * distance**2 - 4.0 * distance + 2.0
    return 0.0


def cubic_table(upscale):
    weights = np.zeros((5, upscale))
    for phase_index in range(upscale):
        centre = (phase_index + 0.5) / upscale - 0.5
        first_tap = math.floor(centre)
        fraction = centre - first_tap
        for tap_index in range(-1, 3):
            weights[first_tap + tap_index + 2, phase_index] += cubic_weight(tap_index - fraction)
    return weights


def filter_axis(padded, kernel, along):
    length = padded.shape[along] - len(kernel) + 1
    running = float(kernel[0]) * lax.slice_in_dim(padded, 0, length, axis=along)
    for offset in range(1, len(kernel)):
        running = running + float(kernel[offset]) * lax.slice_in_dim(
            padded, offset, offset + length, axis=along
        )
    return running


def upsample_axis(padded, upscale, along):
    weights = cubic_table(upscale)
    length = padded.shape[along] - 4
    phases = []
    for phase_index in range(upscale):
        running = float(weights[0, phase_index]) * lax.slice_in_dim(padded, 0, length, axis=along)
        for offset in range(1, 5):
            running = running + float(weights[offset, phase_index]) * lax.slice_in_dim(
                padded, offset, offset + length, axis=along
            )
        phases.append(running)
    stacked = jnp.stack(phases, axis=along + 1)
    new_shape = padded.shape[:along] + (length * upscale,) + padded.shape[along + 1 :]
    return stacked.reshape(new_shape)


def upsample_columns(padded, upscale):
    weights = cubic_table(upscale)
    last = padded.ndim - 1
    length = padded.shape[last] - 4
    block = 128
    leading = padded.shape[:last]
    positions = np.arange(block)
    running = None
    for offset in range(5):
        table = np.zeros((block, block * upscale), np.float32)
        for phase_index in range(upscale):
            table[positions, positions * upscale + phase_index] = weights[offset, phase_index]
        piece = lax.slice_in_dim(padded, offset, offset + length, axis=last)
        piece = piece.reshape(leading + (length // block, block))
        term = jnp.einsum(
            "...kc,cf->...kf",
            piece,
            jnp.asarray(table, jnp.float32),
            precision=lax.Precision.HIGHEST,
            preferred_element_type=jnp.float32,
        )
        running = term if running is None else running + term
    return running.reshape(leading + (length * upscale,))


def moments(layers):
    flattened = layers.reshape(layers.shape[0], -1)
    products = jnp.dot(
        flattened, flattened.T, precision=lax.Precision.HIGHEST, preferred_element_type=jnp.float32
    )
    return (products, jnp.sum(flattened, axis=1))


def covariance(products, totals, pixels):
    averages = totals / pixels
    return products / pixels - averages[:, None] * averages[None, :]


def solve_spd(matrix, rhs):
    factor = jnp.linalg.cholesky(matrix)
    lower_sol = lax.linalg.triangular_solve(factor, rhs, left_side=True, lower=True)
    return lax.linalg.triangular_solve(
        factor, lower_sol, left_side=True, lower=True, transpose_a=True
    )


def first_gains(products, totals, pixels):
    cov_all = covariance(products, totals, pixels)
    inputs_cov = cov_all[:BANDS, :BANDS]
    cross_cov = cov_all[:BANDS, BANDS:]
    weights = solve_spd(inputs_cov, cross_cov)
    return cross_cov[:, 0] / jnp.sum(cross_cov[:, 0] * weights[:, 0])


def second_fit(products, totals, pixels):
    cov_all = covariance(products, totals, pixels)
    inputs_cov = cov_all[:BANDS, :BANDS]
    cross_cov = cov_all[:BANDS, BANDS:]
    target = jnp.mean(cross_cov, axis=1, keepdims=True)
    weights = solve_spd(inputs_cov, target)[:, 0]
    numerators = jnp.sum(weights[:, None] * cross_cov, axis=0)
    return (weights, numerators / jnp.sum(weights * target[:, 0]))


def local(pan_image, vnir_bands, swir_bands):
    groups = lax.axis_size("band")
    strips = lax.axis_size("rows")
    fine_pixels = pan_image.shape[0] * strips * pan_image.shape[1] * groups
    kernel_fine = gauss_taps(RATIO_V, TAPS_V)
    kernel_coarse = gauss_taps(RATIO_S, TAPS_S)
    radius_fine = TAPS_V // 2
    radius_coarse = TAPS_S // 2
    vnir_local, swir_local = (
        lax.all_to_all(vnir_bands, "band", split_axis=2, concat_axis=0, tiled=True),
        lax.all_to_all(swir_bands, "band", split_axis=2, concat_axis=0, tiled=True),
    )
    vnir_framed = with_halo(vnir_local, (("rows", 1), ("band", 2)), 2)
    vnir_up = upsample_columns(upsample_axis(vnir_framed, RATIO_V, 1), RATIO_V)
    swir_framed = with_halo(swir_local, (("rows", 1), ("band", 2)), 2)
    swir_up = upsample_columns(upsample_axis(swir_framed, RATIO_S, 1), RATIO_S)
    pan_framed = with_halo(pan_image, (("rows", 0), ("band", 1)), radius_fine)
    pan_low = filter_axis(filter_axis(pan_framed, kernel_fine, 0), kernel_fine, 1)
    products, totals = moments(jnp.concatenate([vnir_up, pan_low[None]], axis=0))
    products, totals = lax.psum((products, totals), ("rows", "band"))
    gain_bands = first_gains(products, totals, fine_pixels)
    joined_vnir = vnir_up + gain_bands[:, None, None] * (pan_image - pan_low)[None]
    synthetic = joined_vnir.reshape(
        BANDS, joined_vnir.shape[1] // RATIO_V, RATIO_V, joined_vnir.shape[2] // RATIO_V, RATIO_V
    ).mean(axis=(2, 4))
    synth_framed = with_halo(synthetic, (("rows", 1), ("band", 2)), radius_coarse)
    synthetic_low = filter_axis(filter_axis(synth_framed, kernel_coarse, 1), kernel_coarse, 2)
    products_two, totals_two = moments(jnp.concatenate([synthetic_low, swir_up], axis=0))
    products_two, totals_two = lax.psum((products_two, totals_two), ("rows", "band"))
    weights, shares = second_fit(products_two, totals_two, fine_pixels // 16)
    detail = jnp.einsum(
        "b,bij->ij", weights, synthetic - synthetic_low, precision=lax.Precision.HIGHEST
    )
    joined_swir = swir_up + shares[:, None, None] * detail[None]
    return (joined_vnir, joined_swir)


def solution(mesh):
    return jax.shard_map(
        local,
        mesh=mesh,
        in_specs=(P("rows", "band"), P("band", "rows", None), P("band", "rows", None)),
        out_specs=(P(None, "rows", "band"), P(None, "rows", "band")),
        check_vma=False,
    )
```

profile of v0, /device:TPU:0, one launch (start us, length us, event | category | flops | bytes accessed | tf_op | source)
XLA Modules:
  0.0 417.5 jit_solution(15703165427128953023)
XLA Ops:
  2.0 1.5 reshape.184
  3.4 11.8 %all_to_all.36 = f32[4,1,2048]{2,1,0:T(1,128)S(1)} all-to-all(f32[4,1,2048]{2,1,0:T(1,128)S(1)} %reshape.184), channel_id=1, replica_groups=mesh['rows'=8,'band'=4] {'band'}, dimensions={0} | all-to-all | bytes 65536 | tf_op jit(solution)/shard_map/all_to_all | solution.py:160
  16.4 1.6 reshape.185
  21.0 1.6 fusion.106
  22.7 1.9 collective-permute-done.9
  25.3 2.6 collective-permute-start.10
  30.5 5.4 %collective-permute-start.4 = (f32[8,3072]{1,0:T(8,128)}, f32[8,3072]{1,0:T(8,128)}, u32[]{:S(2)}, u32[]{:S(2)}) collective-permute-start(f32[8,3072]{1,0:T(8,128)} %get-tuple-element.23), channel_id=1, source_target_pairs={{0,4},{4,8},{8,12},{12,16},{16,20},{20,24},{24,28},{1,5},{5,9},{9,... | collective-permute-start | bytes 294920 | tf_op jit(solution)/shard_map/ppermute | solution.py:24
  35.9 2.9 copy.93
  38.8 5.8 %reshape.182 = f32[4,1,18432]{2,1,0:T(1,128)} reshape(f32[3072,2,12]{2,1,0:T(2,128)S(1)} %bitcast.175) | data formatting | bytes 589824
  44.6 4.3 %all-to-all-start = ((f32[4,1,18432]{2,1,0:T(1,128)}), f32[4,1,18432]{2,1,0:T(1,128)S(1)}, u32[]{:S(2)}, u32[]{:S(2)}) async-start(f32[4,1,18432]{2,1,0:T(1,128)} %reshape.182), calls=%async_computation | async-start | bytes 589824 | tf_op jit(solution)/shard_map/all_to_all | solution.py:159
  50.1 1.4 fusion.83
  51.5 1.4 convolution_add_fusion.3
  56.7 4.8 %collective-permute-start.6 = (f32[64,8]{1,0:T(8,128)S(1)}, f32[64,8]{1,0:T(8,128)S(1)}, u32[]{:S(2)}, u32[]{:S(2)}) collective-permute-start(f32[64,8]{1,0:T(8,128)S(1)} %get-tuple-element.19), channel_id=1, source_target_pairs={{0,1},{1,2},{2,3},{4,5},{5,6},{6,7},{8,9},{9,10},{10,11},{12,13},{... | collective-permute-start | bytes 6152 | tf_op jit(solution)/shard_map/ppermute | solution.py:24
  64.7 6.5 %reshape.183 = f32[3072,2,12]{2,1,0:T(2,128)} reshape(f32[4,18432]{1,0:T(4,128)S(1)} %reduce.5) | data formatting | bytes 589824
  71.2 4.0 copy.94
  75.4 2.3 collective-permute-start
  80.0 2.8 collective-permute-done.1
  82.9 4.2 %collective-permute-start.2 = (f32[8,16,2]{2,0,1:T(8,128)S(1)}, f32[8,16,2]{2,0,1:T(8,128)S(1)}, u32[]{:S(2)}, u32[]{:S(2)}) collective-permute-start(f32[8,16,2]{2,0,1:T(8,128)S(1)} %get-tuple-element.27), channel_id=1, source_target_pairs={{0,1},{1,2},{2,3},{4,5},{5,6},{6,7},{8,9},{9,10},{10,11},{12,13},{... | collective-permute-start | bytes 3080 | tf_op jit(solution)/shard_map/ppermute | solution.py:24
  87.1 1.5 collective-permute-start.3
  88.7 2.5 fusion.102
  92.4 1.4 copy.155
  93.8 21.2 %mul.429 = f32[12,4,768,4]{3,2,1,0:T(8,128)} reshape(f32[48,3072]{1,0:T(8,128)S(1)} %get-tuple-element.11) | data formatting | bytes 1179648 | tf_op jit(solution)/shard_map/mul | solution.py:171
  115.8 3.5 fusion.104
  119.3 1.4 reshape.181
  120.7 2.5 reshape.180
  123.2 2.5 reshape.179
  125.6 2.9 reshape.178
  129.9 6.1 %fusion.11 = f32[8,48,6,512]{3,1,2,0:T(8,128)S(1)} fusion(f32[128,512,1,1]{1,0,3,2:T(8,128)} %constant.156, f32[8,48,6,128]{3,2,0,1:T(8,128)} %reshape.177), kind=kOutput, calls=%fused_computation.20 | convolution fusion | flops 1811939328 | bytes 6160384 | tf_op jit(solution)/shard_map/...kc,cf->...kf/dot_general | solution.py:100
  136.1 4.6 %fusion.9 = f32[8,48,6,512]{3,1,2,0:T(8,128)S(1)} fusion(f32[128,512,1,1]{1,0,3,2:T(8,128)S(1)} %copy-done.14, f32[8,48,6,128]{3,2,0,1:T(8,128)S(1)} %copy-done.5), kind=kOutput, calls=%fused_computation.18 | convolution fusion | flops 1811939328 | bytes 6160384 | tf_op jit(solution)/shard_map/...kc,cf->...kf/dot_general | solution.py:100
  140.7 4.8 %fusion.7 = f32[8,48,6,512]{3,1,2,0:T(8,128)S(1)} fusion(f32[128,512,1,1]{1,0,3,2:T(8,128)S(1)} %copy-done.13, f32[8,48,6,128]{3,2,0,1:T(8,128)S(1)} %copy-done.4), kind=kOutput, calls=%fused_computation.16 | convolution fusion | flops 1811939328 | bytes 6160384 | tf_op jit(solution)/shard_map/...kc,cf->...kf/dot_general | solution.py:100
  145.5 4.6 %fusion.5 = f32[8,48,6,512]{3,1,2,0:T(8,128)S(1)} fusion(f32[128,512,1,1]{1,0,3,2:T(8,128)S(1)} %copy-done.12, f32[8,48,6,128]{3,2,0,1:T(8,128)S(1)} %copy-done.3), kind=kOutput, calls=%fused_computation.14 | convolution fusion | flops 1811939328 | bytes 6160384 | tf_op jit(solution)/shard_map/...kc,cf->...kf/dot_general | solution.py:100
  150.1 5.6 %add_add_fusion = f32[8,48,6,512]{3,1,2,0:T(8,128)S(1)} fusion(f32[8,48,6,512]{3,1,2,0:T(8,128)S(1)} %fusion.5, f32[8,48,6,512]{3,1,2,0:T(8,128)S(1)} %fusion.7, f32[8,48,6,512]{3,1,2,0:T(8,128)S(1)} %fusion.11, f32[8,48,6,512]{3,1,2,0:T(8,128)S(1)} %fusion.9, f32[128,512,1,1]{1,0,3,2:T(8,128)S(1)} %copy-done.11, f32[8,48,6,128]{3,2,0,1:T(8,128)S(1)} %reshape.181), kind=kOutput, calls=%fused_computation.7 | convolution fusion | flops 1816657920 | bytes 25034752 | tf_op jit(solution)/shard_map/...kc,cf->...kf/dot_general | solution.py:100
  155.7 2.2 copy-done
  157.9 5.6 %copy.106 = f32[8,48,6,512]{3,2,1,0:T(8,128)} copy(f32[8,48,6,512]{3,1,2,0:T(8,128)S(1)} %add_add_fusion) | data formatting | bytes 9437184 | tf_op jit(solution)/shard_map/add | solution.py:107
  163.5 38.0 %copy.122 = f32[8,48,6,512]{0,3,2,1:T(8,128)} copy(f32[8,48,6,512]{3,1,2,0:T(8,128)} %copy-done) | data formatting | bytes 9437184 | tf_op jit(solution)/shard_map/add | solution.py:107
  201.5 3.1 copy.154
  204.6 2.2 copy-done.1
  206.8 4.9 %copy.107 = f32[8,48,3072]{2,0,1:T(8,128)} copy(f32[8,48,3072]{2,1,0:T(8,128)S(1)} %bitcast.171) | data formatting | bytes 9437184 | tf_op jit(solution)/shard_map/reshape | solution.py:108
  211.6 7.4 %concatenate.49 = f32[8,147456]{1,0:T(8,128)} reshape(f32[8,48,6,512]{3,2,1,0:T(8,128)} %copy.106) | data formatting | bytes 9437184 | tf_op jit(solution)/shard_map/concatenate | solution.py:168
  219.1 15.1 %fusion.13 = f32[9,9]{0,1:T(8,128)S(1)} fusion(f32[1,48,3072]{2,0,1:T(1,128)S(1)} %copy-done.9, f32[8,48,3072]{2,0,1:T(8,128)} %copy.107), kind=kOutput, calls=%fused_computation.22 | convolution fusion | flops 144654336 | bytes 5308740 | tf_op jit(solution)/shard_map/dot_general | solution.py:113
  235.5 44.8 %all-reduce.1 = (f32[9,9]{0,1:T(8,128)S(1)}, f32[9]{0:T(128)S(1)}) all-reduce(f32[9,9]{0,1:T(8,128)S(1)} %fusion.13, f32[9]{0:T(128)S(1)} %maximum_reduce_fusion), channel_id=1, replica_groups=mesh['rows'=8,'band'=4] {'rows','band'}, use_global_device_ids=true, to_apply=%region_0.0 | all-reduce | flops 90 | bytes 720 | tf_op jit(solution)/shard_map/psum | solution.py:169
  284.7 59.6 %add_reduce_fusion = f32[8,12,768]{0,2,1:T(8,128)} fusion(f32[8,12,4,768,4]{0,4,3,2,1:T(4,128)} %bitcast.54, f32[12,4,768,4]{3,2,1,0:T(8,128)} %mul.429, f32[8]{0:T(128)S(1)} %divide_bitcast_fusion), kind=kLoop, calls=%fused_computation | loop fusion | flops 3465216 | bytes 5603360 | tf_op jit(solution)/shard_map/reduce_sum | solution.py:174
  344.3 3.1 copy.123
  348.7 1.5 collective-permute-start.13
  351.6 2.9 collective-permute-done.13
  354.6 3.4 collective-permute-start.14
  359.3 5.4 %multiply_add_fusion = f32[8,48,3072]{2,1,0:T(8,128)} fusion(f32[8,48,3072]{2,1,0:T(8,128)} %bitcast.172, f32[48,3072]{1,0:T(8,128)S(1)} %get-tuple-element.11, f32[8]{0:T(128)S(1)} %divide_bitcast_fusion), kind=kLoop, calls=%fused_computation.6 | loop fusion | flops 2359296 | bytes 10027040 | tf_op jit(solution)/shard_map/add | solution.py:171
  367.3 44.0 %all-reduce = (f32[16,16]{0,1:T(8,128)S(1)}, f32[16]{0:T(128)S(1)}) all-reduce(f32[16,16]{0,1:T(8,128)S(1)} %convolution_bitcast_fusion, f32[16]{0:T(128)S(1)} %maximum_reduce_fusion.1), channel_id=1, replica_groups=mesh['rows'=8,'band'=4] {'rows','band'}, use_global_device_ids=true, to_apply=%region_7.11 | all-reduce | flops 272 | bytes 2176 | tf_op jit(solution)/shard_map/psum | solution.py:178
  (134 shorter events, 41.0 us)
Async XLA Ops:
  0.6 35.3 %copy-start.10 = (f32[2,12,3072]{2,0,1:T(2,128)S(1)}, f32[2,12,3072]{2,0,1:T(2,128)}, u32[]{:S(2)}) copy-start(f32[2,12,3072]{2,0,1:T(2,128)} %param.19) | copy-start | bytes 884740
  18.4 4.2 %collective-permute-start.8 = (f32[8,2,256]{2,1,0:T(2,128)S(1)}, f32[8,2,256]{2,1,0:T(2,128)S(1)}, u32[]{:S(2)}, u32[]{:S(2)}) collective-permute-start(f32[8,2,256]{2,1,0:T(2,128)S(1)} %get-tuple-element.43), channel_id=1, source_target_pairs={{0,4},{4,8},{8,12},{12,16},{16,20},{20,24},{24,28},{1,5},{5,9},{9,... | collective-permute-start | bytes 49160 | tf_op jit(solution)/shard_map/ppermute | solution.py:24
  19.7 4.8 %collective-permute-start.9 = (f32[8,2,256]{2,1,0:T(2,128)S(1)}, f32[8,2,256]{2,1,0:T(2,128)S(1)}, u32[]{:S(2)}, u32[]{:S(2)}) collective-permute-start(f32[8,2,256]{2,1,0:T(2,128)S(1)} %get-tuple-element.44), channel_id=1, source_target_pairs={{4,0},{8,4},{12,8},{16,12},{20,16},{24,20},{28,24},{5,1},{9,5},{13... | collective-permute-start | bytes 49160 | tf_op jit(solution)/shard_map/ppermute | solution.py:27
  25.3 23.6 %collective-permute-start.10 = (f32[8,8,2]{2,1,0:T(8,128)}, f32[8,8,2]{2,1,0:T(8,128)S(1)}, u32[]{:S(2)}, u32[]{:S(2)}) collective-permute-start(f32[8,8,2]{2,1,0:T(8,128)} %get-tuple-element.41), channel_id=1, source_target_pairs={{0,1},{1,2},{2,3},{4,5},{5,6},{6,7},{8,9},{9,10},{10,11},{12,13},{... | collective-permute-start | bytes 1544 | tf_op jit(solution)/shard_map/ppermute | solution.py:24
  27.9 20.9 %collective-permute-start.11 = (f32[8,8,2]{2,1,0:T(8,128)}, f32[8,8,2]{2,1,0:T(8,128)}, u32[]{:S(2)}, u32[]{:S(2)}) collective-permute-start(f32[8,8,2]{2,1,0:T(8,128)} %get-tuple-element.42), channel_id=1, source_target_pairs={{1,0},{2,1},{3,2},{5,4},{6,5},{7,6},{9,8},{10,9},{11,10},{13,12},{... | collective-permute-start | bytes 1544 | tf_op jit(solution)/shard_map/ppermute | solution.py:27
  29.2 25.2 %collective-permute-start.5 = (f32[8,3072]{1,0:T(8,128)}, f32[8,3072]{1,0:T(8,128)}, u32[]{:S(2)}, u32[]{:S(2)}) collective-permute-start(f32[8,3072]{1,0:T(8,128)} %get-tuple-element.22), channel_id=1, source_target_pairs={{4,0},{8,4},{12,8},{16,12},{20,16},{24,20},{28,24},{5,1},{9,5},{13... | collective-permute-start | bytes 294920 | tf_op jit(solution)/shard_map/ppermute | solution.py:27
  30.5 22.9 %collective-permute-start.4 = (f32[8,3072]{1,0:T(8,128)}, f32[8,3072]{1,0:T(8,128)}, u32[]{:S(2)}, u32[]{:S(2)}) collective-permute-start(f32[8,3072]{1,0:T(8,128)} %get-tuple-element.23), channel_id=1, source_target_pairs={{0,4},{4,8},{8,12},{12,16},{16,20},{20,24},{24,28},{1,5},{5,9},{9,... | collective-permute-start | bytes 294920 | tf_op jit(solution)/shard_map/ppermute | solution.py:24
  44.6 8.4 %copy-start.17 = (f32[128,384,1,1]{1,0,3,2:T(8,128)S(1)}, f32[128,384,1,1]{1,0,3,2:T(8,128)}, u32[]{:S(2)}) copy-start(f32[128,384,1,1]{1,0,3,2:T(8,128)} %constant.163) | copy-start | bytes 589828
  44.6 9.8 %copy-start.6 = (f32[48,3072]{1,0:T(8,128)S(1)}, f32[48,3072]{1,0:T(8,128)}, u32[]{:S(2)}) copy-start(f32[48,3072]{1,0:T(8,128)} %param.18) | copy-start | bytes 1769476
  44.6 16.9 %copy-start.16 = (f32[128,384,1,1]{1,0,3,2:T(8,128)S(1)}, f32[128,384,1,1]{1,0,3,2:T(8,128)}, u32[]{:S(2)}) copy-start(f32[128,384,1,1]{1,0,3,2:T(8,128)} %constant.164) | copy-start | bytes 589828
  44.6 18.7 %all-to-all-start = ((f32[4,1,18432]{2,1,0:T(1,128)}), f32[4,1,18432]{2,1,0:T(1,128)S(1)}, u32[]{:S(2)}, u32[]{:S(2)}) async-start(f32[4,1,18432]{2,1,0:T(1,128)} %reshape.182), calls=%async_computation | async-start | bytes 589824 | tf_op jit(solution)/shard_map/all_to_all | solution.py:159
  55.4 7.3 %collective-permute-start.7 = (f32[64,8]{1,0:T(8,128)S(1)}, f32[64,8]{1,0:T(8,128)S(1)}, u32[]{:S(2)}, u32[]{:S(2)}) collective-permute-start(f32[64,8]{1,0:T(8,128)S(1)} %get-tuple-element.18), channel_id=1, source_target_pairs={{1,0},{2,1},{3,2},{5,4},{6,5},{7,6},{9,8},{10,9},{11,10},{13,12},{... | collective-permute-start | bytes 6152 | tf_op jit(solution)/shard_map/ppermute | solution.py:27
  56.7 6.2 %collective-permute-start.6 = (f32[64,8]{1,0:T(8,128)S(1)}, f32[64,8]{1,0:T(8,128)S(1)}, u32[]{:S(2)}, u32[]{:S(2)}) collective-permute-start(f32[64,8]{1,0:T(8,128)S(1)} %get-tuple-element.19), channel_id=1, source_target_pairs={{0,1},{1,2},{2,3},{4,5},{5,6},{6,7},{8,9},{9,10},{10,11},{12,13},{... | collective-permute-start | bytes 6152 | tf_op jit(solution)/shard_map/ppermute | solution.py:24
  75.4 4.6 %collective-permute-start = (f32[8,2,768]{2,0,1:T(8,128)S(1)}, f32[8,2,768]{2,0,1:T(8,128)S(1)}, u32[]{:S(2)}, u32[]{:S(2)}) collective-permute-start(f32[8,2,768]{2,0,1:T(8,128)S(1)} %get-tuple-element.32), channel_id=1, source_target_pairs={{0,4},{4,8},{8,12},{12,16},{16,20},{20,24},{24,28},{1,5},{5,9},{9,... | collective-permute-start | bytes 147464 | tf_op jit(solution)/shard_map/ppermute | solution.py:24
  78.7 4.1 collective-permute-start.1
  82.9 32.1 %collective-permute-start.2 = (f32[8,16,2]{2,0,1:T(8,128)S(1)}, f32[8,16,2]{2,0,1:T(8,128)S(1)}, u32[]{:S(2)}, u32[]{:S(2)}) collective-permute-start(f32[8,16,2]{2,0,1:T(8,128)S(1)} %get-tuple-element.27), channel_id=1, source_target_pairs={{0,1},{1,2},{2,3},{4,5},{5,6},{6,7},{8,9},{9,10},{10,11},{12,13},{... | collective-permute-start | bytes 3080 | tf_op jit(solution)/shard_map/ppermute | solution.py:24
  87.1 27.9 %collective-permute-start.3 = (f32[8,16,2]{2,0,1:T(8,128)S(1)}, f32[8,16,2]{2,0,1:T(8,128)S(1)}, u32[]{:S(2)}, u32[]{:S(2)}) collective-permute-start(f32[8,16,2]{2,0,1:T(8,128)S(1)} %get-tuple-element.28), channel_id=1, source_target_pairs={{1,0},{2,1},{3,2},{5,4},{6,5},{7,6},{9,8},{10,9},{11,10},{13,12},{... | collective-permute-start | bytes 3080 | tf_op jit(solution)/shard_map/ppermute | solution.py:27
  129.9 6.2 %copy-start.5 = (f32[8,48,6,128]{3,2,0,1:T(8,128)S(1)}, f32[8,48,6,128]{3,2,0,1:T(8,128)}, u32[]{:S(2)}) copy-start(f32[8,48,6,128]{3,2,0,1:T(8,128)} %reshape.178) | copy-start | bytes 3538948
  129.9 6.2 %copy-start.14 = (f32[128,512,1,1]{1,0,3,2:T(8,128)S(1)}, f32[128,512,1,1]{1,0,3,2:T(8,128)}, u32[]{:S(2)}) copy-start(f32[128,512,1,1]{1,0,3,2:T(8,128)} %constant.157) | copy-start | bytes 786436
  129.9 10.8 %copy-start.4 = (f32[8,48,6,128]{3,2,0,1:T(8,128)S(1)}, f32[8,48,6,128]{3,2,0,1:T(8,128)}, u32[]{:S(2)}) copy-start(f32[8,48,6,128]{3,2,0,1:T(8,128)} %reshape.179) | copy-start | bytes 3538948
  129.9 10.8 %copy-start.13 = (f32[128,512,1,1]{1,0,3,2:T(8,128)S(1)}, f32[128,512,1,1]{1,0,3,2:T(8,128)}, u32[]{:S(2)}) copy-start(f32[128,512,1,1]{1,0,3,2:T(8,128)} %constant.158) | copy-start | bytes 786436
  136.1 9.4 %copy-start.3 = (f32[8,48,6,128]{3,2,0,1:T(8,128)S(1)}, f32[8,48,6,128]{3,2,0,1:T(8,128)}, u32[]{:S(2)}) copy-start(f32[8,48,6,128]{3,2,0,1:T(8,128)} %reshape.180) | copy-start | bytes 3538948
  136.1 9.4 %copy-start.12 = (f32[128,512,1,1]{1,0,3,2:T(8,128)S(1)}, f32[128,512,1,1]{1,0,3,2:T(8,128)}, u32[]{:S(2)}) copy-start(f32[128,512,1,1]{1,0,3,2:T(8,128)} %constant.159) | copy-start | bytes 786436
  140.7 9.4 %copy-start.11 = (f32[128,512,1,1]{1,0,3,2:T(8,128)S(1)}, f32[128,512,1,1]{1,0,3,2:T(8,128)}, u32[]{:S(2)}) copy-start(f32[128,512,1,1]{1,0,3,2:T(8,128)} %constant.160) | copy-start | bytes 786436
  155.7 2.2 copy-start
  204.6 2.2 copy-start.1
  211.6 7.4 %copy-start.9 = (f32[1,48,3072]{2,0,1:T(1,128)S(1)}, f32[1,48,3072]{2,0,1:T(1,128)}, u32[]{:S(2)}) copy-start(f32[1,48,3072]{2,0,1:T(1,128)} %broadcast_in_dim.2) | copy-start | bytes 1769476
  219.1 15.1 %copy-start.2 = (f32[8,147456]{1,0:T(8,128)S(1)}, f32[8,147456]{1,0:T(8,128)}, u32[]{:S(2)}) copy-start(f32[8,147456]{1,0:T(8,128)} %concatenate.49) | copy-start | bytes 14155780
  219.1 15.1 %copy-start.7 = (f32[1,1,48,3072]{3,1,2,0:T(1,128)S(1)}, f32[1,1,48,3072]{3,1,2,0:T(1,128)}, u32[]{:S(2)}) copy-start(f32[1,1,48,3072]{3,1,2,0:T(1,128)} %copy.155) | copy-start | bytes 1769476
  344.3 6.0 %copy-start.8 = (f32[8,12,2,384]{3,1,2,0:T(8,128)S(1)}, f32[8,12,2,384]{3,1,2,0:T(8,128)}, u32[]{:S(2)}) copy-start(f32[8,12,2,384]{3,1,2,0:T(8,128)} %convolution_add_fusion.1) | copy-start | bytes 884740
  344.3 6.0 %copy-start.15 = (f32[128,384,1,1]{1,0,3,2:T(8,128)S(1)}, f32[128,384,1,1]{1,0,3,2:T(8,128)}, u32[]{:S(2)}) copy-start(f32[128,384,1,1]{1,0,3,2:T(8,128)} %constant.165) | copy-start | bytes 589828
  347.4 4.2 %collective-permute-start.12 = (f32[8,6,768]{2,0,1:T(8,128)S(1)}, f32[8,6,768]{2,0,1:T(8,128)S(1)}, u32[]{:S(2)}, u32[]{:S(2)}) collective-permute-start(f32[8,6,768]{2,0,1:T(8,128)S(1)} %get-tuple-element.29), channel_id=1, source_target_pairs={{0,4},{4,8},{8,12},{12,16},{16,20},{20,24},{24,28},{1,5},{5,9},{9,... | collective-permute-start | bytes 442376 | tf_op jit(solution)/shard_map/ppermute | solution.py:24
  348.7 5.8 %collective-permute-start.13 = (f32[8,6,768]{2,0,1:T(8,128)S(1)}, f32[8,6,768]{2,0,1:T(8,128)S(1)}, u32[]{:S(2)}, u32[]{:S(2)}) collective-permute-start(f32[8,6,768]{2,0,1:T(8,128)S(1)} %get-tuple-element.30), channel_id=1, source_target_pairs={{4,0},{8,4},{12,8},{16,12},{20,16},{24,20},{28,24},{5,1},{9,5},{13... | collective-permute-start | bytes 442376 | tf_op jit(solution)/shard_map/ppermute | solution.py:27
  354.6 10.1 %collective-permute-start.14 = (f32[8,24,6]{2,0,1:T(8,128)S(1)}, f32[8,24,6]{2,0,1:T(8,128)S(1)}, u32[]{:S(2)}, u32[]{:S(2)}) collective-permute-start(f32[8,24,6]{2,0,1:T(8,128)S(1)} %get-tuple-element.20), channel_id=1, source_target_pairs={{0,1},{1,2},{2,3},{4,5},{5,6},{6,7},{8,9},{9,10},{10,11},{12,13},{... | collective-permute-start | bytes 13832 | tf_op jit(solution)/shard_map/ppermute | solution.py:24
  358.0 6.7 %collective-permute-start.15 = (f32[8,24,6]{2,0,1:T(8,128)S(1)}, f32[8,24,6]{2,0,1:T(8,128)S(1)}, u32[]{:S(2)}, u32[]{:S(2)}) collective-permute-start(f32[8,24,6]{2,0,1:T(8,128)S(1)} %get-tuple-element.21), channel_id=1, source_target_pairs={{1,0},{2,1},{3,2},{5,4},{6,5},{7,6},{9,8},{10,9},{11,10},{13,12},{... | collective-permute-start | bytes 13832 | tf_op jit(solution)/shard_map/ppermute | solution.py:27
where the time goes:
time: 425 us; the launch traced here: 417 us
  local copies, waits for them, and re-layouts  135 us (32%)
  blocking collectives  101 us (24%)
  other arithmetic  83.2 us (20%)
  matrix products  48.7 us (11%)
  starting transfers between devices  40.3 us (9%)
  waiting for transfers between devices  7.71 us (2%)
    reduce_sum x1, other arithmetic, local(): synthetic = joined_vnir.reshape(BANDS, joined_vnir.shape[1] // RATIO_V, R...  59.6 us
    psum x1, blocking collectives, local(): products, totals = lax.psum((products, totals), ('rows', 'band'))  44.8 us
    psum x1, blocking collectives, local(): lax.psum((products_two, totals_two), ('rows', 'band'))  44 us
    add x4, local copies, waits for them, and re-layouts, upsample_columns(): running = term if running is None else running + term  43.9 us
    dot_general x10, matrix products, upsample_columns(): jnp.einsum('...kc,cf->...kf', piece, jnp.asarray(table, jnp.float32), pre...  30.6 us
    unnamed x47, local copies, waits for them, and re-layouts  26.4 us
    ppermute x8, starting transfers between devices, with_halo(): lax.ppermute(lax.slice_in_dim(block, block.shape[dim] - width, None, axis...  25.3 us
    mul x1, local copies, waits for them, and re-layouts, local(): gain_bands[:, None, None] * (pan_image - pan_low)[None]  21.2 us
  transfers between devices with their start and end apart: 17, of which 4 were waited for; matrix products, arithmetic and copies ran while one was open for 13% of the time, Pallas kernels for 0%

commit v1 on v0

v1 whole, which is shorter than its diff:
```python
import math

import jax
import jax.numpy as jnp
import ml_dtypes
import numpy as np
from jax import lax
from jax.experimental import pallas as pl
from jax.experimental.pallas import tpu as pltpu
from jax.sharding import PartitionSpec as P

BANDS = 8
RATIO_V = 4
RATIO_S = 3
TAPS_V = 17
TAPS_S = 13
NYQUIST_GAIN = 0.29
LANES = 128
HALF = 64
HALO = 8
F32 = jnp.float32
BF16 = jnp.bfloat16
VMEM_BYTES = 48 * 1024 * 1024


def gauss_taps(upscale, kernel_len):
    spread = upscale * math.sqrt(-2.0 * math.log(NYQUIST_GAIN)) / math.pi
    radius = kernel_len // 2
    offsets = np.arange(-radius, radius + 1) * 1.0
    values = np.exp(-(offsets**2) / (2.0 * spread**2))
    return values / values.sum()


def cubic_weight(distance):
    distance = abs(distance)
    if distance <= 1.0:
        return 1.5 * distance**3 - 2.5 * distance**2 + 1.0
    if distance < 2.0:
        return -0.5 * distance**3 + 2.5 * distance**2 - 4.0 * distance + 2.0
    return 0.0


def cubic_table(upscale):
    weights = np.zeros((5, upscale))
    for phase_index in range(upscale):
        centre = (phase_index + 0.5) / upscale - 0.5
        first_tap = math.floor(centre)
        fraction = centre - first_tap
        for tap_index in range(-1, 3):
            weights[first_tap + tap_index + 2, phase_index] += cubic_weight(tap_index - fraction)
    return weights


KF = gauss_taps(RATIO_V, TAPS_V)
KC = gauss_taps(RATIO_S, TAPS_S)
C4 = cubic_table(RATIO_V)
C3 = cubic_table(RATIO_S)
MEAN4 = C4.mean(axis=1)


def split(table):
    high = np.asarray(table, np.float64).astype(np.float32).astype(ml_dtypes.bfloat16)
    low = (np.asarray(table, np.float64) - high.astype(np.float64)).astype(np.float32)
    return np.stack([high, low.astype(ml_dtypes.bfloat16)])


def band_matrix(size, taps):
    radius = len(taps) // 2
    out = np.zeros((size, size))
    for row in range(size):
        for tap in range(-radius, radius + 1):
            if 0 <= row + tap < size:
                out[row, row + tap] = taps[tap + radius]
    return out


def row_tables(h):
    hc = h // RATIO_V
    mean = np.zeros((3 * hc, 3 * h))
    for row in range(3 * hc):
        mean[row, RATIO_V * row : RATIO_V * (row + 1)] = 1.0 / RATIO_V
    fine = band_matrix(3 * h, KF)
    low = band_matrix(3 * hc, KC)
    mean_fine = mean @ fine
    pad = -(-hc // 8) * 8

    def part(matrix, rows, cols):
        return matrix[rows, :][:, cols]

    def stacked(rows, cols, filt):
        a = mean if filt is None else filt @ mean
        c = mean_fine if filt is None else filt @ mean_fine
        return np.concatenate([part(a, rows, cols), -part(c, rows, cols)], axis=1)

    own = slice(h, 2 * h)
    tables = []
    for variant in range(3):
        keep = np.ones(3 * hc)
        if variant == 1:
            keep[:hc] = 0.0
        if variant == 2:
            keep[2 * hc :] = 0.0
        masked = low * keep[None, :]
        rows = []
        for filt in (None, masked):
            block = np.zeros((pad, 2 * h))
            block[:hc] = stacked(slice(hc, 2 * hc), own, filt)
            rows.append(block)
        for filt in (None, low):
            rows.append(stacked(slice(hc, hc + HALO), slice(0, h), filt))
        for filt in (None, low):
            rows.append(stacked(slice(2 * hc - HALO, 2 * hc), slice(2 * h, 3 * h), filt))
        tables.append(np.concatenate(rows, axis=0))
    coarse_rows = np.stack(tables)
    fine_rows = np.concatenate(
        [fine[h : 2 * h, h : 2 * h], fine[h : h + HALO, 0:h], fine[2 * h - HALO : 2 * h, 2 * h : 3 * h]],
        axis=0,
    )
    return coarse_rows, fine_rows


def up_rows(hc):
    out = np.zeros((RATIO_V * hc, hc + 4))
    for m in range(hc):
        for p in range(RATIO_V):
            out[RATIO_V * m + p, m : m + 5] = C4[:, p]
    return out


def column_tables():
    n = LANES
    fine = np.zeros((2 * n, n))
    mean = np.zeros((5 * n, n))
    mean_fine = np.zeros((5 * n, n))
    low = np.zeros((2 * n, n))
    pair = np.zeros((3, 2 * n, 2 * n))
    up4 = np.zeros((2 * n, RATIO_V * n))
    up3 = np.zeros((2 * n, RATIO_S * n))
    for c in range(n):
        for t in range(-(TAPS_V // 2), TAPS_V // 2 + 1):
            fine[c + HALF + t, c] += KF[t + TAPS_V // 2]
            for q in range(RATIO_V):
                mean_fine[HALF + RATIO_V * c + q + t, c] += KF[t + TAPS_V // 2] / RATIO_V
        for q in range(RATIO_V):
            mean[HALF + RATIO_V * c + q, c] = 1.0 / RATIO_V
        for t in range(-(TAPS_S // 2), TAPS_S // 2 + 1):
            low[c + HALF + t, c] += KC[t + TAPS_S // 2]
            for s in range(-2, 3):
                value = KC[t + TAPS_S // 2] * MEAN4[s + 2]
                pair[0, c + HALF + t + s, n + c] += value
                if c + t >= 0:
                    pair[1, c + HALF + t + s, n + c] += value
                if c + t < n:
                    pair[2, c + HALF + t + s, n + c] += value
        for s in range(-2, 3):
            pair[:, c + HALF + s, c] += MEAN4[s + 2]
            for p in range(RATIO_V):
                up4[c + HALF + s, RATIO_V * c + p] += C4[s + 2, p]
            for p in range(RATIO_S):
                up3[c + HALF + s, RATIO_S * c + p] += C3[s + 2, p]
    return dict(fine=fine, mean=mean, mean_fine=mean_fine, low=low, pair=pair, up4=up4, up3=up3)


def parts2(x):
    high = x.astype(BF16)
    return high, (x - high.astype(F32)).astype(BF16)


def dot(a, b):
    return jnp.dot(a, b, preferred_element_type=F32)


def dot3(x, w):
    return dot(x[0], w[0]) + (dot(x[1], w[0]) + dot(x[0], w[1]))


def lanes_of(x, start, size):
    return tuple(part[:, start : start + size] for part in x)


def call(kernel, out_shape, scratch=(), out_specs=None, **cost):
    extra = {} if out_specs is None else dict(out_specs=out_specs)
    return pl.pallas_call(
        kernel,
        out_shape=out_shape,
        scratch_shapes=list(scratch),
        compiler_params=pltpu.CompilerParams(vmem_limit_bytes=VMEM_BYTES),
        cost_estimate=pl.CostEstimate(transcendentals=0, **cost) if cost else None,
        **extra,
    )


def local(pan_image, vnir_bands, swir_bands):
    groups = lax.axis_size("band")
    strips = lax.axis_size("rows")
    h, w = pan_image.shape
    nb, hc, _ = vnir_bands.shape
    _, hs, swir_width = swir_bands.shape
    wc = w // RATIO_V
    ws = wc // RATIO_S
    wf = wc + LANES
    sf = ws + LANES
    rb = -(-(hc + hs) // 8) * 8
    pad = -(-hc // 8) * 8
    fine_tiles = w // LANES
    coarse_tiles = wc // LANES
    swir_tiles = ws // LANES
    per_block = wf // LANES
    strip_blocks = -(-(h // 8) // per_block)
    fine_pixels = h * strips * w * groups

    def shape(*dims):
        return jax.ShapeDtypeStruct(dims, F32)

    coarse_rows, fine_rows = row_tables(h)
    cols = column_tables()
    lift = up_rows(hc)
    gram = lift.T @ lift
    rise = lift.sum(axis=0)

    def going(d):
        return (["right"] if d == 1 else []) + (["left"] if d == groups - 1 else [])

    chunk_rows = [nb * rb + 8 * strip_blocks * len(going(d)) for d in range(groups)]

    def strip_place(d, side):
        return nb * rb + 8 * strip_blocks * going(d).index(side)

    def pack(pan_ref, vnir_ref, swir_ref, *rest):
        outs, (wide, swide) = rest[:groups], rest[groups:]
        me = lax.axis_index("band")
        full = vnir_ref.shape[2]
        wide[:, :, 0:LANES] = jnp.zeros((nb, hc, LANES), F32)
        wide[:, :, LANES + full : 2 * LANES + full] = jnp.zeros((nb, hc, LANES), F32)
        wide[:, :, LANES : LANES + full] = vnir_ref[...]
        swide[:, :, 0:LANES] = jnp.zeros((nb, hs, LANES), F32)
        swide[:, :, LANES + swir_width : 2 * LANES + swir_width] = jnp.zeros((nb, hs, LANES), F32)
        swide[:, :, LANES : LANES + swir_width] = swir_ref[...]
        for d in range(groups):
            peer = lax.rem(me + d, groups)
            for j in range(nb):
                win = wide[j, :, pl.ds(pl.multiple_of(peer * wc, LANES), wc + 2 * LANES)]
                outs[d][j * rb : j * rb + hc, :] = win[:, HALF : HALF + wf]
                swin = swide[j, :, pl.ds(pl.multiple_of(peer * ws, LANES), ws + 2 * LANES)]
                outs[d][j * rb + hc : j * rb + hc + hs, 0:sf] = swin[:, HALF : HALF + sf]
            for side in going(d):
                first = strip_place(d, side)
                edge = pan_ref[:, w - LANES : w] if side == "right" else pan_ref[:, 0:LANES]
                for t in range(h // 8):
                    row = first + 8 * (t // per_block)
                    lane = LANES * (t % per_block)
                    outs[d][row : row + 8, lane : lane + LANES] = edge[8 * t : 8 * t + 8]

    chunks = call(
        pack,
        tuple(shape(chunk_rows[d], wf) for d in range(groups)),
        [
            pltpu.VMEM((nb, hc, vnir_bands.shape[2] + 2 * LANES), F32),
            pltpu.VMEM((nb, hs, swir_width + 2 * LANES), F32),
        ],
    )(pan_image, vnir_bands, swir_bands)
    got = [chunks[0]] + [
        lax.ppermute(chunks[d], "band", [(i, (i + d) % groups) for i in range(groups)])
        for d in range(1, groups)
    ]

    pan_blocks = -(-w // wc)
    send_rows = HALO + 3 + pan_blocks
    w_fine = split(cols["fine"])
    w_mean = split(cols["mean"])
    w_mean_fine = split(cols["mean_fine"])
    r_coarse = split(coarse_rows)
    r_fine = split(fine_rows)
    r_fine = np.concatenate([r_fine[0], r_fine[1], r_fine[0]], axis=1)

    def assemble(pan_ref, wf_ref, wm_ref, wmf_ref, rc_ref, rf_ref, *rest):
        ins = rest[:groups]
        x_out, s_out, up_out, down_out, d_out, ld_out, low_out, stage = rest[groups:]
        me = lax.axis_index("band")
        row_id = lax.axis_index("rows")
        for d in range(groups):
            source = lax.rem(me - d + groups, groups)
            block = ins[d][0 : nb * rb, :].reshape(nb, rb, wf)
            stage[pl.ds(source * nb, nb)] = block
        x_all = jnp.swapaxes(stage[...], 0, 1)
        x_out[...] = x_all[0:hc]
        s_out[...] = x_all[hc : hc + hs, :, 0:sf]
        up_out[0:HALO] = x_all[hc - HALO : hc]
        down_out[0:HALO] = x_all[0:HALO]
        for out, first in ((up_out, hc + hs - 2), (down_out, hc)):
            out[HALO, :, 0:sf] = x_all[first, :, 0:sf]
            out[HALO, :, wf - sf : wf] = x_all[first + 1, :, 0:sf]

        def strip(d, side, empty):
            first = strip_place(d, side)
            pieces = []
            for t in range(h // 8):
                row = first + 8 * (t // per_block)
                lane = LANES * (t % per_block)
                pieces.append(ins[d][row : row + 8, lane : lane + LANES])
            whole = jnp.concatenate(pieces, axis=0)
            return jnp.where(empty, 0.0, whole)

        left = strip(1, "right", me == 0)
        right = strip(groups - 1, "left", me == groups - 1)
        framed = jnp.concatenate([left[:, HALF:], pan_ref[...], right[:, :HALF]], axis=1)
        panes = parts2(framed)
        variant = jnp.where(row_id == 0, 1, jnp.where(row_id == strips - 1, 2, 0))
        rc = (rc_ref[0, variant], rc_ref[1, variant])
        for k in range(coarse_tiles + 1):
            start = RATIO_V * LANES * k - 2 * LANES
            skip = max(0, -start)
            stop = min(5 * LANES, w + LANES - start)
            piece = lanes_of(panes, start + skip, stop - skip)
            wm = wm_ref[0, skip:stop, :]
            wmf = (wmf_ref[0, skip:stop, :], wmf_ref[1, skip:stop, :])
            means = dot(piece[0], wm) + dot(piece[1], wm)
            fines = dot3(piece, wmf)
            both = parts2(jnp.concatenate([means, fines], axis=0))
            rows = dot(rc[0], both[0]) + (dot(rc[0], both[1]) + dot(rc[1], both[0]))
            at = slice(LANES * k, LANES * (k + 1))
            d_out[:, at] = rows[0:pad]
            ld_out[:, at] = rows[pad : 2 * pad]
            up_out[HALO + 1, :, at] = rows[2 * pad : 2 * pad + 8]
            up_out[HALO + 2, :, at] = rows[2 * pad + 8 : 2 * pad + 16]
            down_out[HALO + 1, :, at] = rows[2 * pad + 16 : 2 * pad + 24]
            down_out[HALO + 2, :, at] = rows[2 * pad + 24 : 2 * pad + 32]
        wfine = (wf_ref[0], wf_ref[1])
        rf = rf_ref[...]
        for k in range(fine_tiles):
            piece = lanes_of(panes, LANES * k, 2 * LANES)
            col = parts2(dot3(piece, wfine))
            rows = dot(rf, jnp.concatenate([col[0], col[0], col[1]], axis=0))
            low_out[:, LANES * k : LANES * (k + 1)] = rows[0:h]
            place = HALO + 3 + (LANES * k) // wc
            lane = (LANES * k) % wc
            up_out[place, :, lane : lane + LANES] = rows[h : h + HALO]
            down_out[place, :, lane : lane + LANES] = rows[h + HALO : h + 2 * HALO]

    x_loc, s_loc, up_send, down_send, d_own, ld_own, low_own = call(
        assemble,
        (
            shape(hc, BANDS, wf),
            shape(hs, BANDS, sf),
            shape(send_rows, BANDS, wf),
            shape(send_rows, BANDS, wf),
            shape(pad, wf),
            shape(pad, wf),
            shape(h, w),
        ),
        [pltpu.VMEM((BANDS, rb, wf), F32)],
    )(pan_image, w_fine, w_mean, w_mean_fine, r_coarse, r_fine, *got)
    from_low = lax.ppermute(up_send, "rows", [(i, i + 1) for i in range(strips - 1)])
    from_high = lax.ppermute(down_send, "rows", [(i + 1, i) for i in range(strips - 1)])

    w_low = split(cols["low"])
    w_pair = split(cols["pair"])
    w_up4 = split(cols["up4"])
    w_up3 = split(cols["up3"])
    r_adj = split(lift.T)
    r_adj = np.concatenate([r_adj[0], r_adj[0], r_adj[0], r_adj[1], r_adj[1]], axis=1)

    def moments(
        pan_ref, x_ref, s_ref, lo_ref, hi_ref, d_ref, ld_ref, low_ref,
        wl_ref, wp_ref, w4_ref, w3_ref, ra_ref,
        mom_out, y_out, diff_out, ugap_out, dgap_out, s_out,
        both, ulow, q_ref,
    ):
        me = lax.axis_index("band")
        row_id = lax.axis_index("rows")

        def x_row(r):
            if r < 0:
                return lo_ref[HALO + r]
            if r >= hc:
                return hi_ref[r - hc]
            return x_ref[r]

        frame = jnp.concatenate([x_row(r) for r in range(-2, hc + 2)], axis=0)
        frame = parts2(frame)
        w4 = (w4_ref[0], w4_ref[1])
        for k in range(coarse_tiles):
            up = dot3(lanes_of(frame, LANES * k, 2 * LANES), w4)
            for q in range(RATIO_V):
                y_out[RATIO_V * k + q] = up[:, LANES * q : LANES * (q + 1)]

        ra = ra_ref[...]
        psum = jnp.zeros((8, LANES), F32)
        psq = jnp.zeros((8, LANES), F32)
        for k in range(fine_tiles):
            at = slice(LANES * k, LANES * (k + 1))
            low = low_ref[:, at]
            place = HALO + 3 + (LANES * k) // wc
            lane = (LANES * k) % wc
            top = low[0:HALO] + lo_ref[place, :, lane : lane + LANES]
            end = low[h - HALO : h] + hi_ref[place, :, lane : lane + LANES]
            low = jnp.concatenate([top, low[HALO : h - HALO], end], axis=0)
            diff_out[k] = pan_ref[:, at] - low
            p1 = low.astype(BF16)
            rest = low - p1.astype(F32)
            p2 = rest.astype(BF16)
            p3 = (rest - p2.astype(F32)).astype(BF16)
            q_ref[k] = dot(ra, jnp.concatenate([p1, p2, p3, p1, p2], axis=0))
            for t in range(h // 8):
                tile = low[8 * t : 8 * t + 8]
                psum += tile
                psq += tile * tile

        def tile_step(k, carry):
            accs = list(carry[:BANDS])
            accp, accv = carry[BANDS], carry[BANDS + 1]
            ys = [y_out[k, pl.ds(8 * m, 8), :] for m in range(hc + 4)]
            for m in range(hc + 4):
                z = None
                for other in range(hc + 4):
                    if gram[m, other] != 0.0:
                        term = float(gram[m, other]) * ys[other]
                        z = term if z is None else z + term
                for i in range(BANDS):
                    accs[i] = accs[i] + z * y_out[k, pl.ds(8 * m + i, 1), :]
                accp = accp + ys[m] * q_ref[k, pl.ds(m, 1), :]
                accv = accv + float(rise[m]) * ys[m]
            return tuple(accs) + (accp, accv)

        zero = jnp.zeros((8, LANES), F32)
        first = lax.fori_loop(0, fine_tiles, tile_step, (zero,) * (BANDS + 2))

        below = jnp.where(row_id > 0, 1.0, 0.0).astype(F32)
        above = jnp.where(row_id < strips - 1, 1.0, 0.0).astype(F32)
        reach = TAPS_S // 2
        means = []
        for r in range(-reach, hc + reach):
            value = float(MEAN4[2]) * x_row(r)
            for t in (1, 2):
                value = value + float(MEAN4[2 + t]) * (x_row(r - t) + x_row(r + t))
            if r < 0:
                value = value * below
            if r >= hc:
                value = value * above
            means.append(value)
        lows = []
        for r in range(hc):
            centre = r + reach
            value = float(KC[reach]) * means[centre]
            for t in range(1, reach + 1):
                value = value + float(KC[reach + t]) * (means[centre - t] + means[centre + t])
            lows.append(value)
        u_rows = parts2(jnp.concatenate(means[reach : reach + hc], axis=0))
        l_rows = parts2(jnp.concatenate(lows, axis=0))
        left = jnp.where(me == 0, 1, 0)
        right = jnp.where(me == groups - 1, 2, 0)
        for k in range(coarse_tiles):
            which = left if k == 0 else (right if k == coarse_tiles - 1 else 0)
            wp = (wp_ref[0, which], wp_ref[1, which])
            mean_k = dot3(lanes_of(u_rows, LANES * k, 2 * LANES), tuple(p[:, :LANES] for p in wp))
            low_k = dot3(lanes_of(l_rows, LANES * k, 2 * LANES), tuple(p[:, LANES:] for p in wp))
            at = slice(LANES * k, LANES * (k + 1))
            ulow[:, at] = low_k
            ugap_out[:, at] = mean_k - low_k

        column = lax.broadcasted_iota(jnp.int32, (1, wf), 1) - HALF + me * wc
        inside = jnp.where((column >= 0) & (column < groups * wc), 1.0, 0.0).astype(F32)
        detail = []
        for index, ref in ((HALO + 1, d_ref), (HALO + 2, ld_ref)):
            both[...] = ref[...]
            both[0:HALO] = both[0:HALO] + lo_ref[index]
            both[hc - HALO : hc] = both[hc - HALO : hc] + hi_ref[index]
            detail.append(both[...])
        dlow_rows = parts2(detail[1] * inside)
        wl = (wl_ref[0], wl_ref[1])
        dlow = jnp.concatenate(
            [dot3(lanes_of(dlow_rows, LANES * k, 2 * LANES), wl) for k in range(coarse_tiles)], axis=1
        )
        dgap_out[...] = detail[0][:, HALF : HALF + wc] - dlow
        both[:, 0:wc] = dlow

        s_rows = [lo_ref[HALO, :, 0:sf], lo_ref[HALO, :, wf - sf : wf]]
        s_rows += [s_ref[r] for r in range(hs)]
        s_rows += [hi_ref[HALO, :, 0:sf], hi_ref[HALO, :, wf - sf : wf]]
        s_parts = parts2(jnp.concatenate(s_rows, axis=0))
        w3 = (w3_ref[0], w3_ref[1])
        s_cols = jnp.concatenate(
            [dot3(lanes_of(s_parts, LANES * k, 2 * LANES), w3) for k in range(swir_tiles)], axis=1
        )
        for m in range(hs):
            for p in range(RATIO_S):
                value = None
                for t in range(5):
                    if C3[t, p] != 0.0:
                        term = float(C3[t, p]) * s_cols[8 * (m + t) : 8 * (m + t) + 8]
                        value = term if value is None else value + term
                s_out[RATIO_S * m + p] = value

        ll = [zero] * BANDS
        cross = [zero] * BANDS
        ld = ls = sd = ss = dd = ds = zero
        for r in range(hc):
            for k in range(coarse_tiles):
                at = slice(LANES * k, LANES * (k + 1))
                u = ulow[8 * r : 8 * r + 8, at]
                s = s_out[r, :, at]
                dl = jnp.broadcast_to(both[r : r + 1, at], (8, LANES))
                for i in range(BANDS):
                    ll[i] = ll[i] + u * ulow[8 * r + i : 8 * r + i + 1, at]
                    cross[i] = cross[i] + u * s_out[r, i : i + 1, at]
                ld = ld + u * dl
                sd = sd + s * dl
                ls = ls + u
                ss = ss + s
                dd = dd + dl * dl
                ds = ds + dl

        lane = lax.broadcasted_iota(jnp.int32, (8, LANES), 1)
        columns = ll + cross + [ld, ls, sd, ss, dd, ds]
        columns += [zero] * (32 - len(columns))
        columns += list(first)
        table = zero
        for index, acc in enumerate(columns):
            if acc is not zero:
                table = jnp.where(lane == index, jnp.sum(acc, axis=1, keepdims=True), table)
        for index, acc in ((42, psq), (43, psum)):
            total = jnp.sum(jnp.sum(acc, axis=0, keepdims=True), axis=1, keepdims=True)
            table = jnp.where(lane == index, total, table)
        mom_out[...] = table

    mom, y_up, diff, ugap, dgap, s_up = call(
        moments,
        (
            shape(8, LANES),
            shape(fine_tiles, 8 * (hc + 4), LANES),
            shape(fine_tiles, h, LANES),
            shape(8 * hc, wc),
            shape(pad, wc),
            shape(hc, BANDS, wc),
        ),
        [
            pltpu.VMEM((pad, wf), F32),
            pltpu.VMEM((8 * hc, wc), F32),
            pltpu.VMEM((fine_tiles, hc + 4, LANES), F32),
        ],
    )(
        pan_image, x_loc, s_loc, from_low, from_high, d_own, ld_own, low_own,
        w_low, w_pair, w_up4, w_up3, r_adj,
    )
    devices = groups * strips
    spread = jnp.broadcast_to(mom[None], (devices,) + mom.shape)
    sums = lax.all_to_all(spread, ("rows", "band"), split_axis=0, concat_axis=0, tiled=True)

    def finish(sums_ref, y_ref, diff_ref, ugap_ref, dgap_ref, s_ref, vnir_out, swir_out, tiles, sems):
        lane = lax.broadcasted_iota(jnp.int32, (8, LANES), 1)
        sub = lax.broadcasted_iota(jnp.int32, (8, LANES), 0)
        eye = lane == sub
        total = sums_ref[0]
        for index in range(1, devices):
            total = total + sums_ref[index]

        def column(x, index):
            return jnp.broadcast_to(x[:, index : index + 1], (8, LANES))

        def across(col):
            return jnp.sum(jnp.where(eye, col, 0.0), axis=0, keepdims=True)

        def down(x):
            return jnp.sum(x, axis=0, keepdims=True)

        def solve(matrix, rhs):
            work = jnp.where(lane == 8, rhs, matrix)
            for k in range(BANDS):
                pivot_row = work[k : k + 1, :] / column(work, k)[k : k + 1, :]
                other = work - column(work, k) * pivot_row
                work = jnp.where(sub == k, pivot_row, other)
            return column(work, 8)

        n1 = float(fine_pixels)
        mean_v = column(total, 41) / n1
        mean_p = column(total, 43) / n1
        cov_v = pltpu.roll(total, LANES - 32, 1) / n1 - mean_v * across(mean_v)
        cov_p = column(total, 40) / n1 - mean_v * mean_p
        fit = solve(cov_v, cov_p)
        gain = cov_p / down(cov_p * fit)

        def tile_step(k, carry):
            for m in range(hc):
                ys = [y_ref[k, pl.ds(8 * (m + t), 8), :] for t in range(5)]
                for p in range(RATIO_V):
                    r = RATIO_V * m + p
                    value = gain * diff_ref[k, pl.ds(r, 1), :]
                    for t in range(5):
                        if C4[t, p] != 0.0:
                            value = value + float(C4[t, p]) * ys[t]
                    tiles[k, pl.ds(r, 8, stride=h), :] = value
            pltpu.make_async_copy(
                tiles.at[k], vnir_out.at[:, pl.ds(pl.multiple_of(LANES * k, LANES), LANES)], sems.at[k]
            ).start()
            return carry

        lax.fori_loop(0, fine_tiles, tile_step, 0)

        n2 = float(fine_pixels // (RATIO_V * RATIO_V))
        mean_l = column(total, 17) / n2
        mean_s = column(total, 19) / n2
        mean_d = column(total, 21) / n2
        cov_ll = total / n2 - mean_l * across(mean_l)
        cov_ls = pltpu.roll(total, LANES - 8, 1) / n2 - mean_l * across(mean_s)
        cov_ld = column(total, 16) / n2 - mean_l * mean_d
        cov_sd = column(total, 18) / n2 - mean_s * mean_d
        cov_dd = column(total, 20) / n2 - mean_d * mean_d
        gain_row = across(gain)
        a2 = cov_ll + gain * across(cov_ld) + cov_ld * gain_row + gain * gain_row * cov_dd
        b2 = cov_ls + gain * across(cov_sd)
        b2 = jnp.where(lane < BANDS, b2, 0.0)
        target = jnp.broadcast_to(jnp.sum(b2, axis=1, keepdims=True) / BANDS, (8, LANES))
        fit2 = solve(a2, target)
        numer = down(fit2 * b2)
        share_row = numer / down(fit2 * target)
        share = jnp.sum(jnp.where(eye, jnp.broadcast_to(share_row, (8, LANES)), 0.0), axis=1, keepdims=True)
        scale = down(fit2 * gain)[:, 0:1]
        fit_col = fit2[:, 0:1]
        for r in range(hc):
            seen = jnp.sum(fit_col * ugap_ref[8 * r : 8 * r + 8, :], axis=0, keepdims=True)
            seen = seen + scale * dgap_ref[r : r + 1, :]
            swir_out[:, r, :] = s_ref[r] + share * seen

        def drain(k, carry):
            pltpu.make_async_copy(
                tiles.at[k], vnir_out.at[:, pl.ds(pl.multiple_of(LANES * k, LANES), LANES)], sems.at[k]
            ).wait()
            return carry

        lax.fori_loop(0, fine_tiles, drain, 0)

    joined_vnir, joined_swir = call(
        finish,
        (shape(BANDS * h, w), shape(BANDS, hc, wc)),
        [pltpu.VMEM((fine_tiles, BANDS * h, LANES), F32), pltpu.SemaphoreType.DMA((fine_tiles,))],
        out_specs=(pl.BlockSpec(memory_space=pl.ANY), pl.BlockSpec(memory_space=pltpu.VMEM)),
    )(sums, y_up, diff, ugap, dgap, s_up)
    return joined_vnir.reshape(BANDS, h, w), joined_swir


def solution(mesh):
    return jax.shard_map(
        local,
        mesh=mesh,
        in_specs=(P("rows", "band"), P("band", "rows", None), P("band", "rows", None)),
        out_specs=(P(None, "rows", "band"), P(None, "rows", "band")),
        check_vma=False,
    )
```

time: 425 us -> 74.1 us (0.17); the launches traced: 417 us -> 73.4 us
  local copies, waits for them, and re-layouts: 135 us -> 14.4 us
  other arithmetic: 83.2 us -> 0 us
  blocking collectives: 101 us -> 18.9 us
  matrix products: 48.7 us -> 0 us
  starting transfers between devices: 40.3 us -> 9.37 us
  Pallas kernels: 0 us -> 15.8 us
  waiting for transfers between devices: 7.71 us -> 14.2 us
    psum x2 -> x0, blocking collectives: 88.8 us -> none  [the longest x1 44.8 us: local(): products, totals = lax.psum((products, totals), ('rows', 'band'))]
    reduce_sum x5 -> x0, other arithmetic: 61.3 us -> none  [the longest x1 59.6 us: local(): synthetic = joined_vnir.reshape(BANDS, joined_vnir.shape[1] // RATIO_V, R...]
    dot_general x13 -> x0, matrix products: 46.9 us -> none  [the longest x10 30.6 us: upsample_columns(): jnp.einsum('...kc,cf->...kf', piece, jnp.asarray(table, jnp.float32), pre...]
    add x4 -> x0, local copies, waits for them, and re-layouts: 43.9 us -> none  [upsample_columns(): running = term if running is None else running + term]
    ppermute x16 -> x5, starting transfers between devices: 36.1 us -> 9.37 us  [the longest x3 6.11 us: local(): lax.ppermute(chunks[d], 'band', [(i, (i + d) % groups) for i in range(gro...]
    mul x1 -> x0, local copies, waits for them, and re-layouts: 21.2 us -> none  [local(): gain_bands[:, None, None] * (pan_image - pan_low)[None]]
    reshape x9 -> x0, local copies, waits for them, and re-layouts: 18.9 us -> none  [the longest x6 10.7 us: upsample_columns(): piece = piece.reshape(leading + (length // block, block))]
    pallas_call x0 -> x4, Pallas kernels: none -> 15.8 us  [the longest x1 5.9 us: local(): call(assemble, (shape(hc, BANDS, wf), shape(hs, BANDS, sf), shape(send_ro...]
  transfers between devices with their start and end apart: 17 -> 5, of which waited for: 4 -> 3; matrix products, arithmetic and copies ran while one was open for 13% -> 0% of each run, Pallas kernels for 0% -> 0%
where the time goes in v1:
time: 74.1 us; the launch traced here: 73.4 us
  blocking collectives  18.9 us (26%)
  Pallas kernels  15.8 us (21%)
  local copies, waits for them, and re-layouts  14.4 us (19%)
  waiting for transfers between devices  14.2 us (19%)
  starting transfers between devices  9.37 us (13%)
    all_to_all x1, blocking collectives, local(): lax.all_to_all(spread, ('rows', 'band'), split_axis=0, concat_axis=0, til...  18.9 us
    unnamed x28, local copies, waits for them, and re-layouts  14.4 us
    ppermute x3, waiting for transfers between devices, local(): lax.ppermute(chunks[d], 'band', [(i, (i + d) % groups) for i in range(gro...  10.7 us
    ppermute x3, starting transfers between devices, local(): lax.ppermute(chunks[d], 'band', [(i, (i + d) % groups) for i in range(gro...  6.11 us
    pallas_call x1, Pallas kernels, local(): call(assemble, (shape(hc, BANDS, wf), shape(hs, BANDS, sf), shape(send_ro...  5.9 us
    pallas_call x1, Pallas kernels, local(): call(moments, (shape(8, LANES), shape(fine_tiles, 8 * (hc + 4), LANES), s...  5.48 us
    pallas_call x1, Pallas kernels, local(): call(finish, (shape(BANDS * h, w), shape(BANDS, hc, wc)), [pltpu.VMEM((fi...  4.1 us
    ppermute x1, waiting for transfers between devices, local(): lax.ppermute(down_send, 'rows', [(i + 1, i) for i in range(strips - 1)])  3.37 us
  transfers between devices with their start and end apart: 5, of which 3 were waited for; matrix products, arithmetic and copies ran while one was open for 0% of the time, Pallas kernels for 0%

profile of v1, /device:TPU:0, one launch (start us, length us, event | category | flops | bytes accessed | tf_op | source)
XLA Modules:
  0.0 73.4 jit_solution(12440181821642546420)
XLA Ops:
  0.6 1.1 %copy.15.vnir_ref = f32[2,12,3072]{2,1,0:T(8,128)S(1)} copy(f32[2,12,3072]{2,0,1:T(2,128)} %param.14) | data formatting | bytes 589824 | tf_op args[1]
  1.7 0.0 copy-start
  1.7 1.1 %copy-done = f32[48,3072]{1,0:T(8,128)S(1)} copy-done((f32[48,3072]{1,0:T(8,128)S(1)}, f32[48,3072]{1,0:T(8,128)}, u32[]{:S(2)}) %copy-start) | copy-done | bytes 589848
  2.8 0.0 copy-start.11
  2.8 0.8 %copy-done.11 = f32[2,4,1024]{2,1,0:T(4,128)S(1)} copy-done((f32[2,4,1024]{2,1,0:T(4,128)S(1)}, f32[2,4,1024]{2,1,0:T(4,128)}, u32[]{:S(2)}) %copy-start.11) | copy-done | bytes 32792
  3.5 0.3 shard_map.140
  3.8 3.1 %collective-permute-start = (f32[40,896]{1,0:T(8,128)S(1)}, f32[40,896]{1,0:T(8,128)S(1)}, u32[]{:S(2)}, u32[]{:S(2)}) collective-permute-start(f32[40,896]{1,0:T(8,128)S(1)} %get-tuple-element.22), channel_id=1, source_target_pairs={{0,1},{1,2},{2,3},{3,0},{4,5},{5,6},{6,7},{7,4},{8,9},{9,10},{10,1... | collective-permute-start | bytes 430088 | tf_op jit(solution)/shard_map/ppermute | solution.py:263
  6.9 2.1 %collective-permute-start.2 = (f32[40,896]{1,0:T(8,128)S(1)}, f32[40,896]{1,0:T(8,128)S(1)}, u32[]{:S(2)}, u32[]{:S(2)}) collective-permute-start(f32[40,896]{1,0:T(8,128)S(1)} %get-tuple-element.24), channel_id=1, source_target_pairs={{0,3},{1,0},{2,1},{3,2},{4,7},{5,4},{6,5},{7,6},{8,11},{9,8},{10,9... | collective-permute-start | bytes 430088 | tf_op jit(solution)/shard_map/ppermute | solution.py:263
  9.0 0.9 %collective-permute-start.1 = (f32[32,896]{1,0:T(8,128)S(1)}, f32[32,896]{1,0:T(8,128)S(1)}, u32[]{:S(2)}, u32[]{:S(2)}) collective-permute-start(f32[32,896]{1,0:T(8,128)S(1)} %get-tuple-element.23), channel_id=1, source_target_pairs={{0,2},{1,3},{2,0},{3,1},{4,6},{5,7},{6,4},{7,5},{8,10},{9,11},{10,... | collective-permute-start | bytes 344072 | tf_op jit(solution)/shard_map/ppermute | solution.py:263
  9.9 10.7 %collective-permute-done.1.rest_2_ = f32[32,896]{1,0:T(8,128)S(1)} collective-permute-done((f32[32,896]{1,0:T(8,128)S(1)}, f32[32,896]{1,0:T(8,128)S(1)}, u32[]{:S(2)}, u32[]{:S(2)}) %collective-permute-start.1) | collective-permute-done | bytes 114720 | tf_op jit(solution)/shard_map/ppermute | solution.py:263
  20.6 0.0 collective-permute-done.rest_1_
  20.6 0.0 collective-permute-done.2.rest_3_
  20.7 0.0 copy-start.5
  20.7 1.0 %copy-done.5 = bf16[2,640,128]{2,1,0:T(8,128)(2,1)S(1)} copy-done((bf16[2,640,128]{2,1,0:T(8,128)(2,1)S(1)}, bf16[2,640,128]{2,1,0:T(8,128)(2,1)}, u32[]{:S(2)}) %copy-start.5) | copy-done | bytes 327704
  21.6 0.0 copy-start.6
  21.6 1.0 %copy-done.6 = bf16[2,640,128]{2,1,0:T(8,128)(2,1)S(1)} copy-done((bf16[2,640,128]{2,1,0:T(8,128)(2,1)S(1)}, bf16[2,640,128]{2,1,0:T(8,128)(2,1)}, u32[]{:S(2)}) %copy-start.6) | copy-done | bytes 327704
  22.6 0.0 copy-start.8
  22.6 0.9 %copy-done.8 = bf16[2,256,128]{2,1,0:T(8,128)(2,1)S(1)} copy-done((bf16[2,256,128]{2,1,0:T(8,128)(2,1)S(1)}, bf16[2,256,128]{2,1,0:T(8,128)(2,1)}, u32[]{:S(2)}) %copy-start.8) | copy-done | bytes 131096
  23.5 0.0 copy-start.9
  23.5 0.9 %copy-done.9 = bf16[2,3,64,96]{3,2,1,0:T(8,128)(2,1)S(1)} copy-done((bf16[2,3,64,96]{3,2,1,0:T(8,128)(2,1)S(1)}, bf16[2,3,64,96]{3,2,1,0:T(8,128)(2,1)}, u32[]{:S(2)}) %copy-start.9) | copy-done | bytes 73752
  24.4 0.0 copy-start.10
  24.4 0.8 %copy-done.10 = bf16[64,144]{1,0:T(8,128)(2,1)S(1)} copy-done((bf16[64,144]{1,0:T(8,128)(2,1)S(1)}, bf16[64,144]{1,0:T(8,128)(2,1)}, u32[]{:S(2)}) %copy-start.10) | copy-done | bytes 18456
  25.2 5.9 %shard_map.141 = (f32[12,8,896]{2,1,0:T(8,128)S(1)}, f32[4,8,384]{2,1,0:T(8,128)S(1)}, f32[15,8,896]{2,1,0:T(8,128)S(1)}, f32[15,8,896]{2,1,0:T(8,128)S(1)}, f32...) custom-call(f32[48,3072]{1,0:T(8,128)S(1)} %copy-done, bf16[2,256,128]{2,1,0:T(8,128)(2,1)S(1)} %copy-done.8, ...), custom_call_target="tpu_custom_call" | custom-call | tf_op jit(solution)/shard_map/pallas_call | solution.py:340
  31.1 2.0 %collective-permute-start.3 = (f32[15,8,896]{2,1,0:T(8,128)S(1)}, f32[15,8,896]{2,1,0:T(8,128)S(1)}, u32[]{:S(2)}, u32[]{:S(2)}) collective-permute-start(f32[15,8,896]{2,1,0:T(8,128)S(1)} %get-tuple-element.27), channel_id=1, source_target_pairs={{0,4},{4,8},{8,12},{12,16},{16,20},{20,24},{24,28},{1,5},{5,9},{9,... | collective-permute-start | bytes 1290248 | tf_op jit(solution)/shard_map/ppermute | solution.py:353
  33.0 1.3 %collective-permute-start.4 = (f32[15,8,896]{2,1,0:T(8,128)S(1)}, f32[15,8,896]{2,1,0:T(8,128)S(1)}, u32[]{:S(2)}, u32[]{:S(2)}) collective-permute-start(f32[15,8,896]{2,1,0:T(8,128)S(1)} %get-tuple-element.28), channel_id=1, source_target_pairs={{4,0},{8,4},{12,8},{16,12},{20,16},{24,20},{28,24},{5,1},{9,5},{13... | collective-permute-start | bytes 1290248 | tf_op jit(solution)/shard_map/ppermute | solution.py:354
  34.3 0.1 collective-permute-done.3.lo_ref
  34.4 3.4 %collective-permute-done.4.hi_ref = f32[15,8,896]{2,1,0:T(8,128)S(1)} collective-permute-done((f32[15,8,896]{2,1,0:T(8,128)S(1)}, f32[15,8,896]{2,1,0:T(8,128)S(1)}, u32[]{:S(2)}, u32[]{:S(2)}) %collective-permute-start.4) | collective-permute-done | bytes 430112 | tf_op jit(solution)/shard_map/ppermute | solution.py:354
  37.8 0.0 copy-start.2
  37.8 1.1 %copy-done.2 = bf16[2,3,256,256]{3,2,1,0:T(8,128)(2,1)S(1)} copy-done((bf16[2,3,256,256]{3,2,1,0:T(8,128)(2,1)S(1)}, bf16[2,3,256,256]{3,2,1,0:T(8,128)(2,1)}, u32[]{:S(2)}) %copy-start.2) | copy-done | bytes 786456
  38.9 0.0 copy-start.3
  38.9 1.0 %copy-done.3 = bf16[2,256,512]{2,1,0:T(8,128)(2,1)S(1)} copy-done((bf16[2,256,512]{2,1,0:T(8,128)(2,1)S(1)}, bf16[2,256,512]{2,1,0:T(8,128)(2,1)}, u32[]{:S(2)}) %copy-start.3) | copy-done | bytes 524312
  39.9 0.0 copy-start.4
  39.9 1.0 %copy-done.4 = bf16[2,256,384]{2,1,0:T(8,128)(2,1)S(1)} copy-done((bf16[2,256,384]{2,1,0:T(8,128)(2,1)S(1)}, bf16[2,256,384]{2,1,0:T(8,128)(2,1)}, u32[]{:S(2)}) %copy-start.4) | copy-done | bytes 393240
  40.9 0.0 copy-start.7
  40.9 0.9 %copy-done.7 = bf16[2,256,128]{2,1,0:T(8,128)(2,1)S(1)} copy-done((bf16[2,256,128]{2,1,0:T(8,128)(2,1)S(1)}, bf16[2,256,128]{2,1,0:T(8,128)(2,1)}, u32[]{:S(2)}) %copy-start.7) | copy-done | bytes 131096
  41.8 0.0 copy-start.12
  41.8 0.7 copy-done.12
  42.5 5.5 %shard_map.142 = (f32[8,128]{1,0:T(8,128)S(1)}, f32[24,128,128]{2,1,0:T(8,128)}, f32[24,48,128]{2,1,0:T(8,128)S(1)}, f32[96,768]{1,0:T(8,128)S(1)}, f32[16,768]{1,0:T(8,128)S(1)}, /*index=5*/f32[12,8,768]{2,1,0:T(8,128)S(1)}) custom-call(f32[48,3072]{1,0:T(8,128)S(1)} %copy-done, f32[12,8,896]{2,1,0:T(8,128)S(1)} %get-tuple-element.25.x_ref, ...), custom_call_target="tpu_custom_call" | custom-call | tf_op jit(solution)/shard_map/pallas_call | solution.py:526
  48.0 18.9 %all_to_all.5.sums_ref = f32[32,8,128]{2,1,0:T(8,128)S(1)} all-to-all(f32[32,8,128]{2,1,0:T(8,128)S(1)} %broadcast_in_dim.2), channel_id=1, replica_groups=mesh['rows'=8,'band'=4] {'rows','band'}, dimensions={0} | all-to-all | bytes 262144 | tf_op jit(solution)/shard_map/all_to_all | solution.py:547
  67.0 0.0 copy-start.1
  67.0 1.4 %copy-done.1 = f32[24,128,128]{2,1,0:T(8,128)S(1)} copy-done((f32[24,128,128]{2,1,0:T(8,128)S(1)}, f32[24,128,128]{2,1,0:T(8,128)}, u32[]{:S(2)}) %copy-start.1) | copy-done | bytes 1572888
  68.4 4.1 %shard_map.143 = (f32[384,3072]{1,0:T(8,128)}, f32[8,12,768]{2,1,0:T(8,128)S(1)}) custom-call(f32[32,8,128]{2,1,0:T(8,128)S(1)} %all_to_all.5.sums_ref, f32[24,128,128]{2,1,0:T(8,128)S(1)} %copy-done.1, f32[24,48,128]{2,1,0:T(8,128)S(1)} %get-tuple-element.34.diff_ref, f32[96,768]{1,0:T(8,128)S(1)} %get-tuple-element.35.ugap_ref, ...), custom_call_target="tpu_custom_call" | custom-call | tf_op jit(solution)/shard_map/pallas_call | solution.py:632
  72.5 0.9 %copy.16 = f32[8,12,768]{2,0,1:T(8,128)} copy(f32[8,12,768]{2,1,0:T(8,128)S(1)} %get-tuple-element.41) | data formatting | bytes 589824
  (1 shorter events, 0.0 us)
Async XLA Ops:
  1.7 1.1 %copy-start = (f32[48,3072]{1,0:T(8,128)S(1)}, f32[48,3072]{1,0:T(8,128)}, u32[]{:S(2)}) copy-start(f32[48,3072]{1,0:T(8,128)} %pan_ref.5) | copy-start | bytes 1769476
  2.8 0.8 %copy-start.11 = (f32[2,4,1024]{2,1,0:T(4,128)S(1)}, f32[2,4,1024]{2,1,0:T(4,128)}, u32[]{:S(2)}) copy-start(f32[2,4,1024]{2,1,0:T(4,128)} %swir_ref.1) | copy-start | bytes 98308
  3.8 16.9 %collective-permute-start = (f32[40,896]{1,0:T(8,128)S(1)}, f32[40,896]{1,0:T(8,128)S(1)}, u32[]{:S(2)}, u32[]{:S(2)}) collective-permute-start(f32[40,896]{1,0:T(8,128)S(1)} %get-tuple-element.22), channel_id=1, source_target_pairs={{0,1},{1,2},{2,3},{3,0},{4,5},{5,6},{6,7},{7,4},{8,9},{9,10},{10,1... | collective-permute-start | bytes 430088 | tf_op jit(solution)/shard_map/ppermute | solution.py:263
  6.9 13.8 %collective-permute-start.2 = (f32[40,896]{1,0:T(8,128)S(1)}, f32[40,896]{1,0:T(8,128)S(1)}, u32[]{:S(2)}, u32[]{:S(2)}) collective-permute-start(f32[40,896]{1,0:T(8,128)S(1)} %get-tuple-element.24), channel_id=1, source_target_pairs={{0,3},{1,0},{2,1},{3,2},{4,7},{5,4},{6,5},{7,6},{8,11},{9,8},{10,9... | collective-permute-start | bytes 430088 | tf_op jit(solution)/shard_map/ppermute | solution.py:263
  9.0 11.7 %collective-permute-start.1 = (f32[32,896]{1,0:T(8,128)S(1)}, f32[32,896]{1,0:T(8,128)S(1)}, u32[]{:S(2)}, u32[]{:S(2)}) collective-permute-start(f32[32,896]{1,0:T(8,128)S(1)} %get-tuple-element.23), channel_id=1, source_target_pairs={{0,2},{1,3},{2,0},{3,1},{4,6},{5,7},{6,4},{7,5},{8,10},{9,11},{10,... | collective-permute-start | bytes 344072 | tf_op jit(solution)/shard_map/ppermute | solution.py:263
  20.7 1.0 %copy-start.5 = (bf16[2,640,128]{2,1,0:T(8,128)(2,1)S(1)}, bf16[2,640,128]{2,1,0:T(8,128)(2,1)}, u32[]{:S(2)}) copy-start(bf16[2,640,128]{2,1,0:T(8,128)(2,1)} %constant.22.clone.wmf_ref) | copy-start | bytes 983044
  21.6 1.0 %copy-start.6 = (bf16[2,640,128]{2,1,0:T(8,128)(2,1)S(1)}, bf16[2,640,128]{2,1,0:T(8,128)(2,1)}, u32[]{:S(2)}) copy-start(bf16[2,640,128]{2,1,0:T(8,128)(2,1)} %constant.21.clone.wm_ref) | copy-start | bytes 983044
  22.6 0.9 %copy-start.8 = (bf16[2,256,128]{2,1,0:T(8,128)(2,1)S(1)}, bf16[2,256,128]{2,1,0:T(8,128)(2,1)}, u32[]{:S(2)}) copy-start(bf16[2,256,128]{2,1,0:T(8,128)(2,1)} %constant.20.clone.wf_ref) | copy-start | bytes 393220
  23.5 0.9 %copy-start.9 = (bf16[2,3,64,96]{3,2,1,0:T(8,128)(2,1)S(1)}, bf16[2,3,64,96]{3,2,1,0:T(8,128)(2,1)}, u32[]{:S(2)}) copy-start(bf16[2,3,64,96]{3,2,1,0:T(8,128)(2,1)} %constant.23.clone.rc_ref) | copy-start | bytes 221188
  24.4 0.8 %copy-start.10 = (bf16[64,144]{1,0:T(8,128)(2,1)S(1)}, bf16[64,144]{1,0:T(8,128)(2,1)}, u32[]{:S(2)}) copy-start(bf16[64,144]{1,0:T(8,128)(2,1)} %constant.24.clone.rf_ref) | copy-start | bytes 55300
  31.1 3.3 %collective-permute-start.3 = (f32[15,8,896]{2,1,0:T(8,128)S(1)}, f32[15,8,896]{2,1,0:T(8,128)S(1)}, u32[]{:S(2)}, u32[]{:S(2)}) collective-permute-start(f32[15,8,896]{2,1,0:T(8,128)S(1)} %get-tuple-element.27), channel_id=1, source_target_pairs={{0,4},{4,8},{8,12},{12,16},{16,20},{20,24},{24,28},{1,5},{5,9},{9,... | collective-permute-start | bytes 1290248 | tf_op jit(solution)/shard_map/ppermute | solution.py:353
  33.0 4.7 %collective-permute-start.4 = (f32[15,8,896]{2,1,0:T(8,128)S(1)}, f32[15,8,896]{2,1,0:T(8,128)S(1)}, u32[]{:S(2)}, u32[]{:S(2)}) collective-permute-start(f32[15,8,896]{2,1,0:T(8,128)S(1)} %get-tuple-element.28), channel_id=1, source_target_pairs={{4,0},{8,4},{12,8},{16,12},{20,16},{24,20},{28,24},{5,1},{9,5},{13... | collective-permute-start | bytes 1290248 | tf_op jit(solution)/shard_map/ppermute | solution.py:354
  37.8 1.1 %copy-start.2 = (bf16[2,3,256,256]{3,2,1,0:T(8,128)(2,1)S(1)}, bf16[2,3,256,256]{3,2,1,0:T(8,128)(2,1)}, u32[]{:S(2)}) copy-start(bf16[2,3,256,256]{3,2,1,0:T(8,128)(2,1)} %constant.26.clone.wp_ref) | copy-start | bytes 2359300
  38.9 1.0 %copy-start.3 = (bf16[2,256,512]{2,1,0:T(8,128)(2,1)S(1)}, bf16[2,256,512]{2,1,0:T(8,128)(2,1)}, u32[]{:S(2)}) copy-start(bf16[2,256,512]{2,1,0:T(8,128)(2,1)} %constant.27.clone.w4_ref) | copy-start | bytes 1572868
  39.9 1.0 %copy-start.4 = (bf16[2,256,384]{2,1,0:T(8,128)(2,1)S(1)}, bf16[2,256,384]{2,1,0:T(8,128)(2,1)}, u32[]{:S(2)}) copy-start(bf16[2,256,384]{2,1,0:T(8,128)(2,1)} %constant.28.clone.w3_ref) | copy-start | bytes 1179652
  40.9 0.9 %copy-start.7 = (bf16[2,256,128]{2,1,0:T(8,128)(2,1)S(1)}, bf16[2,256,128]{2,1,0:T(8,128)(2,1)}, u32[]{:S(2)}) copy-start(bf16[2,256,128]{2,1,0:T(8,128)(2,1)} %constant.25.clone.wl_ref) | copy-start | bytes 393220
  41.8 0.7 copy-start.12
  67.0 1.4 %copy-start.1 = (f32[24,128,128]{2,1,0:T(8,128)S(1)}, f32[24,128,128]{2,1,0:T(8,128)}, u32[]{:S(2)}) copy-start(f32[24,128,128]{2,1,0:T(8,128)} %get-tuple-element.33.y_ref) | copy-start | bytes 4718596

commit v2 on v1

v2 whole, which is shorter than its diff:
```python
import math

import jax
import jax.numpy as jnp
import ml_dtypes
import numpy as np
from jax import lax
from jax.experimental import pallas as pl
from jax.experimental.pallas import tpu as pltpu
from jax.sharding import PartitionSpec as P

BANDS = 8
RATIO_V = 4
RATIO_S = 3
TAPS_V = 17
TAPS_S = 13
NYQUIST_GAIN = 0.29
LANES = 128
HALF = 64
REACH = 32
HALO = 8
F32 = jnp.float32
BF16 = jnp.bfloat16
VMEM_BYTES = 24 * 1024 * 1024
VMEM_MOST = 56 * 1024 * 1024


def gauss_taps(upscale, kernel_len):
    spread = upscale * math.sqrt(-2.0 * math.log(NYQUIST_GAIN)) / math.pi
    radius = kernel_len // 2
    offsets = np.arange(-radius, radius + 1) * 1.0
    values = np.exp(-(offsets**2) / (2.0 * spread**2))
    return values / values.sum()


def cubic_weight(distance):
    distance = abs(distance)
    if distance <= 1.0:
        return 1.5 * distance**3 - 2.5 * distance**2 + 1.0
    if distance < 2.0:
        return -0.5 * distance**3 + 2.5 * distance**2 - 4.0 * distance + 2.0
    return 0.0


def cubic_table(upscale):
    weights = np.zeros((5, upscale))
    for phase_index in range(upscale):
        centre = (phase_index + 0.5) / upscale - 0.5
        first_tap = math.floor(centre)
        fraction = centre - first_tap
        for tap_index in range(-1, 3):
            weights[first_tap + tap_index + 2, phase_index] += cubic_weight(tap_index - fraction)
    return weights


KF = gauss_taps(RATIO_V, TAPS_V)
KC = gauss_taps(RATIO_S, TAPS_S)
C4 = cubic_table(RATIO_V)
C3 = cubic_table(RATIO_S)
MEAN4 = C4.mean(axis=1)


def split(table):
    high = np.asarray(table, np.float64).astype(np.float32).astype(ml_dtypes.bfloat16)
    low = (np.asarray(table, np.float64) - high.astype(np.float64)).astype(np.float32)
    return np.stack([high, low.astype(ml_dtypes.bfloat16)])


def band_matrix(size, taps):
    radius = len(taps) // 2
    out = np.zeros((size, size))
    for row in range(size):
        for tap in range(-radius, radius + 1):
            if 0 <= row + tap < size:
                out[row, row + tap] = taps[tap + radius]
    return out


def row_tables(h):
    hc = h // RATIO_V
    mean = np.zeros((3 * hc, 3 * h))
    for row in range(3 * hc):
        mean[row, RATIO_V * row : RATIO_V * (row + 1)] = 1.0 / RATIO_V
    fine = band_matrix(3 * h, KF)
    low = band_matrix(3 * hc, KC)
    mean_fine = mean @ fine
    pad = -(-hc // 8) * 8

    def part(matrix, rows, cols):
        return matrix[rows, :][:, cols]

    def stacked(rows, cols, filt):
        a = mean if filt is None else filt @ mean
        c = mean_fine if filt is None else filt @ mean_fine
        return np.concatenate([part(a, rows, cols), -part(c, rows, cols)], axis=1)

    own = slice(h, 2 * h)
    tables = []
    for variant in range(3):
        keep = np.ones(3 * hc)
        if variant == 1:
            keep[:hc] = 0.0
        if variant == 2:
            keep[2 * hc :] = 0.0
        masked = low * keep[None, :]
        rows = []
        for filt in (None, masked):
            block = np.zeros((pad, 2 * h))
            block[:hc] = stacked(slice(hc, 2 * hc), own, filt)
            rows.append(block)
        for filt in (None, low):
            rows.append(stacked(slice(hc, hc + HALO), slice(0, h), filt))
        for filt in (None, low):
            rows.append(stacked(slice(2 * hc - HALO, 2 * hc), slice(2 * h, 3 * h), filt))
        tables.append(np.concatenate(rows, axis=0))
    coarse_rows = np.stack(tables)
    fine_rows = np.concatenate(
        [fine[h : 2 * h, h : 2 * h], fine[h : h + HALO, 0:h], fine[2 * h - HALO : 2 * h, 2 * h : 3 * h]],
        axis=0,
    )
    return coarse_rows, fine_rows


def up_rows(hc):
    out = np.zeros((RATIO_V * hc, hc + 4))
    for m in range(hc):
        for p in range(RATIO_V):
            out[RATIO_V * m + p, m : m + 5] = C4[:, p]
    return out


def column_tables():
    n = LANES
    fine = np.zeros((4 * n, 2 * n))
    mean = np.zeros((6 * n, n))
    mean_fine = np.zeros((6 * n, n))
    low = np.zeros((2 * n, n))
    pair = np.zeros((3, 2 * n, 2 * n))
    up4 = np.zeros((2 * n, RATIO_V * n))
    up3 = np.zeros((2 * n, RATIO_S * n))
    for c in range(2 * n):
        for t in range(-(TAPS_V // 2), TAPS_V // 2 + 1):
            fine[n + c + t, c] += KF[t + TAPS_V // 2]
    for c in range(n):
        for q in range(RATIO_V):
            mean[n + RATIO_V * c + q, c] = 1.0 / RATIO_V
            for t in range(-(TAPS_V // 2), TAPS_V // 2 + 1):
                mean_fine[n + RATIO_V * c + q + t, c] += KF[t + TAPS_V // 2] / RATIO_V
        for t in range(-(TAPS_S // 2), TAPS_S // 2 + 1):
            low[c + HALF + t, c] += KC[t + TAPS_S // 2]
            for s in range(-2, 3):
                value = KC[t + TAPS_S // 2] * MEAN4[s + 2]
                pair[0, c + HALF + t + s, n + c] += value
                if c + t >= 0:
                    pair[1, c + HALF + t + s, n + c] += value
                if c + t < n:
                    pair[2, c + HALF + t + s, n + c] += value
        for s in range(-2, 3):
            pair[:, c + HALF + s, c] += MEAN4[s + 2]
            for p in range(RATIO_V):
                up4[c + HALF + s, RATIO_V * c + p] += C4[s + 2, p]
            for p in range(RATIO_S):
                up3[c + HALF + s, RATIO_S * c + p] += C3[s + 2, p]
    return dict(fine=fine, mean=mean, mean_fine=mean_fine, low=low, pair=pair, up4=up4, up3=up3)


def stack_tables(tables):
    wide = 2 * LANES
    pieces, place, top = [], {}, 0
    for name, value in tables.items():
        stack = value.reshape((-1,) + value.shape[-2:])
        height, width = stack.shape[1:]
        starts = []
        for lane in range(0, width, wide):
            part = stack[:, :, lane : lane + wide]
            starts.append((top, part.shape[2]))
            piece = np.zeros((stack.shape[0] * height, wide), ml_dtypes.bfloat16)
            piece[:, : part.shape[2]] = part.reshape(-1, part.shape[2])
            pieces.append(piece)
            top += piece.shape[0]
        place[name] = (starts, height, width)
    return np.concatenate(pieces, axis=0), place


def parts2(x):
    high = x.astype(BF16)
    return high, (x - high.astype(F32)).astype(BF16)


def dot(a, b):
    return jnp.dot(a, b, preferred_element_type=F32)


def dot3(x, w):
    return dot(x[0], w[0]) + (dot(x[1], w[0]) + dot(x[0], w[1]))


def windows(x, starts, size):
    return tuple(jnp.concatenate([part[:, a : a + size] for a in starts], axis=0) for part in x)


def blocks(x, count):
    rows = x.shape[0] // count
    return jnp.concatenate([x[rows * k : rows * (k + 1)] for k in range(count)], axis=1)


def call(kernel, out_shape, scratch=(), cost=(0, 0), room=VMEM_BYTES, **specs):
    return pl.pallas_call(
        kernel,
        out_shape=out_shape,
        scratch_shapes=list(scratch),
        compiler_params=pltpu.CompilerParams(vmem_limit_bytes=room),
        cost_estimate=pl.CostEstimate(flops=cost[0], bytes_accessed=cost[1], transcendentals=0),
        **specs,
    )


ANY = pl.BlockSpec(memory_space=pl.ANY)
VMEM = pl.BlockSpec(memory_space=pltpu.VMEM)


def local(pan_image, vnir_bands, swir_bands):
    groups = lax.axis_size("band")
    strips = lax.axis_size("rows")
    h, w = pan_image.shape
    nb, hc, full = vnir_bands.shape
    _, hs, sfull = swir_bands.shape
    wc = w // RATIO_V
    ws = wc // RATIO_S
    wf = wc + LANES
    sf = ws + LANES
    pad = -(-hc // 8) * 8
    fine_tiles = w // LANES
    coarse_tiles = wc // LANES
    frame_tiles = coarse_tiles + 1
    swir_tiles = ws // LANES
    fine_pixels = h * strips * w * groups
    pairs = w // (2 * LANES)
    middle = frame_tiles - 2
    margin = RATIO_V * LANES

    def shape(*dims):
        return jax.ShapeDtypeStruct(dims, F32)

    coarse_rows, fine_rows = row_tables(h)
    cols = column_tables()
    lift = up_rows(hc)
    gram = lift.T @ lift
    rise = lift.sum(axis=0)

    swir_rows = -(-hs // RATIO_S)
    at_swir = hc
    at_edge = hc + swir_rows
    at_strip = at_edge + 1
    piece = REACH * (h // 8)
    per_row = wc // piece
    strip_rows = -(-(8 // nb) // per_row)

    def going(d):
        return (["right"] if d == 1 else []) + (["left"] if d == groups - 1 else [])

    def strip_place(d, side):
        return at_strip + strip_rows * going(d).index(side)

    chunk_rows = [at_strip + strip_rows * len(going(d)) for d in range(groups)]

    def pack(pan_ref, vnir_ref, swir_ref, *rest):
        outs, (wide, swide, edges, sems) = rest[:groups], rest[groups:]
        me = lax.axis_index("band")
        copies = [
            pltpu.make_async_copy(vnir_ref, wide.at[:, :, pl.ds(LANES, full)], sems.at[0]),
            pltpu.make_async_copy(swir_ref, swide.at[:, :, pl.ds(LANES, sfull)], sems.at[1]),
            pltpu.make_async_copy(pan_ref.at[:, pl.ds(0, LANES)], edges.at[0], sems.at[2]),
            pltpu.make_async_copy(pan_ref.at[:, pl.ds(w - LANES, LANES)], edges.at[1], sems.at[3]),
        ]
        for copy in copies:
            copy.start()
        wide[:, :, 0:LANES] = jnp.zeros((hc, nb, LANES), F32)
        wide[:, :, LANES + full : 2 * LANES + full] = jnp.zeros((hc, nb, LANES), F32)
        swide[:, :, 0:LANES] = jnp.zeros((nb, hs, LANES), F32)
        swide[:, :, LANES + sfull : 2 * LANES + sfull] = jnp.zeros((nb, hs, LANES), F32)
        for copy in copies:
            copy.wait()
        for d in range(groups):
            peer = lax.rem(me + d, groups)
            base = pl.multiple_of(peer * wc, LANES)
            sbase = pl.multiple_of(peer * ws, LANES)
            out = outs[d]
            out[0:hc] = wide[:, :, pl.ds(base + LANES, wc)]
            left = wide[:, :, pl.ds(base, LANES)]
            right = wide[:, :, pl.ds(base + LANES + wc, LANES)]
            borders = []
            for r in range(hc):
                borders += [left[r, :, LANES - HALO :], right[r, :, :HALO]]
            swin = swide[:, :, pl.ds(sbase, ws + 2 * LANES)]
            for q in range(hs):
                row = swin[:, q, :]
                lane = ws * (q % RATIO_S)
                out[at_swir + q // RATIO_S, :, lane : lane + ws] = row[:, LANES : LANES + ws]
                borders += [row[:, LANES - 2 : LANES], row[:, LANES + ws : LANES + ws + 2]]
            border = jnp.concatenate(borders, axis=1)
            out[at_edge, :, 0 : border.shape[1]] = border
            for side in going(d):
                first = strip_place(d, side)
                edge = edges[1, :, LANES - REACH :] if side == "right" else edges[0, :, :REACH]
                flat = jnp.concatenate([edge[8 * t : 8 * t + 8] for t in range(h // 8)], axis=1)
                for i in range(8 // nb):
                    lane = piece * (i % per_row)
                    out[first + i // per_row, :, lane : lane + piece] = flat[nb * i : nb * (i + 1)]

    chunks = call(
        pack,
        tuple(shape(chunk_rows[d], nb, wc) for d in range(groups)),
        [
            pltpu.VMEM((hc, nb, full + 2 * LANES), F32),
            pltpu.VMEM((nb, hs, sfull + 2 * LANES), F32),
            pltpu.VMEM((2, h, LANES), F32),
            pltpu.SemaphoreType.DMA((4,)),
        ],
        room=VMEM_MOST,
        in_specs=[ANY] * 3,
    )(pan_image, jnp.transpose(vnir_bands, (1, 0, 2)), swir_bands)
    got = [chunks[0]] + [
        lax.ppermute(chunks[d], "band", [(i, (i + d) % groups) for i in range(groups)])
        for d in range(1, groups)
    ]

    mean_parts, fine_parts = split(cols["mean"]), split(cols["mean_fine"])
    r_fine = split(fine_rows)
    r_adj = split(lift.T)
    table, place = stack_tables(
        dict(
            tall=np.concatenate([mean_parts[0], fine_parts[0]], axis=1),
            tall_low=fine_parts[1],
            fine=split(cols["fine"]),
            rows=split(coarse_rows),
            rows_fine=np.concatenate([r_fine[0], r_fine[1], r_fine[0]], axis=1),
            low=split(cols["low"]),
            pair=split(cols["pair"]),
            up4=split(cols["up4"]),
            up3=split(cols["up3"]),
            adjoint=np.concatenate([r_adj[0], r_adj[0], r_adj[0], r_adj[1], r_adj[1]], axis=1),
        )
    )

    def take(ref, name, index=0, rows=None):
        starts, height, width = place[name]
        first, height = (0, height) if rows is None else (rows[0], rows[1] - rows[0])
        pieces = []
        for start, part in starts:
            base = start + first
            if not isinstance(index, int) or index:
                base = pl.multiple_of(base + index * place[name][1], 16)
            pieces.append(ref[pl.ds(base, height), 0:part])
        return pieces[0] if len(pieces) == 1 else jnp.concatenate(pieces, axis=1)

    def both_parts(ref, name, index=0, stacked=1):
        return take(ref, name, index), take(ref, name, index + stacked)

    def shrink(panes, tall, low):
        both = dot(panes[0], tall) + dot(panes[1], tall)
        return both[:, :LANES], both[:, LANES:] + dot(panes[0], low)

    def along_rows(rc, means, fines):
        both = parts2(jnp.concatenate([means, fines], axis=0))
        return dot(rc[0], both[0]) + (dot(rc[0], both[1]) + dot(rc[1], both[0]))

    def filter_rows(rf, x):
        col = parts2(x)
        return dot(rf, jnp.concatenate([col[0], col[0], col[1]], axis=0))

    def row_variant():
        row_id = lax.axis_index("rows")
        return jnp.where(row_id == 0, 1, jnp.where(row_id == strips - 1, 2, 0))

    def early(pan_ref, table_ref, order_ref, coarse_out, fine_out):
        panes = parts2(pan_ref[...])
        starts = [margin * k - 3 * LANES for k in range(1, frame_tiles - 1)]
        means, fines = shrink(
            windows(panes, starts, 6 * LANES), take(table_ref, "tall"), take(table_ref, "tall_low")
        )
        rc = both_parts(table_ref, "rows", row_variant(), 3)
        coarse_out[...] = along_rows(rc, blocks(means, middle), blocks(fines, middle))
        starts = [2 * LANES * k - LANES for k in range(1, pairs - 1)]
        col = dot3(windows(panes, starts, 4 * LANES), both_parts(table_ref, "fine"))
        fine_out[...] = filter_rows(take(table_ref, "rows_fine"), blocks(col, pairs - 2))

    coarse_mid, fine_mid = call(
        early,
        (shape(2 * pad + 32, LANES * middle), shape(h + 2 * HALO, 2 * LANES * (pairs - 2))),
        cost=(2_000_000_000, 8_000_000),
        in_specs=[VMEM, VMEM, ANY],
    )(pan_image, table, chunks[0])

    at_s = HALO * frame_tiles
    at_ld = at_s + 2 * (sf // LANES)
    at_d = at_ld + frame_tiles
    at_low = at_d + -(-2 * frame_tiles // 8)
    sent = at_low + fine_tiles

    def assemble(pan_ref, table_ref, cm_ref, fm_ref, *rest):
        ins = rest[:groups]
        x_out, s_out, up_out, down_out, ce_out, fe_out = rest[groups:]
        me = lax.axis_index("band")

        def gather(row, lane, size):
            rows = [ins[(groups - i) % groups][row, :, lane : lane + size] for i in range(groups)]
            return pltpu.roll(jnp.concatenate(rows, axis=0), nb * me, 0)

        borders = gather(at_edge, 0, wc)
        zeros = jnp.zeros((8, HALF), F32)

        def framed(main, lane, reach):
            return jnp.concatenate(
                [
                    zeros[:, : HALF - reach],
                    borders[:, lane : lane + reach],
                    main,
                    borders[:, lane + reach : lane + 2 * reach],
                    zeros[:, : HALF - reach],
                ],
                axis=1,
            )

        for r in range(hc):
            row = framed(gather(r, 0, wc), 2 * HALO * r, HALO)
            x_out[r] = row
            for t in range(frame_tiles):
                tile = row[:, LANES * t : LANES * (t + 1)]
                if r >= hc - HALO:
                    up_out[frame_tiles * (r - hc + HALO) + t] = tile
                if r < HALO:
                    down_out[frame_tiles * r + t] = tile
        per = sf // LANES
        for q in range(hs):
            main = gather(at_swir + q // RATIO_S, ws * (q % RATIO_S), ws)
            row = framed(main, 2 * HALO * hc + 4 * q, 2)
            s_out[q] = row
            for t in range(per):
                tile = row[:, LANES * t : LANES * (t + 1)]
                if q >= hs - 2:
                    up_out[at_s + per * (q - hs + 2) + t] = tile
                if q < 2:
                    down_out[at_s + per * q + t] = tile

        def strip(d, side, empty):
            first = strip_place(d, side)
            rows = []
            for i in range(8 // nb):
                lane = piece * (i % per_row)
                rows.append(ins[d][first + i // per_row, :, lane : lane + piece])
            flat = jnp.where(empty, 0.0, jnp.concatenate(rows, axis=0))
            whole = [flat[:, REACH * t : REACH * (t + 1)] for t in range(h // 8)]
            return jnp.concatenate(whole, axis=0)

        blank = jnp.zeros((h, LANES - REACH), F32)
        left = jnp.concatenate([blank, strip(1, "right", me == 0), pan_ref[:, 0 : 3 * LANES]], axis=1)
        right = jnp.concatenate(
            [pan_ref[:, w - 3 * LANES : w], strip(groups - 1, "left", me == groups - 1), blank], axis=1
        )
        left, right = parts2(left), parts2(right)
        cut = 2 * LANES
        inner = (cut, 6 * LANES)
        lm, lf = shrink(left, take(table_ref, "tall", 0, inner), take(table_ref, "tall_low", 0, inner))
        inner = (0, 4 * LANES)
        rm, rfine = shrink(right, take(table_ref, "tall", 0, inner), take(table_ref, "tall_low", 0, inner))
        rc = both_parts(table_ref, "rows", row_variant(), 3)
        edge = along_rows(rc, jnp.concatenate([lm, rm], axis=1), jnp.concatenate([lf, rfine], axis=1))
        ce_out[...] = edge
        outer = tuple(jnp.concatenate([a, b], axis=0) for a, b in zip(left, right))
        fine_edge = filter_rows(
            take(table_ref, "rows_fine"), blocks(dot3(outer, both_parts(table_ref, "fine")), 2)
        )
        fe_out[...] = fine_edge

        def coarse(rows, k):
            if k == 0:
                return edge[rows, 0:LANES]
            if k == frame_tiles - 1:
                return edge[rows, LANES:]
            return cm_ref[rows, LANES * (k - 1) : LANES * k]

        first = 2 * pad
        for out, at, dead in ((up_out, first, 0), (down_out, first + 16, HALO - 2)):
            for k in range(frame_tiles):
                out[at_ld + k] = coarse(slice(at + 8, at + 16), k)
                small = coarse(slice(at, at + 8), k)[dead : dead + 2]
                out[at_d + k // 4, 2 * (k % 4) : 2 * (k % 4) + 2, :] = small
        for out, at in ((up_out, h), (down_out, h + HALO)):
            for k in range(fine_tiles):
                if k < 2:
                    tile = fine_edge[at : at + 8, LANES * k : LANES * (k + 1)]
                elif k >= fine_tiles - 2:
                    lane = LANES * (k - fine_tiles + 4)
                    tile = fine_edge[at : at + 8, lane : lane + LANES]
                else:
                    tile = fm_ref[at : at + 8, LANES * (k - 2) : LANES * (k - 1)]
                out[at_low + k] = tile

    x_loc, s_loc, up_send, down_send, coarse_edge, fine_edge = call(
        assemble,
        (
            shape(hc, BANDS, wf),
            shape(hs, BANDS, sf),
            shape(sent, 8, LANES),
            shape(sent, 8, LANES),
            shape(2 * pad + 32, 2 * LANES),
            shape(h + 2 * HALO, 4 * LANES),
        ),
        cost=(200_000_000, 3_000_000),
    )(pan_image, table, coarse_mid, fine_mid, *got)
    from_low = lax.ppermute(up_send, "rows", [(i, i + 1) for i in range(strips - 1)])
    from_high = lax.ppermute(down_send, "rows", [(i + 1, i) for i in range(strips - 1)])

    def moments(
        pan_ref, x_ref, s_ref, lo_ref, hi_ref, cm_ref, fm_ref, ce_ref, fe_ref,
        table_ref,
        mom_out, y_out, diff_out, ugap_out, dgap_out, s_out,
        both, ulow, q_ref,
    ):
        me = lax.axis_index("band")
        row_id = lax.axis_index("rows")

        def tiles(ref, first, number):
            return jnp.concatenate([ref[first + t] for t in range(number)], axis=1)

        def x_row(r):
            if r < 0:
                return tiles(lo_ref, frame_tiles * (HALO + r), frame_tiles)
            if r >= hc:
                return tiles(hi_ref, frame_tiles * (r - hc), frame_tiles)
            return x_ref[r]

        block_starts = [LANES * k for k in range(coarse_tiles)]
        frame = parts2(jnp.concatenate([x_row(r) for r in range(-2, hc + 2)], axis=0))
        up = dot3(windows(frame, block_starts, 2 * LANES), both_parts(table_ref, "up4"))
        size = 8 * (hc + 4)
        for k in range(coarse_tiles):
            for q in range(RATIO_V):
                y_out[RATIO_V * k + q] = up[size * k : size * (k + 1), LANES * q : LANES * (q + 1)]

        low = jnp.concatenate([fe_ref[0:h, 0 : 2 * LANES], fm_ref[0:h, :], fe_ref[0:h, 2 * LANES :]], axis=1)
        top = low[0:HALO] + tiles(lo_ref, at_low, fine_tiles)
        end = low[h - HALO : h] + tiles(hi_ref, at_low, fine_tiles)
        low = jnp.concatenate([top, low[HALO : h - HALO], end], axis=0)
        diff = pan_ref[...] - low
        p1 = low.astype(BF16)
        rest = low - p1.astype(F32)
        p2 = rest.astype(BF16)
        p3 = (rest - p2.astype(F32)).astype(BF16)
        adjoint = dot(take(table_ref, "adjoint"), jnp.concatenate([p1, p2, p3, p1, p2], axis=0))
        psum = jnp.zeros((8, LANES), F32)
        for k in range(fine_tiles):
            at = slice(LANES * k, LANES * (k + 1))
            diff_out[k] = diff[:, at]
            q_ref[k] = adjoint[:, at]
            for t in range(h // 8):
                psum = psum + low[8 * t : 8 * t + 8, at]

        zero = jnp.zeros((8, LANES), F32)
        turns = BANDS // 2 + 1

        def tile_step(k, carry):
            accs = list(carry[:turns])
            accp, accv = carry[turns], carry[turns + 1]
            ys = [y_out[k, pl.ds(8 * m, 8), :] for m in range(hc + 4)]
            for m in range(hc + 4):
                z = None
                for other in range(hc + 4):
                    if gram[m, other] != 0.0:
                        term = float(gram[m, other]) * ys[other]
                        z = term if z is None else z + term
                accs[0] = accs[0] + z * ys[m]
                for i in range(1, turns):
                    accs[i] = accs[i] + z * pltpu.roll(ys[m], i, 0)
                accp = accp + ys[m] * q_ref[k, pl.ds(m, 1), :]
                accv = accv + float(rise[m]) * ys[m]
            return tuple(accs) + (accp, accv)

        first = lax.fori_loop(0, fine_tiles, tile_step, (zero,) * (turns + 2))

        below = jnp.where(row_id > 0, 1.0, 0.0).astype(F32)
        above = jnp.where(row_id < strips - 1, 1.0, 0.0).astype(F32)
        reach = TAPS_S // 2
        means = []
        for r in range(-reach, hc + reach):
            value = float(MEAN4[2]) * x_row(r)
            for t in (1, 2):
                value = value + float(MEAN4[2 + t]) * (x_row(r - t) + x_row(r + t))
            if r < 0:
                value = value * below
            if r >= hc:
                value = value * above
            means.append(value)
        lows = []
        for r in range(hc):
            centre = r + reach
            value = float(KC[reach]) * means[centre]
            for t in range(1, reach + 1):
                value = value + float(KC[reach + t]) * (means[centre - t] + means[centre + t])
            lows.append(value)
        u_rows = windows(parts2(jnp.concatenate(means[reach : reach + hc], axis=0)), block_starts, 2 * LANES)
        l_rows = windows(parts2(jnp.concatenate(lows, axis=0)), block_starts, 2 * LANES)
        u_all = dot3(u_rows, tuple(x[:, :LANES] for x in both_parts(table_ref, "pair", 0, 3)))
        left = jnp.where(me == 0, 1, 0)
        right = jnp.where(me == groups - 1, 2, 0)
        size = 8 * hc
        last = coarse_tiles - 1
        for which, lo_k, hi_k in ((left, 0, 1), (0, 1, last), (right, last, last + 1)):
            if hi_k <= lo_k:
                continue
            wp = tuple(x[:, LANES:] for x in both_parts(table_ref, "pair", which, 3))
            part = dot3(tuple(x[size * lo_k : size * hi_k] for x in l_rows), wp)
            for k in range(lo_k, hi_k):
                at = slice(LANES * k, LANES * (k + 1))
                low_k = part[size * (k - lo_k) : size * (k - lo_k + 1)]
                ulow[:, at] = low_k
                ugap_out[:, at] = u_all[size * k : size * (k + 1)] - low_k

        column = lax.broadcasted_iota(jnp.int32, (1, wf), 1) - HALF + me * wc
        inside = jnp.where((column >= 0) & (column < groups * wc), 1.0, 0.0).astype(F32)

        def own(rows):
            return jnp.concatenate([ce_ref[rows, 0:LANES], cm_ref[rows, :], ce_ref[rows, LANES:]], axis=1)

        def small(ref):
            return jnp.concatenate(
                [ref[at_d + k // 4, 2 * (k % 4) : 2 * (k % 4) + 2, :] for k in range(frame_tiles)], axis=1
            )

        both[...] = own(slice(0, pad))
        both[0:2] = both[0:2] + small(lo_ref)
        both[hc - 2 : hc] = both[hc - 2 : hc] + small(hi_ref)
        detail = both[...]
        both[...] = own(slice(pad, 2 * pad))
        both[0:HALO] = both[0:HALO] + tiles(lo_ref, at_ld, frame_tiles)
        both[hc - HALO : hc] = both[hc - HALO : hc] + tiles(hi_ref, at_ld, frame_tiles)
        dlow_rows = windows(parts2(both[...] * inside), block_starts, 2 * LANES)
        dlow = blocks(dot3(dlow_rows, both_parts(table_ref, "low")), coarse_tiles)
        dgap_out[...] = detail[:, HALF : HALF + wc] - dlow
        both[:, 0:wc] = dlow

        per = sf // LANES
        s_rows = [tiles(lo_ref, at_s + per * q, per) for q in range(2)]
        s_rows += [s_ref[r] for r in range(hs)]
        s_rows += [tiles(hi_ref, at_s + per * q, per) for q in range(2)]
        s_parts = windows(parts2(jnp.concatenate(s_rows, axis=0)), block_starts[:swir_tiles], 2 * LANES)
        s_cols = blocks(dot3(s_parts, both_parts(table_ref, "up3")), swir_tiles)
        for m in range(hs):
            for p in range(RATIO_S):
                value = None
                for t in range(5):
                    if C3[t, p] != 0.0:
                        term = float(C3[t, p]) * s_cols[8 * (m + t) : 8 * (m + t) + 8]
                        value = term if value is None else value + term
                s_out[RATIO_S * m + p] = value

        ll = [zero] * turns
        cross = [zero] * BANDS
        ld = ls = sd = ss = dd = ds = zero
        for r in range(hc):
            for k in range(coarse_tiles):
                at = slice(LANES * k, LANES * (k + 1))
                u = ulow[8 * r : 8 * r + 8, at]
                s = s_out[r, :, at]
                dl = jnp.broadcast_to(both[r : r + 1, at], (8, LANES))
                ll[0] = ll[0] + u * u
                for i in range(1, turns):
                    ll[i] = ll[i] + u * pltpu.roll(u, i, 0)
                for i in range(BANDS):
                    cross[i] = cross[i] + u * s_out[r, i : i + 1, at]
                ld = ld + u * dl
                sd = sd + s * dl
                ls = ls + u
                ss = ss + s
                dd = dd + dl * dl
                ds = ds + dl

        lane = lax.broadcasted_iota(jnp.int32, (8, LANES), 1)
        sub = lax.broadcasted_iota(jnp.int32, (8, LANES), 0)

        def column_of(acc):
            return jnp.broadcast_to(jnp.sum(acc, axis=1, keepdims=True), (8, LANES))

        table = zero
        for base, accs in ((0, ll), (32, first[:turns])):
            for i in range(turns):
                col = column_of(accs[i])
                table = jnp.where(lane == base + lax.rem(sub + BANDS - i, BANDS), col, table)
                if 0 < i < BANDS // 2:
                    turned = pltpu.roll(col, BANDS - i, 0)
                    table = jnp.where(lane == base + lax.rem(sub + i, BANDS), turned, table)
        singles = [(8 + i, cross[i]) for i in range(BANDS)]
        singles += [(16, ld), (17, ls), (18, sd), (19, ss), (20, dd), (21, ds)]
        singles += [(40, first[turns]), (41, first[turns + 1])]
        for index, acc in singles:
            table = jnp.where(lane == index, column_of(acc), table)
        total = jnp.sum(jnp.sum(psum, axis=0, keepdims=True), axis=1, keepdims=True)
        table = jnp.where(lane == 43, total, table)
        turned = pltpu.roll(table, HALF, 1)
        mom_out[...] = jnp.where(lane[0:4] < HALF, table[0:4], turned[4:8])

    mom, y_up, diff, ugap, dgap, s_up = call(
        moments,
        (
            shape(4, LANES),
            shape(fine_tiles, 8 * (hc + 4), LANES),
            shape(fine_tiles, h, LANES),
            shape(8 * hc, wc),
            shape(pad, wc),
            shape(hc, BANDS, wc),
        ),
        [
            pltpu.VMEM((pad, wf), F32),
            pltpu.VMEM((8 * hc, wc), F32),
            pltpu.VMEM((fine_tiles, hc + 4, LANES), F32),
        ],
        cost=(1_000_000_000, 8_000_000),
    )(
        pan_image, x_loc, s_loc, from_low, from_high, coarse_mid, fine_mid, coarse_edge, fine_edge, table,
    )
    devices = groups * strips
    spread = jnp.broadcast_to(mom[None], (devices,) + mom.shape)
    sums = lax.all_to_all(spread, ("rows", "band"), split_axis=0, concat_axis=0, tiled=True)

    def finish(sums_ref, y_ref, diff_ref, ugap_ref, dgap_ref, s_ref, vnir_out, swir_out, tiles, sems):
        lane = lax.broadcasted_iota(jnp.int32, (8, LANES), 1)
        sub = lax.broadcasted_iota(jnp.int32, (8, LANES), 0)
        eye = lane == sub
        terms = [sums_ref[index] for index in range(devices)]
        while len(terms) > 1:
            terms = [sum(terms[i : i + 2][1:], terms[i]) for i in range(0, len(terms), 2)]
        total = jnp.concatenate([terms[0], pltpu.roll(terms[0], HALF, 1)], axis=0)
        def column(x, index):
            return jnp.broadcast_to(x[:, index : index + 1], (8, LANES))

        def across(col):
            return jnp.sum(jnp.where(eye, col, 0.0), axis=0, keepdims=True)

        def down(x):
            return jnp.sum(x, axis=0, keepdims=True)

        def solve(matrix, rhs):
            work = jnp.where(lane == 8, rhs, matrix)
            for k in range(BANDS):
                pivot_row = work[k : k + 1, :] / column(work, k)[k : k + 1, :]
                other = work - column(work, k) * pivot_row
                work = jnp.where(sub == k, pivot_row, other)
            return column(work, 8)

        n1 = float(fine_pixels)
        mean_v = column(total, 41) / n1
        mean_p = column(total, 43) / n1
        cov_v = pltpu.roll(total, LANES - 32, 1) / n1 - mean_v * across(mean_v)
        cov_p = column(total, 40) / n1 - mean_v * mean_p
        fit = solve(cov_v, cov_p)
        gain = cov_p / down(cov_p * fit)

        def tile_step(k, carry):
            for m in range(hc):
                ys = [y_ref[k, pl.ds(8 * (m + t), 8), :] for t in range(5)]
                for p in range(RATIO_V):
                    r = RATIO_V * m + p
                    value = gain * diff_ref[k, pl.ds(r, 1), :]
                    for t in range(5):
                        if C4[t, p] != 0.0:
                            value = value + float(C4[t, p]) * ys[t]
                    tiles[k, pl.ds(r, 8, stride=h), :] = value
            pltpu.make_async_copy(
                tiles.at[k], vnir_out.at[:, pl.ds(pl.multiple_of(LANES * k, LANES), LANES)], sems.at[k]
            ).start()
            return carry

        lax.fori_loop(0, fine_tiles, tile_step, 0)

        n2 = float(fine_pixels // (RATIO_V * RATIO_V))
        mean_l = column(total, 17) / n2
        mean_s = column(total, 19) / n2
        mean_d = column(total, 21) / n2
        cov_ll = total / n2 - mean_l * across(mean_l)
        cov_ls = pltpu.roll(total, LANES - 8, 1) / n2 - mean_l * across(mean_s)
        cov_ld = column(total, 16) / n2 - mean_l * mean_d
        cov_sd = column(total, 18) / n2 - mean_s * mean_d
        cov_dd = column(total, 20) / n2 - mean_d * mean_d
        gain_row = across(gain)
        a2 = cov_ll + gain * across(cov_ld) + cov_ld * gain_row + gain * gain_row * cov_dd
        b2 = cov_ls + gain * across(cov_sd)
        b2 = jnp.where(lane < BANDS, b2, 0.0)
        target = jnp.broadcast_to(jnp.sum(b2, axis=1, keepdims=True) / BANDS, (8, LANES))
        fit2 = solve(a2, target)
        numer = down(fit2 * b2)
        share_row = numer / down(fit2 * target)
        share = jnp.sum(jnp.where(eye, jnp.broadcast_to(share_row, (8, LANES)), 0.0), axis=1, keepdims=True)
        scale = down(fit2 * gain)[:, 0:1]
        fit_col = fit2[:, 0:1]
        for r in range(hc):
            seen = jnp.sum(fit_col * ugap_ref[8 * r : 8 * r + 8, :], axis=0, keepdims=True)
            seen = seen + scale * dgap_ref[r : r + 1, :]
            swir_out[r] = s_ref[r] + share * seen

        def drain(k, carry):
            pltpu.make_async_copy(
                tiles.at[k], vnir_out.at[:, pl.ds(pl.multiple_of(LANES * k, LANES), LANES)], sems.at[k]
            ).wait()
            return carry

        lax.fori_loop(0, fine_tiles, drain, 0)

    joined_vnir, joined_swir = call(
        finish,
        (shape(BANDS * h, w), shape(hc, BANDS, wc)),
        [pltpu.VMEM((fine_tiles, BANDS * h, LANES), F32), pltpu.SemaphoreType.DMA((fine_tiles,))],
        cost=(100_000_000, 8_000_000),
        out_specs=(ANY, VMEM),
    )(sums, y_up, diff, ugap, dgap, s_up)
    return joined_vnir.reshape(BANDS, h, w), jnp.transpose(joined_swir, (1, 0, 2))


def solution(mesh):
    return jax.shard_map(
        local,
        mesh=mesh,
        in_specs=(P("rows", "band"), P("band", "rows", None), P("band", "rows", None)),
        out_specs=(P(None, "rows", "band"), P(None, "rows", "band")),
        check_vma=False,
    )
```

time: 74.1 us -> 50.5 us (0.68)
  local copies, waits for them, and re-layouts: 14.4 us -> 4 us
  waiting for transfers between devices: 14.2 us -> 4.01 us
  Pallas kernels: 15.8 us -> 13.1 us
  starting transfers between devices: 9.37 us -> 10.7 us
  blocking collectives: 18.9 us -> 17.7 us
    ppermute x3, waiting for transfers between devices: 10.7 us -> 0.01 us  [local(): lax.ppermute(chunks[d], 'band', [(i, (i + d) % groups) for i in range(gro...]
    unnamed x28 -> x8, local copies, waits for them, and re-layouts: 14.4 us -> 3.99 us
    pallas_call x4 -> x5, Pallas kernels: 15.8 us -> 13.1 us  [the longest x1 4.78 us: local(): call(finish, (shape(BANDS * h, w), shape(hc, BANDS, wc)), [pltpu.VMEM((fi...]
    ppermute x3, starting transfers between devices: 6.11 us -> 7.92 us  [local(): lax.ppermute(chunks[d], 'band', [(i, (i + d) % groups) for i in range(gro...]
    all_to_all x1, blocking collectives: 18.9 us -> 17.7 us  [local(): lax.all_to_all(spread, ('rows', 'band'), split_axis=0, concat_axis=0, til...]
  transfers between devices with their start and end apart: 5 -> 5, of which waited for: 3 -> 1; matrix products, arithmetic and copies ran while one was open for 0% -> 0% of each run, Pallas kernels for 0% -> 3%
where the time goes in v2:
time: 50.5 us; the launch traced here: 50.2 us
  blocking collectives  17.7 us (35%)
  Pallas kernels  13.1 us (26%)
  starting transfers between devices  10.7 us (21%)
  waiting for transfers between devices  4.01 us (8%)
  local copies, waits for them, and re-layouts  4 us (8%)
  between operations  0.71 us (1%)
    all_to_all x1, blocking collectives, local(): lax.all_to_all(spread, ('rows', 'band'), split_axis=0, concat_axis=0, til...  17.7 us
    ppermute x3, starting transfers between devices, local(): lax.ppermute(chunks[d], 'band', [(i, (i + d) % groups) for i in range(gro...  7.92 us
    pallas_call x1, Pallas kernels, local(): call(finish, (shape(BANDS * h, w), shape(hc, BANDS, wc)), [pltpu.VMEM((fi...  4.78 us
    ppermute x1, waiting for transfers between devices, local(): lax.ppermute(down_send, 'rows', [(i + 1, i) for i in range(strips - 1)])  4 us
    unnamed x8, local copies, waits for them, and re-layouts  3.99 us
    pallas_call x1, Pallas kernels, local(): call(moments, (shape(4, LANES), shape(fine_tiles, 8 * (hc + 4), LANES), s...  3.97 us
    pallas_call x1, Pallas kernels, local(): call(pack, tuple((shape(chunk_rows[d], nb, wc) for d in range(groups))),...  1.97 us
    pallas_call x1, Pallas kernels, local(): call(early, (shape(2 * pad + 32, LANES * middle), shape(h + 2 * HALO, 2 *...  1.53 us
  transfers between devices with their start and end apart: 5, of which 1 were waited for; matrix products, arithmetic and copies ran while one was open for 0% of the time, Pallas kernels for 3%

profile of v2, /device:TPU:0, one launch (start us, length us, event | category | flops | bytes accessed | tf_op | source)
XLA Modules:
  0.0 50.2 jit_solution(10521919401118622145)
XLA Ops:
  0.6 2.0 %shard_map.59 = (f32[15,2,768]{2,1,0:T(2,128)}, f32[16,2,768]{2,1,0:T(2,128)}, f32[15,2,768]{2,1,0:T(2,128)}, f32[16,2,768]{2,1,0:T(2,128)}) custom-call(f32[48,3072]{1,0:T(8,128)} %pan_ref.7, f32[12,2,3072]{2,1,0:T(2,128)} %bitcast.3, f32[2,4,1024]{2,1,0:T(4,128)} %swir_ref.1), custom_call_target="tpu_custom_call" | custom-call | tf_op jit(solution)/shard_map/pallas_call | solution.py:311
  2.6 4.1 %collective-permute-start.1 = (f32[15,2,768]{2,1,0:T(2,128)}, f32[15,2,768]{2,1,0:T(2,128)S(1)}, u32[]{:S(2)}, u32[]{:S(2)}) collective-permute-start(f32[15,2,768]{2,1,0:T(2,128)} %get-tuple-element.26), channel_id=1, source_target_pairs={{0,2},{1,3},{2,0},{3,1},{4,6},{5,7},{6,4},{7,5},{8,10},{9,11},{10,... | collective-permute-start | bytes 276488 | tf_op jit(solution)/shard_map/ppermute | solution.py:324
  6.7 1.6 %collective-permute-start = (f32[16,2,768]{2,1,0:T(2,128)}, f32[16,2,768]{2,1,0:T(2,128)S(1)}, u32[]{:S(2)}, u32[]{:S(2)}) collective-permute-start(f32[16,2,768]{2,1,0:T(2,128)} %get-tuple-element.25), channel_id=1, source_target_pairs={{0,1},{1,2},{2,3},{3,0},{4,5},{5,6},{6,7},{7,4},{8,9},{9,10},{10,1... | collective-permute-start | bytes 294920 | tf_op jit(solution)/shard_map/ppermute | solution.py:324
  8.3 2.2 %collective-permute-start.2 = (f32[16,2,768]{2,1,0:T(2,128)}, f32[16,2,768]{2,1,0:T(2,128)S(1)}, u32[]{:S(2)}, u32[]{:S(2)}) collective-permute-start(f32[16,2,768]{2,1,0:T(2,128)} %get-tuple-element.27), channel_id=1, source_target_pairs={{0,3},{1,0},{2,1},{3,2},{4,7},{5,4},{6,5},{7,6},{8,11},{9,8},{10,9... | collective-permute-start | bytes 294920 | tf_op jit(solution)/shard_map/ppermute | solution.py:324
  10.5 0.0 copy-start
  10.5 2.0 %copy-done = bf16[7120,256]{1,0:T(8,128)(2,1)S(1)} copy-done((bf16[7120,256]{1,0:T(8,128)(2,1)S(1)}, bf16[7120,256]{1,0:T(8,128)(2,1)}, u32[]{:S(2)}) %copy-start) | copy-done | bytes 3645464
  12.6 0.0 copy-start.2
  12.6 1.1 %copy-done.2 = f32[48,3072]{1,0:T(8,128)S(1)} copy-done((f32[48,3072]{1,0:T(8,128)S(1)}, f32[48,3072]{1,0:T(8,128)}, u32[]{:S(2)}) %copy-start.2) | copy-done | bytes 589848
  13.6 0.0 copy-start.3
  13.6 0.9 %copy-done.3 = f32[15,2,768]{2,1,0:T(2,128)S(1)} copy-done((f32[15,2,768]{2,1,0:T(2,128)S(1)}, f32[15,2,768]{2,1,0:T(2,128)}, u32[]{:S(2)}) %copy-start.3) | copy-done | bytes 92184
  14.5 1.5 %shard_map.60 = (f32[64,640]{1,0:T(8,128)S(1)}, f32[64,2560]{1,0:T(8,128)S(1)}) custom-call(f32[48,3072]{1,0:T(8,128)S(1)} %copy-done.2, bf16[7120,256]{1,0:T(8,128)(2,1)S(1)} %copy-done, f32[15,2,768]{2,1,0:T(2,128)S(1)} %copy-done.3), custom_call_target="tpu_custom_call" | custom-call | flops 2000000000 | bytes 8000000 | tf_op jit(solution)/shard_map/pallas_call | solution.py:388
  16.1 0.0 copy-start.1
  16.1 0.0 collective-permute-done.1.rest_2_
  16.1 0.0 collective-permute-done.rest_1_
  16.1 0.0 collective-permute-done.2.rest_3_
  16.1 0.8 %shard_map.61 = (f32[12,8,896]{2,1,0:T(8,128)S(1)}, f32[4,8,384]{2,1,0:T(8,128)S(1)}, f32[95,8,128]{2,1,0:T(8,128)S(1)}, f32[95,8,128]{2,1,0:T(8,128)S(1)}, f32[...) custom-call(f32[48,3072]{1,0:T(8,128)S(1)} %copy-done.2, bf16[7120,256]{1,0:T(8,128)(2,1)S(1)} %copy-done, ...), custom_call_target="tpu_custom_call" | custom-call | flops 200000000 | bytes 3000000 | tf_op jit(solution)/shard_map/pallas_call | solution.py:500
  16.9 1.4 %collective-permute-start.3 = (f32[95,8,128]{2,1,0:T(8,128)S(1)}, f32[95,8,128]{2,1,0:T(8,128)S(1)}, u32[]{:S(2)}, u32[]{:S(2)}) collective-permute-start(f32[95,8,128]{2,1,0:T(8,128)S(1)} %get-tuple-element.30), channel_id=1, source_target_pairs={{0,4},{4,8},{8,12},{12,16},{16,20},{20,24},{24,28},{1,5},{5,9},{9,... | collective-permute-start | bytes 1167368 | tf_op jit(solution)/shard_map/ppermute | solution.py:512
  18.4 1.3 %collective-permute-start.4 = (f32[95,8,128]{2,1,0:T(8,128)S(1)}, f32[95,8,128]{2,1,0:T(8,128)S(1)}, u32[]{:S(2)}, u32[]{:S(2)}) collective-permute-start(f32[95,8,128]{2,1,0:T(8,128)S(1)} %get-tuple-element.31), channel_id=1, source_target_pairs={{4,0},{8,4},{12,8},{16,12},{20,16},{24,20},{28,24},{5,1},{9,5},{13... | collective-permute-start | bytes 1167368 | tf_op jit(solution)/shard_map/ppermute | solution.py:513
  19.7 0.0 collective-permute-done.3.lo_ref
  19.7 4.0 %collective-permute-done.4.hi_ref = f32[95,8,128]{2,1,0:T(8,128)S(1)} collective-permute-done((f32[95,8,128]{2,1,0:T(8,128)S(1)}, f32[95,8,128]{2,1,0:T(8,128)S(1)}, u32[]{:S(2)}, u32[]{:S(2)}) %collective-permute-start.4) | collective-permute-done | bytes 389152 | tf_op jit(solution)/shard_map/ppermute | solution.py:513
  23.7 0.0 copy-done.1
  23.7 4.0 %shard_map.62 = (f32[4,128]{1,0:T(4,128)S(1)}, f32[24,128,128]{2,1,0:T(8,128)S(1)}, f32[24,48,128]{2,1,0:T(8,128)S(1)}, f32[96,768]{1,0:T(8,128)S(1)}, f32[16,768]{1,0:T(8,128)S(1)}, /*index=5*/f32[12,8,768]{2,1,0:T(8,128)S(1)}) custom-call(f32[48,3072]{1,0:T(8,128)S(1)} %copy-done.2, f32[12,8,896]{2,1,0:T(8,128)S(1)} %get-tuple-element.28.x_ref, ...), custom_call_target="tpu_custom_call" | custom-call | flops 1000000000 | bytes 8000000 | tf_op jit(solution)/shard_map/pallas_call | solution.py:703
  27.7 17.7 %all_to_all.5.sums_ref = f32[32,4,128]{2,1,0:T(4,128)S(1)} all-to-all(f32[32,4,128]{2,1,0:T(4,128)S(1)} %broadcast_in_dim.2), channel_id=1, replica_groups=mesh['rows'=8,'band'=4] {'rows','band'}, dimensions={0} | all-to-all | bytes 131072 | tf_op jit(solution)/shard_map/all_to_all | solution.py:724
  45.4 4.8 %shard_map.63 = (f32[384,3072]{1,0:T(8,128)}, f32[12,8,768]{2,1,0:T(8,128)}) custom-call(f32[32,4,128]{2,1,0:T(4,128)S(1)} %all_to_all.5.sums_ref, f32[24,128,128]{2,1,0:T(8,128)S(1)} %get-tuple-element.35.y_ref, f32[24,48,128]{2,1,0:T(8,128)S(1)} %get-tuple-element.36.diff_ref, f32[96,768]{1,0:T(8,128)S(1)} %get-tuple-element.37.ugap_ref, ...), custom_call_target="tpu_custom_call" | custom-call | flops 100000000 | bytes 8000000 | tf_op jit(solution)/shard_map/pallas_call | solution.py:809
  (1 shorter events, 0.0 us)
Async XLA Ops:
  2.6 13.5 %collective-permute-start.1 = (f32[15,2,768]{2,1,0:T(2,128)}, f32[15,2,768]{2,1,0:T(2,128)S(1)}, u32[]{:S(2)}, u32[]{:S(2)}) collective-permute-start(f32[15,2,768]{2,1,0:T(2,128)} %get-tuple-element.26), channel_id=1, source_target_pairs={{0,2},{1,3},{2,0},{3,1},{4,6},{5,7},{6,4},{7,5},{8,10},{9,11},{10,... | collective-permute-start | bytes 276488 | tf_op jit(solution)/shard_map/ppermute | solution.py:324
  6.7 9.4 %collective-permute-start = (f32[16,2,768]{2,1,0:T(2,128)}, f32[16,2,768]{2,1,0:T(2,128)S(1)}, u32[]{:S(2)}, u32[]{:S(2)}) collective-permute-start(f32[16,2,768]{2,1,0:T(2,128)} %get-tuple-element.25), channel_id=1, source_target_pairs={{0,1},{1,2},{2,3},{3,0},{4,5},{5,6},{6,7},{7,4},{8,9},{9,10},{10,1... | collective-permute-start | bytes 294920 | tf_op jit(solution)/shard_map/ppermute | solution.py:324
  8.3 7.8 %collective-permute-start.2 = (f32[16,2,768]{2,1,0:T(2,128)}, f32[16,2,768]{2,1,0:T(2,128)S(1)}, u32[]{:S(2)}, u32[]{:S(2)}) collective-permute-start(f32[16,2,768]{2,1,0:T(2,128)} %get-tuple-element.27), channel_id=1, source_target_pairs={{0,3},{1,0},{2,1},{3,2},{4,7},{5,4},{6,5},{7,6},{8,11},{9,8},{10,9... | collective-permute-start | bytes 294920 | tf_op jit(solution)/shard_map/ppermute | solution.py:324
  10.5 2.0 %copy-start = (bf16[7120,256]{1,0:T(8,128)(2,1)S(1)}, bf16[7120,256]{1,0:T(8,128)(2,1)}, u32[]{:S(2)}) copy-start(bf16[7120,256]{1,0:T(8,128)(2,1)} %constant.2.clone.table_ref) | copy-start | bytes 10936324
  12.6 1.1 %copy-start.2 = (f32[48,3072]{1,0:T(8,128)S(1)}, f32[48,3072]{1,0:T(8,128)}, u32[]{:S(2)}) copy-start(f32[48,3072]{1,0:T(8,128)} %pan_ref.7) | copy-start | bytes 1769476
  13.6 0.9 %copy-start.3 = (f32[15,2,768]{2,1,0:T(2,128)S(1)}, f32[15,2,768]{2,1,0:T(2,128)}, u32[]{:S(2)}) copy-start(f32[15,2,768]{2,1,0:T(2,128)} %get-tuple-element.22.order_ref.rest_0_) | copy-start | bytes 276484
  16.1 7.6 %copy-start.1 = (bf16[7120,256]{1,0:T(8,128)(2,1)S(1)}, bf16[7120,256]{1,0:T(8,128)(2,1)}, u32[]{:S(2)}) copy-start(bf16[7120,256]{1,0:T(8,128)(2,1)} %constant.2.clone.table_ref) | copy-start | bytes 10936324
  16.9 2.8 %collective-permute-start.3 = (f32[95,8,128]{2,1,0:T(8,128)S(1)}, f32[95,8,128]{2,1,0:T(8,128)S(1)}, u32[]{:S(2)}, u32[]{:S(2)}) collective-permute-start(f32[95,8,128]{2,1,0:T(8,128)S(1)} %get-tuple-element.30), channel_id=1, source_target_pairs={{0,4},{4,8},{8,12},{12,16},{16,20},{20,24},{24,28},{1,5},{5,9},{9,... | collective-permute-start | bytes 1167368 | tf_op jit(solution)/shard_map/ppermute | solution.py:512
  18.4 5.3 %collective-permute-start.4 = (f32[95,8,128]{2,1,0:T(8,128)S(1)}, f32[95,8,128]{2,1,0:T(8,128)S(1)}, u32[]{:S(2)}, u32[]{:S(2)}) collective-permute-start(f32[95,8,128]{2,1,0:T(8,128)S(1)} %get-tuple-element.31), channel_id=1, source_target_pairs={{4,0},{8,4},{12,8},{16,12},{20,16},{24,20},{28,24},{5,1},{9,5},{13... | collective-permute-start | bytes 1167368 | tf_op jit(solution)/shard_map/ppermute | solution.py:513

commit v3 on v2

--- a/solution.py
+++ b/solution.py
@@ -250,7 +250,11 @@
 
     swir_rows = -(-hs // RATIO_S)
     at_swir = hc
-    at_edge = hc + swir_rows
+    edge_size = 2 * HALO * hc + 4 * hs
+    edge_lane = ws * (hs % RATIO_S)
+    shared = hs % RATIO_S and edge_lane + edge_size <= wc
+    at_edge = hc + swir_rows - 1 if shared else hc + swir_rows
+    edge_lane = edge_lane if shared else 0
     at_strip = at_edge + 1
     piece = REACH * (h // 8)
     per_row = wc // piece
@@ -264,14 +268,36 @@
 
     chunk_rows = [at_strip + strip_rows * len(going(d)) for d in range(groups)]
 
-    def pack(pan_ref, vnir_ref, swir_ref, *rest):
-        outs, (wide, swide, edges, sems) = rest[:groups], rest[groups:]
+    mean_parts, fine_parts = split(cols["mean"]), split(cols["mean_fine"])
+    r_fine = split(fine_rows)
+    r_adj = split(lift.T)
+    table, place = stack_tables(
+        dict(
+            tall=np.concatenate([mean_parts[0], fine_parts[0]], axis=1),
+            tall_low=fine_parts[1],
+            fine=split(cols["fine"]),
+            rows=split(coarse_rows),
+            rows_fine=np.concatenate([r_fine[0], r_fine[1], r_fine[0]], axis=1),
+            low=split(cols["low"]),
+            pair=split(cols["pair"]),
+            up4=split(cols["up4"]),
+            up3=split(cols["up3"]),
+            adjoint=np.concatenate([r_adj[0], r_adj[0], r_adj[0], r_adj[1], r_adj[1]], axis=1),
+        )
+    )
+
+    sources = (pan_image, jnp.transpose(vnir_bands, (1, 0, 2)), swir_bands, jnp.asarray(table))
+
+    def pack(pan_ref, vnir_ref, swir_ref, table_ref, *rest):
+        outs, (pan_out, table_out, wide, swide, edges, sems) = rest[:groups], rest[groups:]
         me = lax.axis_index("band")
         copies = [
             pltpu.make_async_copy(vnir_ref, wide.at[:, :, pl.ds(LANES, full)], sems.at[0]),
             pltpu.make_async_copy(swir_ref, swide.at[:, :, pl.ds(LANES, sfull)], sems.at[1]),
             pltpu.make_async_copy(pan_ref.at[:, pl.ds(0, LANES)], edges.at[0], sems.at[2]),
             pltpu.make_async_copy(pan_ref.at[:, pl.ds(w - LANES, LANES)], edges.at[1], sems.at[3]),
+            pltpu.make_async_copy(pan_ref, pan_out, sems.at[4]),
+            pltpu.make_async_copy(table_ref, table_out, sems.at[5]),
         ]
         for copy in copies:
             copy.start()
@@ -279,7 +305,7 @@
         wide[:, :, LANES + full : 2 * LANES + full] = jnp.zeros((hc, nb, LANES), F32)
         swide[:, :, 0:LANES] = jnp.zeros((nb, hs, LANES), F32)
         swide[:, :, LANES + sfull : 2 * LANES + sfull] = jnp.zeros((nb, hs, LANES), F32)
-        for copy in copies:
+        for copy in copies[:4]:
             copy.wait()
         for d in range(groups):
             peer = lax.rem(me + d, groups)
@@ -299,7 +325,7 @@
                 out[at_swir + q // RATIO_S, :, lane : lane + ws] = row[:, LANES : LANES + ws]
                 borders += [row[:, LANES - 2 : LANES], row[:, LANES + ws : LANES + ws + 2]]
             border = jnp.concatenate(borders, axis=1)
-            out[at_edge, :, 0 : border.shape[1]] = border
+            out[at_edge, :, edge_lane : edge_lane + edge_size] = border
             for side in going(d):
                 first = strip_place(d, side)
                 edge = edges[1, :, LANES - REACH :] if side == "right" else edges[0, :, :REACH]
@@ -307,41 +333,27 @@
                 for i in range(8 // nb):
                     lane = piece * (i % per_row)
                     out[first + i // per_row, :, lane : lane + piece] = flat[nb * i : nb * (i + 1)]
-
-    chunks = call(
+        for copy in copies[4:]:
+            copy.wait()
+
+    staged = call(
         pack,
-        tuple(shape(chunk_rows[d], nb, wc) for d in range(groups)),
+        tuple(shape(chunk_rows[d], nb, wc) for d in range(groups))
+        + (shape(h, w), jax.ShapeDtypeStruct(table.shape, BF16)),
         [
             pltpu.VMEM((hc, nb, full + 2 * LANES), F32),
             pltpu.VMEM((nb, hs, sfull + 2 * LANES), F32),
             pltpu.VMEM((2, h, LANES), F32),
-            pltpu.SemaphoreType.DMA((4,)),
+            pltpu.SemaphoreType.DMA((6,)),
         ],
-        room=VMEM_MOST,
-        in_specs=[ANY] * 3,
-    )(pan_image, jnp.transpose(vnir_bands, (1, 0, 2)), swir_bands)
+        cost=(0, 8_000_000),
+        in_specs=[ANY] * 4,
+    )(*(pltpu.with_memory_space_constraint(x, pltpu.HBM) for x in sources))
+    chunks, pan_held, table_held = staged[:groups], staged[groups], staged[groups + 1]
     got = [chunks[0]] + [
         lax.ppermute(chunks[d], "band", [(i, (i + d) % groups) for i in range(groups)])
         for d in range(1, groups)
     ]
-
-    mean_parts, fine_parts = split(cols["mean"]), split(cols["mean_fine"])
-    r_fine = split(fine_rows)
-    r_adj = split(lift.T)
-    table, place = stack_tables(
-        dict(
-            tall=np.concatenate([mean_parts[0], fine_parts[0]], axis=1),
-            tall_low=fine_parts[1],
-            fine=split(cols["fine"]),
-            rows=split(coarse_rows),
-            rows_fine=np.concatenate([r_fine[0], r_fine[1], r_fine[0]], axis=1),
-            low=split(cols["low"]),
-            pair=split(cols["pair"]),
-            up4=split(cols["up4"]),
-            up3=split(cols["up3"]),
-            adjoint=np.concatenate([r_adj[0], r_adj[0], r_adj[0], r_adj[1], r_adj[1]], axis=1),
-        )
-    )
 
     def take(ref, name, index=0, rows=None):
         starts, height, width = place[name]
@@ -373,75 +385,112 @@
         row_id = lax.axis_index("rows")
         return jnp.where(row_id == 0, 1, jnp.where(row_id == strips - 1, 2, 0))
 
-    def early(pan_ref, table_ref, order_ref, coarse_out, fine_out):
+    pairs_in = [(i, i ^ 1) for i in range(strips) if i ^ 1 < strips]
+    pairs_out = [(i, i + 1) for i in range(1, strips - 1, 2)]
+    pairs_out += [(j, i) for i, j in pairs_out]
+
+    def is_even():
+        return lax.rem(lax.axis_index("rows"), 2) == 0
+
+    def put(outs, index, up, down):
+        even = is_even()
+        outs[0][index] = jnp.where(even, up, down)
+        outs[1][index] = jnp.where(even, down, up)
+
+    def arrived(refs, index, low):
+        even = is_even()
+        inner, outer = refs[0][index], refs[1][index]
+        return jnp.where(even, outer, inner) if low else jnp.where(even, inner, outer)
+
+    def trade(inner, outer):
+        return lax.ppermute(inner, "rows", pairs_in), lax.ppermute(outer, "rows", pairs_out)
+
+    at_up, at_down = 2 * pad, 2 * pad + 16
+
+    def put_small(outs, first, ups, downs):
+        blank = jnp.zeros((2, LANES), F32)
+        for i in range(0, len(ups), 4):
+            up = ups[i : i + 4] + [blank] * (4 - len(ups[i : i + 4]))
+            down = downs[i : i + 4] + [blank] * (4 - len(downs[i : i + 4]))
+            put(outs, first + i // 4, jnp.concatenate(up, axis=0), jnp.concatenate(down, axis=0))
+
+    inner_fine = fine_tiles - 4
+    mid_low = 0
+    mid_sent = inner_fine
+
+    def early(pan_ref, table_ref, coarse_out, fine_out, *outs):
         panes = parts2(pan_ref[...])
         starts = [margin * k - 3 * LANES for k in range(1, frame_tiles - 1)]
         means, fines = shrink(
             windows(panes, starts, 6 * LANES), take(table_ref, "tall"), take(table_ref, "tall_low")
         )
         rc = both_parts(table_ref, "rows", row_variant(), 3)
-        coarse_out[...] = along_rows(rc, blocks(means, middle), blocks(fines, middle))
+        rows = along_rows(rc, blocks(means, middle), blocks(fines, middle))
+        coarse_out[...] = rows
         starts = [2 * LANES * k - LANES for k in range(1, pairs - 1)]
         col = dot3(windows(panes, starts, 4 * LANES), both_parts(table_ref, "fine"))
-        fine_out[...] = filter_rows(take(table_ref, "rows_fine"), blocks(col, pairs - 2))
-
-    coarse_mid, fine_mid = call(
+        rows = filter_rows(take(table_ref, "rows_fine"), blocks(col, pairs - 2))
+        fine_out[...] = rows[0:h]
+        for k in range(inner_fine):
+            at = slice(LANES * k, LANES * (k + 1))
+            put(outs, mid_low + k, rows[h : h + HALO, at], rows[h + HALO : h + 2 * HALO, at])
+
+    coarse_mid, fine_mid, mid_in, mid_out = call(
         early,
-        (shape(2 * pad + 32, LANES * middle), shape(h + 2 * HALO, 2 * LANES * (pairs - 2))),
+        (
+            shape(2 * pad + 32, LANES * middle),
+            shape(h, LANES * inner_fine),
+            shape(mid_sent, 8, LANES),
+            shape(mid_sent, 8, LANES),
+        ),
         cost=(2_000_000_000, 8_000_000),
-        in_specs=[VMEM, VMEM, ANY],
-    )(pan_image, table, chunks[0])
-
-    at_s = HALO * frame_tiles
-    at_ld = at_s + 2 * (sf // LANES)
+    )(pan_held, table_held)
+    mid_in, mid_out = trade(mid_in, mid_out)
+
+    border_tiles = -(-edge_size // LANES)
+    at_s = HALO * coarse_tiles
+    at_h = at_s + 2 * swir_tiles
+    at_ld = at_h + border_tiles
     at_d = at_ld + frame_tiles
-    at_low = at_d + -(-2 * frame_tiles // 8)
-    sent = at_low + fine_tiles
-
-    def assemble(pan_ref, table_ref, cm_ref, fm_ref, *rest):
+    at_low = at_d + -(-frame_tiles // 4)
+    sent = at_low + 4
+
+    def framed(main, borders, lane, reach):
+        blank = jnp.zeros((8, HALF - reach), F32)
+        left = borders[:, lane : lane + reach]
+        right = borders[:, lane + reach : lane + 2 * reach]
+        return jnp.concatenate([blank, left, main, right, blank], axis=1)
+
+    def assemble(pan_ref, table_ref, cm_ref, order_ref, order_too_ref, *rest):
         ins = rest[:groups]
-        x_out, s_out, up_out, down_out, ce_out, fe_out = rest[groups:]
+        x_out, s_out, ce_out, fe_out = rest[groups : groups + 4]
+        outs = rest[groups + 4 :]
         me = lax.axis_index("band")
 
         def gather(row, lane, size):
             rows = [ins[(groups - i) % groups][row, :, lane : lane + size] for i in range(groups)]
             return pltpu.roll(jnp.concatenate(rows, axis=0), nb * me, 0)
 
-        borders = gather(at_edge, 0, wc)
-        zeros = jnp.zeros((8, HALF), F32)
-
-        def framed(main, lane, reach):
-            return jnp.concatenate(
-                [
-                    zeros[:, : HALF - reach],
-                    borders[:, lane : lane + reach],
-                    main,
-                    borders[:, lane + reach : lane + 2 * reach],
-                    zeros[:, : HALF - reach],
-                ],
-                axis=1,
-            )
-
+        def tile(x, t):
+            return x[:, LANES * t : LANES * (t + 1)]
+
+        borders = gather(at_edge, edge_lane, edge_size)
+        blank = jnp.zeros((8, LANES * border_tiles - edge_size), F32)
+        borders = jnp.concatenate([borders, blank], axis=1)
+        for t in range(border_tiles):
+            put(outs, at_h + t, tile(borders, t), tile(borders, t))
+        mains = [gather(r, 0, wc) for r in range(hc)]
         for r in range(hc):
-            row = framed(gather(r, 0, wc), 2 * HALO * r, HALO)
-            x_out[r] = row
-            for t in range(frame_tiles):
-                tile = row[:, LANES * t : LANES * (t + 1)]
-                if r >= hc - HALO:
-                    up_out[frame_tiles * (r - hc + HALO) + t] = tile
-                if r < HALO:
-                    down_out[frame_tiles * r + t] = tile
-        per = sf // LANES
+            x_out[r] = framed(mains[r], borders, 2 * HALO * r, HALO)
+        for r in range(HALO):
+            for t in range(coarse_tiles):
+                put(outs, coarse_tiles * r + t, tile(mains[hc - HALO + r], t), tile(mains[r], t))
+        shorts = [gather(at_swir + q // RATIO_S, ws * (q % RATIO_S), ws) for q in range(hs)]
         for q in range(hs):
-            main = gather(at_swir + q // RATIO_S, ws * (q % RATIO_S), ws)
-            row = framed(main, 2 * HALO * hc + 4 * q, 2)
-            s_out[q] = row
-            for t in range(per):
-                tile = row[:, LANES * t : LANES * (t + 1)]
-                if q >= hs - 2:
-                    up_out[at_s + per * (q - hs + 2) + t] = tile
-                if q < 2:
-                    down_out[at_s + per * q + t] = tile
+            s_out[q] = framed(shorts[q], borders, 2 * HALO * hc + 4 * q, 2)
+        for q in range(2):
+            for t in range(swir_tiles):
+                put(outs, at_s + swir_tiles * q + t, tile(shorts[hs - 2 + q], t), tile(shorts[q], t))
 
         def strip(d, side, empty):
             first = strip_place(d, side)
@@ -466,118 +515,211 @@
         rm, rfine = shrink(right, take(table_ref, "tall", 0, inner), take(table_ref, "tall_low", 0, inner))
         rc = both_parts(table_ref, "rows", row_variant(), 3)
         edge = along_rows(rc, jnp.concatenate([lm, rm], axis=1), jnp.concatenate([lf, rfine], axis=1))
-        ce_out[...] = edge
+        ce_out[...] = edge[0 : 2 * pad]
         outer = tuple(jnp.concatenate([a, b], axis=0) for a, b in zip(left, right))
         fine_edge = filter_rows(
             take(table_ref, "rows_fine"), blocks(dot3(outer, both_parts(table_ref, "fine")), 2)
         )
-        fe_out[...] = fine_edge
-
-        def coarse(rows, k):
-            if k == 0:
-                return edge[rows, 0:LANES]
-            if k == frame_tiles - 1:
-                return edge[rows, LANES:]
-            return cm_ref[rows, LANES * (k - 1) : LANES * k]
-
-        first = 2 * pad
-        for out, at, dead in ((up_out, first, 0), (down_out, first + 16, HALO - 2)):
-            for k in range(frame_tiles):
-                out[at_ld + k] = coarse(slice(at + 8, at + 16), k)
-                small = coarse(slice(at, at + 8), k)[dead : dead + 2]
-                out[at_d + k // 4, 2 * (k % 4) : 2 * (k % 4) + 2, :] = small
-        for out, at in ((up_out, h), (down_out, h + HALO)):
-            for k in range(fine_tiles):
-                if k < 2:
-                    tile = fine_edge[at : at + 8, LANES * k : LANES * (k + 1)]
-                elif k >= fine_tiles - 2:
-                    lane = LANES * (k - fine_tiles + 4)
-                    tile = fine_edge[at : at + 8, lane : lane + LANES]
-                else:
-                    tile = fm_ref[at : at + 8, LANES * (k - 2) : LANES * (k - 1)]
-                out[at_low + k] = tile
-
-    x_loc, s_loc, up_send, down_send, coarse_edge, fine_edge = call(
+        fe_out[...] = fine_edge[0:h]
+        sides = jnp.concatenate([edge[:, :LANES], cm_ref[...], edge[:, LANES:]], axis=1)
+        ups, downs = [], []
+        for k in range(frame_tiles):
+            part = tile(sides, k)
+            put(outs, at_ld + k, part[at_up + 8 : at_up + 16], part[at_down + 8 : at_down + 16])
+            ups.append(part[at_up : at_up + 2])
+            downs.append(part[at_down + HALO - 2 : at_down + HALO])
+        put_small(outs, at_d, ups, downs)
+        for k in range(4):
+            at = slice(LANES * k, LANES * (k + 1))
+            put(outs, at_low + k, fine_edge[h : h + HALO, at], fine_edge[h + HALO : h + 2 * HALO, at])
+
+    x_loc, s_loc, coarse_edge, fine_edge, rest_in, rest_out = call(
         assemble,
         (
             shape(hc, BANDS, wf),
             shape(hs, BANDS, sf),
+            shape(2 * pad, 2 * LANES),
+            shape(h, 4 * LANES),
             shape(sent, 8, LANES),
             shape(sent, 8, LANES),
-            shape(2 * pad + 32, 2 * LANES),
-            shape(h + 2 * HALO, 4 * LANES),
         ),
         cost=(200_000_000, 3_000_000),
-    )(pan_image, table, coarse_mid, fine_mid, *got)
-    from_low = lax.ppermute(up_send, "rows", [(i, i + 1) for i in range(strips - 1)])
-    from_high = lax.ppermute(down_send, "rows", [(i + 1, i) for i in range(strips - 1)])
+        in_specs=[VMEM, VMEM, VMEM, ANY, ANY] + [VMEM] * groups,
+    )(pan_held, table_held, coarse_mid, mid_in, mid_out, *got)
+    rest_in, rest_out = trade(rest_in, rest_out)
+
+    turns = BANDS // 2 + 1
+    block_starts = [LANES * k for k in range(coarse_tiles)]
+    own_rows = range(2, hc + 2)
+    halo_rows = (0, 1, hc + 2, hc + 3)
+    whole_rows = range(2, hc - 2)
+    first_whole = RATIO_V * whole_rows[0]
+    whole_count = RATIO_V * len(whole_rows)
+
+    def lifted(rows, table_ref, store):
+        stack = windows(parts2(jnp.concatenate(rows, axis=0)), block_starts, 2 * LANES)
+        up = dot3(stack, both_parts(table_ref, "up4"))
+        size = 8 * len(rows)
+        for k in range(coarse_tiles):
+            for q in range(RATIO_V):
+                store(RATIO_V * k + q, up[size * k : size * (k + 1), LANES * q : LANES * (q + 1)])
+
+    def weighted(pairs):
+        value = None
+        for weight, x in pairs:
+            if weight != 0.0:
+                value = float(weight) * x if value is None else value + float(weight) * x
+        return value
+
+    def adjoint_of(table_ref, low):
+        p1 = low.astype(BF16)
+        over = low - p1.astype(F32)
+        p2 = over.astype(BF16)
+        p3 = (over - p2.astype(F32)).astype(BF16)
+        return dot(take(table_ref, "adjoint"), jnp.concatenate([p1, p2, p3, p1, p2], axis=0))
+
+    def tile_sum(x):
+        total = jnp.zeros((8, LANES), F32)
+        for k in range(x.shape[1] // LANES):
+            for t in range(x.shape[0] // 8):
+                total = total + x[8 * t : 8 * t + 8, LANES * k : LANES * (k + 1)]
+        return total
+
+    def joined_low(low, top, end):
+        return jnp.concatenate([low[0:HALO] + top, low[HALO : h - HALO], low[h - HALO : h] + end], axis=0)
+
+    def inside(
+        pan_ref, x_ref, s_ref, mid_in_ref, mid_out_ref, fm_ref, table_ref,
+        y_out, v_out, acc_out, s_out, diff_out, q_out,
+    ):
+        def store(index, value):
+            y_out[index] = value
+
+        lifted([x_ref[r] for r in range(hc)], table_ref, store)
+        rows = parts2(jnp.concatenate([s_ref[q] for q in range(hs)], axis=0))
+        s_cols = dot3(windows(rows, block_starts[:swir_tiles], 2 * LANES), both_parts(table_ref, "up3"))
+        s_out[...] = blocks(s_cols, swir_tiles)
+
+        mid = (mid_in_ref, mid_out_ref)
+        top, end = (
+            jnp.concatenate([arrived(mid, mid_low + k, low) for k in range(inner_fine)], axis=1)
+            for low in (True, False)
+        )
+        low = joined_low(fm_ref[...], top, end)
+        diff = pan_ref[:, 2 * LANES : w - 2 * LANES] - low
+        adjoint = adjoint_of(table_ref, low)
+        for k in range(inner_fine):
+            at = slice(LANES * k, LANES * (k + 1))
+            diff_out[k] = diff[:, at]
+            q_out[k] = adjoint[:, at]
+        acc_out[turns + 1] = tile_sum(low)
+
+        def tile_step(k, carry):
+            accs, accv = list(carry[:turns]), carry[turns]
+            ys = {m: y_out[k, pl.ds(8 * (m - 2), 8), :] for m in own_rows}
+            for m in own_rows:
+                z = weighted((gram[m, other], ys[other]) for other in own_rows)
+                accs[0] = accs[0] + z * ys[m]
+                for i in range(1, turns):
+                    accs[i] = accs[i] + z * pltpu.roll(ys[m], i, 0)
+                accv = accv + float(rise[m]) * ys[m]
+            for m in whole_rows:
+                for p in range(RATIO_V):
+                    r = RATIO_V * m + p - first_whole
+                    v_out[k, pl.ds(8 * r, 8), :] = weighted((C4[t, p], ys[m + t]) for t in range(5) if C4[t, p] != 0.0)
+            return tuple(accs) + (accv,)
+
+        zero = jnp.zeros((8, LANES), F32)
+        first = lax.fori_loop(0, fine_tiles, tile_step, (zero,) * (turns + 1))
+        for i in range(turns + 1):
+            acc_out[i] = first[i]
+
+    y_own, v_own, acc_own, s_own, diff_mid, q_mid = call(
+        inside,
+        (
+            shape(fine_tiles, 8 * hc, LANES),
+            shape(fine_tiles, 8 * whole_count, LANES),
+            shape(turns + 2, 8, LANES),
+            shape(8 * hs, wc),
+            shape(inner_fine, h, LANES),
+            shape(inner_fine, hc + 4, LANES),
+        ),
+        cost=(2_000_000_000, 8_000_000),
+    )(pan_held, x_loc, s_loc, mid_in, mid_out, fine_mid, table_held)
 
     def moments(
-        pan_ref, x_ref, s_ref, lo_ref, hi_ref, cm_ref, fm_ref, ce_ref, fe_ref,
-        table_ref,
+        pan_ref, x_ref, y_ref, acc_ref, scol_ref, diff_ref, qmid_ref,
+        rest_in_ref, rest_out_ref, cm_ref, ce_ref, fe_ref, table_ref,
         mom_out, y_out, diff_out, ugap_out, dgap_out, s_out,
         both, ulow, q_ref,
     ):
         me = lax.axis_index("band")
         row_id = lax.axis_index("rows")
-
-        def tiles(ref, first, number):
-            return jnp.concatenate([ref[first + t] for t in range(number)], axis=1)
+        rest = (rest_in_ref, rest_out_ref)
+
+        def tiles(refs, low, indices):
+            return jnp.concatenate([arrived(refs, i, low) for i in indices], axis=1)
+
+        def halo(first, per, reach, start, count):
+            sides = []
+            for low, base in ((True, start[0]), (False, start[1])):
+                borders = tiles(rest, low, range(at_h, at_h + border_tiles))
+                rows = []
+                for r in range(count):
+                    main = tiles(rest, low, range(first + per * r, first + per * (r + 1)))
+                    rows.append(framed(main, borders, base + 2 * reach * r, reach))
+                sides.append(rows)
+            return sides
+
+        x_low, x_high = halo(0, coarse_tiles, HALO, (2 * HALO * (hc - HALO), 0), HALO)
 
         def x_row(r):
             if r < 0:
-                return tiles(lo_ref, frame_tiles * (HALO + r), frame_tiles)
+                return x_low[HALO + r]
             if r >= hc:
-                return tiles(hi_ref, frame_tiles * (r - hc), frame_tiles)
+                return x_high[r - hc]
             return x_ref[r]
 
-        block_starts = [LANES * k for k in range(coarse_tiles)]
-        frame = parts2(jnp.concatenate([x_row(r) for r in range(-2, hc + 2)], axis=0))
-        up = dot3(windows(frame, block_starts, 2 * LANES), both_parts(table_ref, "up4"))
-        size = 8 * (hc + 4)
-        for k in range(coarse_tiles):
-            for q in range(RATIO_V):
-                y_out[RATIO_V * k + q] = up[size * k : size * (k + 1), LANES * q : LANES * (q + 1)]
-
-        low = jnp.concatenate([fe_ref[0:h, 0 : 2 * LANES], fm_ref[0:h, :], fe_ref[0:h, 2 * LANES :]], axis=1)
-        top = low[0:HALO] + tiles(lo_ref, at_low, fine_tiles)
-        end = low[h - HALO : h] + tiles(hi_ref, at_low, fine_tiles)
-        low = jnp.concatenate([top, low[HALO : h - HALO], end], axis=0)
-        diff = pan_ref[...] - low
-        p1 = low.astype(BF16)
-        rest = low - p1.astype(F32)
-        p2 = rest.astype(BF16)
-        p3 = (rest - p2.astype(F32)).astype(BF16)
-        adjoint = dot(take(table_ref, "adjoint"), jnp.concatenate([p1, p2, p3, p1, p2], axis=0))
-        psum = jnp.zeros((8, LANES), F32)
-        for k in range(fine_tiles):
-            at = slice(LANES * k, LANES * (k + 1))
+        def store(index, value):
+            y_out[index] = value
+
+        lifted([x_row(r) for r in (-2, -1, hc, hc + 1)], table_ref, store)
+
+        top, end = (tiles(rest, low, range(at_low, at_low + 4)) for low in (True, False))
+        low = joined_low(fe_ref[...], top, end)
+        diff = jnp.concatenate([pan_ref[:, : 2 * LANES], pan_ref[:, w - 2 * LANES :]], axis=1) - low
+        adjoint = adjoint_of(table_ref, low)
+        psum = acc_ref[turns + 1] + tile_sum(low)
+        outer_tiles = (0, 1, fine_tiles - 2, fine_tiles - 1)
+        for i, k in enumerate(outer_tiles):
+            at = slice(LANES * i, LANES * (i + 1))
             diff_out[k] = diff[:, at]
             q_ref[k] = adjoint[:, at]
-            for t in range(h // 8):
-                psum = psum + low[8 * t : 8 * t + 8, at]
+        for k in range(inner_fine):
+            diff_out[k + 2] = diff_ref[k]
+            q_ref[k + 2] = qmid_ref[k]
 
         zero = jnp.zeros((8, LANES), F32)
-        turns = BANDS // 2 + 1
 
         def tile_step(k, carry):
             accs = list(carry[:turns])
             accp, accv = carry[turns], carry[turns + 1]
-            ys = [y_out[k, pl.ds(8 * m, 8), :] for m in range(hc + 4)]
+            ys = {m: y_ref[k, pl.ds(8 * (m - 2), 8), :] for m in own_rows}
+            for i, m in enumerate(halo_rows):
+                ys[m] = y_out[k, pl.ds(8 * i, 8), :]
+            for m in halo_rows:
+                near = weighted((gram[m, other], ys[other]) for other in own_rows)
+                whole = near + weighted((gram[m, other], ys[other]) for other in halo_rows)
+                accs[0] = accs[0] + ys[m] * (near + whole)
+                for i in range(1, turns):
+                    accs[i] = accs[i] + whole * pltpu.roll(ys[m], i, 0) + ys[m] * pltpu.roll(near, i, 0)
+                accv = accv + float(rise[m]) * ys[m]
             for m in range(hc + 4):
-                z = None
-                for other in range(hc + 4):
-                    if gram[m, other] != 0.0:
-                        term = float(gram[m, other]) * ys[other]
-                        z = term if z is None else z + term
-                accs[0] = accs[0] + z * ys[m]
-                for i in range(1, turns):
-                    accs[i] = accs[i] + z * pltpu.roll(ys[m], i, 0)
                 accp = accp + ys[m] * q_ref[k, pl.ds(m, 1), :]
-                accv = accv + float(rise[m]) * ys[m]
             return tuple(accs) + (accp, accv)
 
-        first = lax.fori_loop(0, fine_tiles, tile_step, (zero,) * (turns + 2))
+        start = tuple(acc_ref[i] for i in range(turns)) + (zero, acc_ref[turns])
+        first = lax.fori_loop(0, fine_tiles, tile_step, start)
 
         below = jnp.where(row_id > 0, 1.0, 0.0).astype(F32)
         above = jnp.where(row_id < strips - 1, 1.0, 0.0).astype(F32)
@@ -618,34 +760,31 @@
                 ugap_out[:, at] = u_all[size * k : size * (k + 1)] - low_k
 
         column = lax.broadcasted_iota(jnp.int32, (1, wf), 1) - HALF + me * wc
-        inside = jnp.where((column >= 0) & (column < groups * wc), 1.0, 0.0).astype(F32)
+        valid = jnp.where((column >= 0) & (column < groups * wc), 1.0, 0.0).astype(F32)
 
         def own(rows):
             return jnp.concatenate([ce_ref[rows, 0:LANES], cm_ref[rows, :], ce_ref[rows, LANES:]], axis=1)
 
-        def small(ref):
-            return jnp.concatenate(
-                [ref[at_d + k // 4, 2 * (k % 4) : 2 * (k % 4) + 2, :] for k in range(frame_tiles)], axis=1
-            )
+        def small(low):
+            rows = [arrived(rest, at_d + k // 4, low)[2 * (k % 4) : 2 * (k % 4) + 2] for k in range(frame_tiles)]
+            return jnp.concatenate(rows, axis=1)
 
         both[...] = own(slice(0, pad))
-        both[0:2] = both[0:2] + small(lo_ref)
-        both[hc - 2 : hc] = both[hc - 2 : hc] + small(hi_ref)
+        both[0:2] = both[0:2] + small(True)
+        both[hc - 2 : hc] = both[hc - 2 : hc] + small(False)
         detail = both[...]
         both[...] = own(slice(pad, 2 * pad))
-        both[0:HALO] = both[0:HALO] + tiles(lo_ref, at_ld, frame_tiles)
-        both[hc - HALO : hc] = both[hc - HALO : hc] + tiles(hi_ref, at_ld, frame_tiles)
-        dlow_rows = windows(parts2(both[...] * inside), block_starts, 2 * LANES)
+        both[0:HALO] = both[0:HALO] + tiles(rest, True, range(at_ld, at_ld + frame_tiles))
+        both[hc - HALO : hc] = both[hc - HALO : hc] + tiles(rest, False, range(at_ld, at_ld + frame_tiles))
+        dlow_rows = windows(parts2(both[...] * valid), block_starts, 2 * LANES)
         dlow = blocks(dot3(dlow_rows, both_parts(table_ref, "low")), coarse_tiles)
         dgap_out[...] = detail[:, HALF : HALF + wc] - dlow
         both[:, 0:wc] = dlow
 
-        per = sf // LANES
-        s_rows = [tiles(lo_ref, at_s + per * q, per) for q in range(2)]
-        s_rows += [s_ref[r] for r in range(hs)]
-        s_rows += [tiles(hi_ref, at_s + per * q, per) for q in range(2)]
-        s_parts = windows(parts2(jnp.concatenate(s_rows, axis=0)), block_starts[:swir_tiles], 2 * LANES)
-        s_cols = blocks(dot3(s_parts, both_parts(table_ref, "up3")), swir_tiles)
+        s_low, s_high = halo(at_s, swir_tiles, 2, (2 * HALO * hc + 4 * (hs - 2), 2 * HALO * hc), 2)
+        s_parts = windows(parts2(jnp.concatenate(s_low + s_high, axis=0)), block_starts[:swir_tiles], 2 * LANES)
+        s_around = blocks(dot3(s_parts, both_parts(table_ref, "up3")), swir_tiles)
+        s_cols = jnp.concatenate([s_around[0:16], scol_ref[...], s_around[16:32]], axis=0)
         for m in range(hs):
             for p in range(RATIO_S):
                 value = None
@@ -700,11 +839,11 @@
         turned = pltpu.roll(table, HALF, 1)
         mom_out[...] = jnp.where(lane[0:4] < HALF, table[0:4], turned[4:8])
 
-    mom, y_up, diff, ugap, dgap, s_up = call(
+    mom, y_halo, diff, ugap, dgap, s_up = call(
         moments,
         (
             shape(4, LANES),
-            shape(fine_tiles, 8 * (hc + 4), LANES),
+            shape(fine_tiles, 32, LANES),
             shape(fine_tiles, h, LANES),
             shape(8 * hc, wc),
             shape(pad, wc),
@@ -717,13 +856,17 @@
         ],
         cost=(1_000_000_000, 8_000_000),
     )(
-        pan_image, x_loc, s_loc, from_low, from_high, coarse_mid, fine_mid, coarse_edge, fine_edge, table,
+        pan_held, x_loc, y_own, acc_own, s_own, diff_mid, q_mid,
+        rest_in, rest_out, coarse_mid, coarse_edge, fine_edge, table_held,
     )
     devices = groups * strips
     spread = jnp.broadcast_to(mom[None], (devices,) + mom.shape)
     sums = lax.all_to_all(spread, ("rows", "band"), split_axis=0, concat_axis=0, tiled=True)
 
-    def finish(sums_ref, y_ref, diff_ref, ugap_ref, dgap_ref, s_ref, vnir_out, swir_out, tiles, sems):
+    def finish(
+        sums_ref, y_ref, yh_ref, v_ref, diff_ref, ugap_ref, dgap_ref, s_ref,
+        vnir_out, swir_out, tiles, swir, sems,
+    ):
         lane = lax.broadcasted_iota(jnp.int32, (8, LANES), 1)
         sub = lax.broadcasted_iota(jnp.int32, (8, LANES), 0)
         eye = lane == sub
@@ -731,6 +874,7 @@
         while len(terms) > 1:
             terms = [sum(terms[i : i + 2][1:], terms[i]) for i in range(0, len(terms), 2)]
         total = jnp.concatenate([terms[0], pltpu.roll(terms[0], HALF, 1)], axis=0)
+
         def column(x, index):
             return jnp.broadcast_to(x[:, index : index + 1], (8, LANES))
 
@@ -741,37 +885,22 @@
             return jnp.sum(x, axis=0, keepdims=True)
 
         def solve(matrix, rhs):
-            work = jnp.where(lane == 8, rhs, matrix)
+            cols = [column(matrix, j) for j in range(BANDS)] + [rhs]
+            inverse = jnp.zeros((8, LANES), F32)
             for k in range(BANDS):
-                pivot_row = work[k : k + 1, :] / column(work, k)[k : k + 1, :]
-                other = work - column(work, k) * pivot_row
-                work = jnp.where(sub == k, pivot_row, other)
-            return column(work, 8)
+                pivot = 1.0 / jnp.broadcast_to(cols[k][k : k + 1], (8, LANES))
+                inverse = jnp.where(sub == k, pivot, inverse)
+                factor = jnp.where(sub == k, 0.0, cols[k] * pivot)
+                for j in range(k + 1, BANDS + 1):
+                    cols[j] = cols[j] - factor * jnp.broadcast_to(cols[j][k : k + 1], (8, LANES))
+            return cols[BANDS] * inverse
 
         n1 = float(fine_pixels)
         mean_v = column(total, 41) / n1
         mean_p = column(total, 43) / n1
         cov_v = pltpu.roll(total, LANES - 32, 1) / n1 - mean_v * across(mean_v)
         cov_p = column(total, 40) / n1 - mean_v * mean_p
-        fit = solve(cov_v, cov_p)
-        gain = cov_p / down(cov_p * fit)
-
-        def tile_step(k, carry):
-            for m in range(hc):
-                ys = [y_ref[k, pl.ds(8 * (m + t), 8), :] for t in range(5)]
-                for p in range(RATIO_V):
-                    r = RATIO_V * m + p
-                    value = gain * diff_ref[k, pl.ds(r, 1), :]
-                    for t in range(5):
-                        if C4[t, p] != 0.0:
-                            value = value + float(C4[t, p]) * ys[t]
-                    tiles[k, pl.ds(r, 8, stride=h), :] = value
-            pltpu.make_async_copy(
-                tiles.at[k], vnir_out.at[:, pl.ds(pl.multiple_of(LANES * k, LANES), LANES)], sems.at[k]
-            ).start()
-            return carry
-
-        lax.fori_loop(0, fine_tiles, tile_step, 0)
+        gain = cov_p / down(cov_p * solve(cov_v, cov_p))
 
         n2 = float(fine_pixels // (RATIO_V * RATIO_V))
         mean_l = column(total, 17) / n2
@@ -784,10 +913,40 @@
         cov_dd = column(total, 20) / n2 - mean_d * mean_d
         gain_row = across(gain)
         a2 = cov_ll + gain * across(cov_ld) + cov_ld * gain_row + gain * gain_row * cov_dd
-        b2 = cov_ls + gain * across(cov_sd)
-        b2 = jnp.where(lane < BANDS, b2, 0.0)
+        b2 = jnp.where(lane < BANDS, cov_ls + gain * across(cov_sd), 0.0)
         target = jnp.broadcast_to(jnp.sum(b2, axis=1, keepdims=True) / BANDS, (8, LANES))
-        fit2 = solve(a2, target)
+
+        def sent_tile(k):
+            lanes = pl.ds(pl.multiple_of(LANES * k, LANES), LANES)
+            return pltpu.make_async_copy(tiles.at[k], vnir_out.at[:, lanes], sems.at[k])
+
+        def tile_step(k, carry):
+            work, inverse = carry
+            here = sub == k
+            row = down(jnp.where(here, work, 0.0))
+            col = jnp.sum(jnp.where(lane == k, work, 0.0), axis=1, keepdims=True)
+            pivot = 1.0 / jnp.where(k < BANDS, down(jnp.where(here[:, 0:1], col, 0.0)), 1.0)
+            inverse = jnp.where(here, pivot, inverse)
+            work = work - jnp.where(here, 0.0, col * pivot) * row
+
+            ys = {m: y_ref[k, pl.ds(8 * (m - 2), 8), :] for m in own_rows}
+            for i, m in enumerate(halo_rows):
+                ys[m] = yh_ref[k, pl.ds(8 * i, 8), :]
+            for m in range(hc):
+                for p in range(RATIO_V):
+                    r = RATIO_V * m + p
+                    if m in whole_rows:
+                        value = v_ref[k, pl.ds(8 * (r - first_whole), 8), :]
+                    else:
+                        value = weighted((C4[t, p], ys[m + t]) for t in range(5) if C4[t, p] != 0.0)
+                    value = value + gain * diff_ref[k, pl.ds(r, 1), :]
+                    tiles[k, pl.ds(r, 8, stride=h), :] = value
+            sent_tile(k).start()
+            return work, inverse
+
+        start = (jnp.where(lane == BANDS, target, a2), jnp.zeros((8, LANES), F32))
+        work, inverse = lax.fori_loop(0, fine_tiles, tile_step, start)
+        fit2 = column(work, BANDS) * inverse
         numer = down(fit2 * b2)
         share_row = numer / down(fit2 * target)
         share = jnp.sum(jnp.where(eye, jnp.broadcast_to(share_row, (8, LANES)), 0.0), axis=1, keepdims=True)
@@ -796,23 +955,28 @@
         for r in range(hc):
             seen = jnp.sum(fit_col * ugap_ref[8 * r : 8 * r + 8, :], axis=0, keepdims=True)
             seen = seen + scale * dgap_ref[r : r + 1, :]
-            swir_out[r] = s_ref[r] + share * seen
+            swir[r] = s_ref[r] + share * seen
+        last = pltpu.make_async_copy(swir, swir_out, sems.at[fine_tiles])
+        last.start()
 
         def drain(k, carry):
-            pltpu.make_async_copy(
-                tiles.at[k], vnir_out.at[:, pl.ds(pl.multiple_of(LANES * k, LANES), LANES)], sems.at[k]
-            ).wait()
+            sent_tile(k).wait()
             return carry
 
         lax.fori_loop(0, fine_tiles, drain, 0)
+        last.wait()
 
     joined_vnir, joined_swir = call(
         finish,
         (shape(BANDS * h, w), shape(hc, BANDS, wc)),
-        [pltpu.VMEM((fine_tiles, BANDS * h, LANES), F32), pltpu.SemaphoreType.DMA((fine_tiles,))],
+        [
+            pltpu.VMEM((fine_tiles, BANDS * h, LANES), F32),
+            pltpu.VMEM((hc, BANDS, wc), F32),
+            pltpu.SemaphoreType.DMA((fine_tiles + 1,)),
+        ],
         cost=(100_000_000, 8_000_000),
-        out_specs=(ANY, VMEM),
-    )(sums, y_up, diff, ugap, dgap, s_up)
+        out_specs=(ANY, ANY),
+    )(sums, y_own, y_halo, v_own, diff, ugap, dgap, s_up)
     return joined_vnir.reshape(BANDS, h, w), jnp.transpose(joined_swir, (1, 0, 2))
 
 

time: 50.5 us -> 47.7 us (0.945)
  local copies, waits for them, and re-layouts: 4 us -> 0.01 us
  starting transfers between devices: 10.7 us -> 13.7 us
  waiting for transfers between devices: 4.01 us -> 1.85 us
  Pallas kernels: 13.1 us -> 13.9 us
    unnamed x8 -> x0, local copies, waits for them, and re-layouts: 3.99 us -> none
    ppermute x2 -> x4, waiting for transfers between devices: 4 us -> 0.6 us  [the longest x2 0.59 us: trade(): lax.ppermute(inner, 'rows', pairs_in)]
    ppermute x2 -> x4, starting transfers between devices: 2.73 us -> 5.79 us  [the longest x2 4.46 us: trade(): lax.ppermute(inner, 'rows', pairs_in)]
    pallas_call x4 -> x5, Pallas kernels: 8.28 us -> 10 us  [the longest x1 2.79 us: local(): call(moments, (shape(4, LANES), shape(fine_tiles, 32, LANES), shape(fine_...]
    ppermute x3, waiting for transfers between devices: 0.01 us -> 1.25 us  [local(): lax.ppermute(chunks[d], 'band', [(i, (i + d) % groups) for i in range(gro...]
    pallas_call x1, Pallas kernels: 4.78 us -> 3.84 us  [local(): call(finish, (shape(BANDS * h, w), shape(hc, BANDS, wc)), [pltpu.VMEM((fi...]
  transfers between devices with their start and end apart: 5 -> 7, of which waited for: 1 -> 3; matrix products, arithmetic and copies ran while one was open for 0% -> 0% of each run, Pallas kernels for 3% -> 8%
where the time goes in v3:
time: 47.7 us; the launch traced here: 47.5 us
  blocking collectives  17.3 us (36%)
  Pallas kernels  13.9 us (29%)
  starting transfers between devices  13.7 us (29%)
  waiting for transfers between devices  1.85 us (4%)
  between operations  0.71 us (1%)
    all_to_all x1, blocking collectives, local(): lax.all_to_all(spread, ('rows', 'band'), split_axis=0, concat_axis=0, til...  17.3 us
    ppermute x3, starting transfers between devices, local(): lax.ppermute(chunks[d], 'band', [(i, (i + d) % groups) for i in range(gro...  7.93 us
    ppermute x2, starting transfers between devices, trade(): lax.ppermute(inner, 'rows', pairs_in)  4.46 us
    pallas_call x1, Pallas kernels, local(): call(finish, (shape(BANDS * h, w), shape(hc, BANDS, wc)), [pltpu.VMEM((fi...  3.84 us
    pallas_call x1, Pallas kernels, local(): call(moments, (shape(4, LANES), shape(fine_tiles, 32, LANES), shape(fine_...  2.79 us
    pallas_call x1, Pallas kernels, local(): call(inside, (shape(fine_tiles, 8 * hc, LANES), shape(fine_tiles, 8 * who...  2.49 us
    pallas_call x1, Pallas kernels, local(): call(pack, tuple((shape(chunk_rows[d], nb, wc) for d in range(groups))) +...  2.43 us
    pallas_call x1, Pallas kernels, local(): call(early, (shape(2 * pad + 32, LANES * middle), shape(h, LANES * inner_...  1.53 us
  transfers between devices with their start and end apart: 7, of which 3 were waited for; matrix products, arithmetic and copies ran while one was open for 0% of the time, Pallas kernels for 8%

profile of v3, /device:TPU:0, one launch (start us, length us, event | category | flops | bytes accessed | tf_op | source)
XLA Modules:
  0.0 47.5 jit_solution(14527874713355673905)
XLA Ops:
  0.6 2.4 %shard_map.59 = (f32[14,2,768]{2,1,0:T(2,128)S(1)}, f32[15,2,768]{2,1,0:T(2,128)S(1)}, f32[14,2,768]{2,1,0:T(2,128)S(1)}, f32[15,2,768]{2,1,0:T(2,128)S(1)}, f32...) custom-call(f32[48,3072]{1,0:T(8,128)} %pan_ref.1, f32[12,2,3072]{2,1,0:T(2,128)} %bitcast.3, f32[2,4,1024]{2,1,0:T(4,128)} %swir_ref.1, ...), custom_call_target="tpu_custom_call" | custom-call | bytes 8000000 | tf_op jit(solution)/shard_map/pallas_call | solution.py:339
  3.1 4.1 %collective-permute-start.3 = (f32[14,2,768]{2,1,0:T(2,128)S(1)}, f32[14,2,768]{2,1,0:T(2,128)S(1)}, u32[]{:S(2)}, u32[]{:S(2)}) collective-permute-start(f32[14,2,768]{2,1,0:T(2,128)S(1)} %get-tuple-element.39), channel_id=1, source_target_pairs={{0,2},{1,3},{2,0},{3,1},{4,6},{5,7},{6,4},{7,5},{8,10},{9,11},{10,... | collective-permute-start | bytes 258056 | tf_op jit(solution)/shard_map/ppermute | solution.py:354
  7.2 1.6 %collective-permute-start.2 = (f32[15,2,768]{2,1,0:T(2,128)S(1)}, f32[15,2,768]{2,1,0:T(2,128)S(1)}, u32[]{:S(2)}, u32[]{:S(2)}) collective-permute-start(f32[15,2,768]{2,1,0:T(2,128)S(1)} %get-tuple-element.38), channel_id=1, source_target_pairs={{0,1},{1,2},{2,3},{3,0},{4,5},{5,6},{6,7},{7,4},{8,9},{9,10},{10,1... | collective-permute-start | bytes 276488 | tf_op jit(solution)/shard_map/ppermute | solution.py:354
  8.7 2.2 %collective-permute-start.4 = (f32[15,2,768]{2,1,0:T(2,128)S(1)}, f32[15,2,768]{2,1,0:T(2,128)S(1)}, u32[]{:S(2)}, u32[]{:S(2)}) collective-permute-start(f32[15,2,768]{2,1,0:T(2,128)S(1)} %get-tuple-element.40), channel_id=1, source_target_pairs={{0,3},{1,0},{2,1},{3,2},{4,7},{5,4},{6,5},{7,6},{8,11},{9,8},{10,9... | collective-permute-start | bytes 276488 | tf_op jit(solution)/shard_map/ppermute | solution.py:354
  11.0 1.5 %shard_map.60 = (f32[64,640]{1,0:T(8,128)S(1)}, f32[48,2560]{1,0:T(8,128)S(1)}, f32[20,8,128]{2,1,0:T(8,128)S(1)}, f32[20,8,128]{2,1,0:T(8,128)S(1)}) custom-call(f32[48,3072]{1,0:T(8,128)S(1)} %get-tuple-element.32.pan_ref, bf16[7120,256]{1,0:T(8,128)(2,1)S(1)} %get-tuple-element.33.table_ref), custom_call_target="tpu_custom_call" | custom-call | flops 2000000000 | bytes 8000000 | tf_op jit(solution)/shard_map/pallas_call | solution.py:438
  12.5 0.1 collective-permute-start
  12.6 0.7 %collective-permute-start.1 = (f32[20,8,128]{2,1,0:T(8,128)S(1)}, f32[20,8,128]{2,1,0:T(8,128)S(1)}, u32[]{:S(2)}, u32[]{:S(2)}) collective-permute-start(f32[20,8,128]{2,1,0:T(8,128)S(1)} %get-tuple-element.36), channel_id=1, source_target_pairs={{4,8},{12,16},{20,24},{8,4},{16,12},{24,20},{5,9},{13,17},{21,25},... | collective-permute-start | bytes 245768 | tf_op jit(solution)/shard_map/ppermute | solution.py:406
  13.3 0.6 %collective-permute-done.order_ref.mid_in_ref = f32[20,8,128]{2,1,0:T(8,128)S(1)} collective-permute-done((f32[20,8,128]{2,1,0:T(8,128)S(1)}, f32[20,8,128]{2,1,0:T(8,128)S(1)}, u32[]{:S(2)}, u32[]{:S(2)}) %collective-permute-start) | collective-permute-done | bytes 81952 | tf_op jit(solution)/shard_map/ppermute | solution.py:406
  13.9 0.0 collective-permute-done.1.order_too_ref.mid_out_ref
  13.9 0.0 collective-permute-done.3.rest_2_
  13.9 0.4 collective-permute-done.2.rest_1_
  14.2 0.9 %collective-permute-done.4.rest_3_ = f32[15,2,768]{2,1,0:T(2,128)S(1)} collective-permute-done((f32[15,2,768]{2,1,0:T(2,128)S(1)}, f32[15,2,768]{2,1,0:T(2,128)S(1)}, u32[]{:S(2)}, u32[]{:S(2)}) %collective-permute-start.4) | collective-permute-done | bytes 92192 | tf_op jit(solution)/shard_map/ppermute | solution.py:354
  15.1 0.8 %shard_map.61 = (f32[12,8,896]{2,1,0:T(8,128)S(1)}, f32[4,8,384]{2,1,0:T(8,128)S(1)}, f32[32,256]{1,0:T(8,128)S(1)}, f32[48,512]{1,0:T(8,128)S(1)}, f32[67,8,128...) custom-call(f32[48,3072]{1,0:T(8,128)S(1)} %get-tuple-element.32.pan_ref, bf16[7120,256]{1,0:T(8,128)(2,1)S(1)} %get-tuple-element.33.table_ref, ...), custom_call_target="tpu_custom_call" | custom-call | flops 200000000 | bytes 3000000 | tf_op jit(solution)/shard_map/pallas_call | solution.py:536
  15.9 4.4 %collective-permute-start.5 = (f32[67,8,128]{2,1,0:T(8,128)S(1)}, f32[67,8,128]{2,1,0:T(8,128)S(1)}, u32[]{:S(2)}, u32[]{:S(2)}) collective-permute-start(f32[67,8,128]{2,1,0:T(8,128)S(1)} %get-tuple-element.49), channel_id=1, source_target_pairs={{0,4},{4,0},{8,12},{12,8},{16,20},{20,16},{24,28},{28,24},{1,5},{5... | collective-permute-start | bytes 823304 | tf_op jit(solution)/shard_map/ppermute | solution.py:406
  20.3 0.7 %collective-permute-start.6 = (f32[67,8,128]{2,1,0:T(8,128)S(1)}, f32[67,8,128]{2,1,0:T(8,128)S(1)}, u32[]{:S(2)}, u32[]{:S(2)}) collective-permute-start(f32[67,8,128]{2,1,0:T(8,128)S(1)} %get-tuple-element.50), channel_id=1, source_target_pairs={{4,8},{12,16},{20,24},{8,4},{16,12},{24,20},{5,9},{13,17},{21,25},... | collective-permute-start | bytes 823304 | tf_op jit(solution)/shard_map/ppermute | solution.py:406
  21.0 2.5 %shard_map.62 = (f32[24,96,128]{2,1,0:T(8,128)S(1)}, f32[24,256,128]{2,1,0:T(8,128)S(1)}, f32[7,8,128]{2,1,0:T(8,128)S(1)}, f32[32,768]{1,0:T(8,128)S(1)}, f32[2...) custom-call(f32[48,3072]{1,0:T(8,128)S(1)} %get-tuple-element.32.pan_ref, f32[12,8,896]{2,1,0:T(8,128)S(1)} %get-tuple-element.41.x_ref, ...), custom_call_target="tpu_custom_call" | custom-call | flops 2000000000 | bytes 8000000 | tf_op jit(solution)/shard_map/pallas_call | solution.py:637
  23.5 0.0 collective-permute-done.5.rest_in_ref
  23.5 0.0 collective-permute-done.6.rest_out_ref
  23.5 2.8 %shard_map.63 = (f32[4,128]{1,0:T(4,128)S(1)}, f32[24,32,128]{2,1,0:T(8,128)S(1)}, f32[24,48,128]{2,1,0:T(8,128)S(1)}, f32[96,768]{1,0:T(8,128)S(1)}, f32[16,768]{1,0:T(8,128)S(1)}, /*index=5*/f32[12,8,768]{2,1,0:T(8,128)S(1)}) custom-call(f32[48,3072]{1,0:T(8,128)S(1)} %get-tuple-element.32.pan_ref, f32[12,8,896]{2,1,0:T(8,128)S(1)} %get-tuple-element.41.x_ref, ...), custom_call_target="tpu_custom_call" | custom-call | flops 1000000000 | bytes 8000000 | tf_op jit(solution)/shard_map/pallas_call | solution.py:842
  26.3 17.3 %all_to_all.5.sums_ref = f32[32,4,128]{2,1,0:T(4,128)S(1)} all-to-all(f32[32,4,128]{2,1,0:T(4,128)S(1)} %broadcast_in_dim.2), channel_id=1, replica_groups=mesh['rows'=8,'band'=4] {'rows','band'}, dimensions={0} | all-to-all | bytes 131072 | tf_op jit(solution)/shard_map/all_to_all | solution.py:864
  43.6 3.8 %shard_map.64 = (f32[384,3072]{1,0:T(8,128)}, f32[12,8,768]{2,1,0:T(8,128)}) custom-call(f32[32,4,128]{2,1,0:T(4,128)S(1)} %all_to_all.5.sums_ref, f32[24,96,128]{2,1,0:T(8,128)S(1)} %get-tuple-element.44.y_ref, f32[24,32,128]{2,1,0:T(8,128)S(1)} %get-tuple-element.54.yh_ref, f32[24,256,128]{2,1,0:T(8,128)S(1)} %get-tuple-element.55.v_ref, ...), custom_call_target="tpu_custom_call" | custom-call | flops 100000000 | bytes 8000000 | tf_op jit(solution)/shard_map/pallas_call | solution.py:969
  (1 shorter events, 0.0 us)
Async XLA Ops:
  3.1 10.8 %collective-permute-start.3 = (f32[14,2,768]{2,1,0:T(2,128)S(1)}, f32[14,2,768]{2,1,0:T(2,128)S(1)}, u32[]{:S(2)}, u32[]{:S(2)}) collective-permute-start(f32[14,2,768]{2,1,0:T(2,128)S(1)} %get-tuple-element.39), channel_id=1, source_target_pairs={{0,2},{1,3},{2,0},{3,1},{4,6},{5,7},{6,4},{7,5},{8,10},{9,11},{10,... | collective-permute-start | bytes 258056 | tf_op jit(solution)/shard_map/ppermute | solution.py:354
  7.2 7.1 %collective-permute-start.2 = (f32[15,2,768]{2,1,0:T(2,128)S(1)}, f32[15,2,768]{2,1,0:T(2,128)S(1)}, u32[]{:S(2)}, u32[]{:S(2)}) collective-permute-start(f32[15,2,768]{2,1,0:T(2,128)S(1)} %get-tuple-element.38), channel_id=1, source_target_pairs={{0,1},{1,2},{2,3},{3,0},{4,5},{5,6},{6,7},{7,4},{8,9},{9,10},{10,1... | collective-permute-start | bytes 276488 | tf_op jit(solution)/shard_map/ppermute | solution.py:354
  8.7 6.4 %collective-permute-start.4 = (f32[15,2,768]{2,1,0:T(2,128)S(1)}, f32[15,2,768]{2,1,0:T(2,128)S(1)}, u32[]{:S(2)}, u32[]{:S(2)}) collective-permute-start(f32[15,2,768]{2,1,0:T(2,128)S(1)} %get-tuple-element.40), channel_id=1, source_target_pairs={{0,3},{1,0},{2,1},{3,2},{4,7},{5,4},{6,5},{7,6},{8,11},{9,8},{10,9... | collective-permute-start | bytes 276488 | tf_op jit(solution)/shard_map/ppermute | solution.py:354
  12.5 1.3 %collective-permute-start = (f32[20,8,128]{2,1,0:T(8,128)S(1)}, f32[20,8,128]{2,1,0:T(8,128)S(1)}, u32[]{:S(2)}, u32[]{:S(2)}) collective-permute-start(f32[20,8,128]{2,1,0:T(8,128)S(1)} %get-tuple-element.35), channel_id=1, source_target_pairs={{0,4},{4,0},{8,12},{12,8},{16,20},{20,16},{24,28},{28,24},{1,5},{5... | collective-permute-start | bytes 245768 | tf_op jit(solution)/shard_map/ppermute | solution.py:406
  12.6 1.3 %collective-permute-start.1 = (f32[20,8,128]{2,1,0:T(8,128)S(1)}, f32[20,8,128]{2,1,0:T(8,128)S(1)}, u32[]{:S(2)}, u32[]{:S(2)}) collective-permute-start(f32[20,8,128]{2,1,0:T(8,128)S(1)} %get-tuple-element.36), channel_id=1, source_target_pairs={{4,8},{12,16},{20,24},{8,4},{16,12},{24,20},{5,9},{13,17},{21,25},... | collective-permute-start | bytes 245768 | tf_op jit(solution)/shard_map/ppermute | solution.py:406
  15.9 7.6 %collective-permute-start.5 = (f32[67,8,128]{2,1,0:T(8,128)S(1)}, f32[67,8,128]{2,1,0:T(8,128)S(1)}, u32[]{:S(2)}, u32[]{:S(2)}) collective-permute-start(f32[67,8,128]{2,1,0:T(8,128)S(1)} %get-tuple-element.49), channel_id=1, source_target_pairs={{0,4},{4,0},{8,12},{12,8},{16,20},{20,16},{24,28},{28,24},{1,5},{5... | collective-permute-start | bytes 823304 | tf_op jit(solution)/shard_map/ppermute | solution.py:406
  20.3 3.2 %collective-permute-start.6 = (f32[67,8,128]{2,1,0:T(8,128)S(1)}, f32[67,8,128]{2,1,0:T(8,128)S(1)}, u32[]{:S(2)}, u32[]{:S(2)}) collective-permute-start(f32[67,8,128]{2,1,0:T(8,128)S(1)} %get-tuple-element.50), channel_id=1, source_target_pairs={{4,8},{12,16},{20,24},{8,4},{16,12},{24,20},{5,9},{13,17},{21,25},... | collective-permute-start | bytes 823304 | tf_op jit(solution)/shard_map/ppermute | solution.py:406

commit v4 on v3

--- a/solution.py
+++ b/solution.py
@@ -64,6 +64,12 @@
     high = np.asarray(table, np.float64).astype(np.float32).astype(ml_dtypes.bfloat16)
     low = (np.asarray(table, np.float64) - high.astype(np.float64)).astype(np.float32)
     return np.stack([high, low.astype(ml_dtypes.bfloat16)])
+
+
+def split3(table):
+    high, middle = split(table)
+    low = np.asarray(table, np.float64) - high.astype(np.float64) - middle.astype(np.float64)
+    return high, middle, low.astype(np.float32).astype(ml_dtypes.bfloat16)
 
 
 def band_matrix(size, taps):
@@ -126,6 +132,31 @@
     for m in range(hc):
         for p in range(RATIO_V):
             out[RATIO_V * m + p, m : m + 5] = C4[:, p]
+    return out
+
+
+def adjoint_rows(h):
+    hc = h // RATIO_V
+    reach = TAPS_V // 2
+    size = h + 2 * reach
+    lift = np.zeros((size, hc + 8))
+    for r in range(size):
+        m, p = divmod(r - reach, RATIO_V)
+        lift[r, m + 2 : m + 7] = C4[:, p]
+    fine = np.zeros((size, h))
+    for r in range(size):
+        for t in range(-reach, reach + 1):
+            if 0 <= r - reach + t < h:
+                fine[r, r - reach + t] = KF[t + reach]
+    out = np.zeros((3, -(-(hc + 9) // 16) * 16, h))
+    for variant in range(3):
+        keep = np.ones((size, 1))
+        if variant == 1:
+            keep[:reach] = 0.0
+        if variant == 2:
+            keep[h + reach :] = 0.0
+        out[variant, : hc + 8] = (lift * keep).T @ fine
+        out[variant, hc + 8] = (fine * keep).sum(axis=0)
     return out
 
 
@@ -270,7 +301,7 @@
 
     mean_parts, fine_parts = split(cols["mean"]), split(cols["mean_fine"])
     r_fine = split(fine_rows)
-    r_adj = split(lift.T)
+    r_adj = split3(adjoint_rows(h))
     table, place = stack_tables(
         dict(
             tall=np.concatenate([mean_parts[0], fine_parts[0]], axis=1),
@@ -282,7 +313,7 @@
             pair=split(cols["pair"]),
             up4=split(cols["up4"]),
             up3=split(cols["up3"]),
-            adjoint=np.concatenate([r_adj[0], r_adj[0], r_adj[0], r_adj[1], r_adj[1]], axis=1),
+            adjoint=np.concatenate([r_adj[i] for i in (0, 0, 0, 1, 1, 2)], axis=2),
         )
     )
 
@@ -403,7 +434,8 @@
         return jnp.where(even, outer, inner) if low else jnp.where(even, inner, outer)
 
     def trade(inner, outer):
-        return lax.ppermute(inner, "rows", pairs_in), lax.ppermute(outer, "rows", pairs_out)
+        outer = lax.ppermute(outer, "rows", pairs_out)
+        return lax.ppermute(inner, "rows", pairs_in), outer
 
     at_up, at_down = 2 * pad, 2 * pad + 16
 
@@ -415,45 +447,36 @@
             put(outs, first + i // 4, jnp.concatenate(up, axis=0), jnp.concatenate(down, axis=0))
 
     inner_fine = fine_tiles - 4
-    mid_low = 0
-    mid_sent = inner_fine
-
-    def early(pan_ref, table_ref, coarse_out, fine_out, *outs):
+
+    def early(pan_ref, table_ref, coarse_out, fine_out, col_out):
         panes = parts2(pan_ref[...])
         starts = [margin * k - 3 * LANES for k in range(1, frame_tiles - 1)]
         means, fines = shrink(
             windows(panes, starts, 6 * LANES), take(table_ref, "tall"), take(table_ref, "tall_low")
         )
         rc = both_parts(table_ref, "rows", row_variant(), 3)
-        rows = along_rows(rc, blocks(means, middle), blocks(fines, middle))
-        coarse_out[...] = rows
+        coarse_out[...] = along_rows(rc, blocks(means, middle), blocks(fines, middle))
         starts = [2 * LANES * k - LANES for k in range(1, pairs - 1)]
-        col = dot3(windows(panes, starts, 4 * LANES), both_parts(table_ref, "fine"))
-        rows = filter_rows(take(table_ref, "rows_fine"), blocks(col, pairs - 2))
-        fine_out[...] = rows[0:h]
-        for k in range(inner_fine):
-            at = slice(LANES * k, LANES * (k + 1))
-            put(outs, mid_low + k, rows[h : h + HALO, at], rows[h + HALO : h + 2 * HALO, at])
-
-    coarse_mid, fine_mid, mid_in, mid_out = call(
+        col = blocks(dot3(windows(panes, starts, 4 * LANES), both_parts(table_ref, "fine")), pairs - 2)
+        col_out[...] = col
+        fine_out[...] = filter_rows(take(table_ref, "rows_fine"), col)
+
+    coarse_mid, fine_mid, col_mid = call(
         early,
         (
             shape(2 * pad + 32, LANES * middle),
+            shape(h + 2 * HALO, LANES * inner_fine),
             shape(h, LANES * inner_fine),
-            shape(mid_sent, 8, LANES),
-            shape(mid_sent, 8, LANES),
         ),
         cost=(2_000_000_000, 8_000_000),
     )(pan_held, table_held)
-    mid_in, mid_out = trade(mid_in, mid_out)
 
     border_tiles = -(-edge_size // LANES)
     at_s = HALO * coarse_tiles
     at_h = at_s + 2 * swir_tiles
     at_ld = at_h + border_tiles
     at_d = at_ld + frame_tiles
-    at_low = at_d + -(-frame_tiles // 4)
-    sent = at_low + 4
+    sent = at_d + -(-frame_tiles // 4)
 
     def framed(main, borders, lane, reach):
         blank = jnp.zeros((8, HALF - reach), F32)
@@ -461,10 +484,10 @@
         right = borders[:, lane + reach : lane + 2 * reach]
         return jnp.concatenate([blank, left, main, right, blank], axis=1)
 
-    def assemble(pan_ref, table_ref, cm_ref, order_ref, order_too_ref, *rest):
+    def assemble(pan_ref, table_ref, cm_ref, *rest):
         ins = rest[:groups]
-        x_out, s_out, ce_out, fe_out = rest[groups : groups + 4]
-        outs = rest[groups + 4 :]
+        x_out, s_out, ce_out, fe_out, col_out = rest[groups : groups + 5]
+        outs = rest[groups + 5 :]
         me = lax.axis_index("band")
 
         def gather(row, lane, size):
@@ -517,10 +540,9 @@
         edge = along_rows(rc, jnp.concatenate([lm, rm], axis=1), jnp.concatenate([lf, rfine], axis=1))
         ce_out[...] = edge[0 : 2 * pad]
         outer = tuple(jnp.concatenate([a, b], axis=0) for a, b in zip(left, right))
-        fine_edge = filter_rows(
-            take(table_ref, "rows_fine"), blocks(dot3(outer, both_parts(table_ref, "fine")), 2)
-        )
-        fe_out[...] = fine_edge[0:h]
+        col = blocks(dot3(outer, both_parts(table_ref, "fine")), 2)
+        col_out[...] = col
+        fe_out[...] = filter_rows(take(table_ref, "rows_fine"), col)
         sides = jnp.concatenate([edge[:, :LANES], cm_ref[...], edge[:, LANES:]], axis=1)
         ups, downs = [], []
         for k in range(frame_tiles):
@@ -529,29 +551,28 @@
             ups.append(part[at_up : at_up + 2])
             downs.append(part[at_down + HALO - 2 : at_down + HALO])
         put_small(outs, at_d, ups, downs)
-        for k in range(4):
-            at = slice(LANES * k, LANES * (k + 1))
-            put(outs, at_low + k, fine_edge[h : h + HALO, at], fine_edge[h + HALO : h + 2 * HALO, at])
-
-    x_loc, s_loc, coarse_edge, fine_edge, rest_in, rest_out = call(
+
+    x_loc, s_loc, coarse_edge, fine_edge, col_edge, rest_in, rest_out = call(
         assemble,
         (
             shape(hc, BANDS, wf),
             shape(hs, BANDS, sf),
             shape(2 * pad, 2 * LANES),
+            shape(h + 2 * HALO, 4 * LANES),
             shape(h, 4 * LANES),
             shape(sent, 8, LANES),
             shape(sent, 8, LANES),
         ),
         cost=(200_000_000, 3_000_000),
-        in_specs=[VMEM, VMEM, VMEM, ANY, ANY] + [VMEM] * groups,
-    )(pan_held, table_held, coarse_mid, mid_in, mid_out, *got)
+        in_specs=[VMEM] * (groups + 3),
+    )(pan_held, table_held, coarse_mid, *got)
     rest_in, rest_out = trade(rest_in, rest_out)
 
     turns = BANDS // 2 + 1
     block_starts = [LANES * k for k in range(coarse_tiles)]
     own_rows = range(2, hc + 2)
     halo_rows = (0, 1, hc + 2, hc + 3)
+    around = (-2, -1) + halo_rows + (hc + 4, hc + 5)
     whole_rows = range(2, hc - 2)
     first_whole = RATIO_V * whole_rows[0]
     whole_count = RATIO_V * len(whole_rows)
@@ -571,26 +592,17 @@
                 value = float(weight) * x if value is None else value + float(weight) * x
         return value
 
-    def adjoint_of(table_ref, low):
-        p1 = low.astype(BF16)
-        over = low - p1.astype(F32)
+    def adjoint_of(table_ref, col):
+        p1 = col.astype(BF16)
+        over = col - p1.astype(F32)
         p2 = over.astype(BF16)
         p3 = (over - p2.astype(F32)).astype(BF16)
-        return dot(take(table_ref, "adjoint"), jnp.concatenate([p1, p2, p3, p1, p2], axis=0))
-
-    def tile_sum(x):
-        total = jnp.zeros((8, LANES), F32)
-        for k in range(x.shape[1] // LANES):
-            for t in range(x.shape[0] // 8):
-                total = total + x[8 * t : 8 * t + 8, LANES * k : LANES * (k + 1)]
-        return total
-
-    def joined_low(low, top, end):
-        return jnp.concatenate([low[0:HALO] + top, low[HALO : h - HALO], low[h - HALO : h] + end], axis=0)
+        weights = take(table_ref, "adjoint", row_variant())
+        return dot(weights, jnp.concatenate([p1, p2, p3, p1, p2, p1], axis=0))
 
     def inside(
-        pan_ref, x_ref, s_ref, mid_in_ref, mid_out_ref, fm_ref, table_ref,
-        y_out, v_out, acc_out, s_out, diff_out, q_out,
+        pan_ref, x_ref, s_ref, fm_ref, fe_ref, colm_ref, cole_ref, table_ref,
+        y_out, v_out, acc_out, s_out, diff_out, q_out, *outs,
     ):
         def store(index, value):
             y_out[index] = value
@@ -600,22 +612,23 @@
         s_cols = dot3(windows(rows, block_starts[:swir_tiles], 2 * LANES), both_parts(table_ref, "up3"))
         s_out[...] = blocks(s_cols, swir_tiles)
 
-        mid = (mid_in_ref, mid_out_ref)
-        top, end = (
-            jnp.concatenate([arrived(mid, mid_low + k, low) for k in range(inner_fine)], axis=1)
-            for low in (True, False)
-        )
-        low = joined_low(fm_ref[...], top, end)
-        diff = pan_ref[:, 2 * LANES : w - 2 * LANES] - low
-        adjoint = adjoint_of(table_ref, low)
-        for k in range(inner_fine):
+        def joined(outer, inner):
+            return jnp.concatenate([outer[:, : 2 * LANES], inner, outer[:, 2 * LANES :]], axis=1)
+
+        low = joined(fe_ref[...], fm_ref[...])
+        diff = pan_ref[...] - low[0:h]
+        adjoint = adjoint_of(table_ref, joined(cole_ref[...], colm_ref[...]))
+        total = jnp.zeros((1, LANES), F32)
+        for k in range(fine_tiles):
             at = slice(LANES * k, LANES * (k + 1))
             diff_out[k] = diff[:, at]
             q_out[k] = adjoint[:, at]
-        acc_out[turns + 1] = tile_sum(low)
+            total = total + adjoint[hc + 8 : hc + 9, at]
+            put(outs, k, low[h : h + HALO, at], low[h + HALO : h + 2 * HALO, at])
+        acc_out[turns + 2] = jnp.concatenate([total, jnp.zeros((7, LANES), F32)], axis=0)
 
         def tile_step(k, carry):
-            accs, accv = list(carry[:turns]), carry[turns]
+            accs, accv, accp = list(carry[:turns]), carry[turns], carry[turns + 1]
             ys = {m: y_out[k, pl.ds(8 * (m - 2), 8), :] for m in own_rows}
             for m in own_rows:
                 z = weighted((gram[m, other], ys[other]) for other in own_rows)
@@ -623,35 +636,39 @@
                 for i in range(1, turns):
                     accs[i] = accs[i] + z * pltpu.roll(ys[m], i, 0)
                 accv = accv + float(rise[m]) * ys[m]
+                accp = accp + ys[m] * q_out[k, pl.ds(m + 2, 1), :]
             for m in whole_rows:
                 for p in range(RATIO_V):
                     r = RATIO_V * m + p - first_whole
                     v_out[k, pl.ds(8 * r, 8), :] = weighted((C4[t, p], ys[m + t]) for t in range(5) if C4[t, p] != 0.0)
-            return tuple(accs) + (accv,)
+            return tuple(accs) + (accv, accp)
 
         zero = jnp.zeros((8, LANES), F32)
-        first = lax.fori_loop(0, fine_tiles, tile_step, (zero,) * (turns + 1))
-        for i in range(turns + 1):
+        first = lax.fori_loop(0, fine_tiles, tile_step, (zero,) * (turns + 2))
+        for i in range(turns + 2):
             acc_out[i] = first[i]
 
-    y_own, v_own, acc_own, s_own, diff_mid, q_mid = call(
+    q_rows = -(-(hc + 9) // 16) * 16
+    y_own, v_own, acc_own, s_own, diff, q_own, low_in, low_out = call(
         inside,
         (
             shape(fine_tiles, 8 * hc, LANES),
             shape(fine_tiles, 8 * whole_count, LANES),
-            shape(turns + 2, 8, LANES),
+            shape(turns + 3, 8, LANES),
             shape(8 * hs, wc),
-            shape(inner_fine, h, LANES),
-            shape(inner_fine, hc + 4, LANES),
+            shape(fine_tiles, h, LANES),
+            shape(fine_tiles, q_rows, LANES),
+            shape(fine_tiles, 8, LANES),
+            shape(fine_tiles, 8, LANES),
         ),
         cost=(2_000_000_000, 8_000_000),
-    )(pan_held, x_loc, s_loc, mid_in, mid_out, fine_mid, table_held)
+    )(pan_held, x_loc, s_loc, fine_mid, fine_edge, col_mid, col_edge, table_held)
+    low_in, low_out = trade(low_in, low_out)
 
     def moments(
-        pan_ref, x_ref, y_ref, acc_ref, scol_ref, diff_ref, qmid_ref,
-        rest_in_ref, rest_out_ref, cm_ref, ce_ref, fe_ref, table_ref,
-        mom_out, y_out, diff_out, ugap_out, dgap_out, s_out,
-        both, ulow, q_ref,
+        x_ref, y_ref, acc_ref, scol_ref, q_ref, rest_in_ref, rest_out_ref, cm_ref, ce_ref, table_ref,
+        mom_out, y_out, ugap_out, dgap_out, s_out,
+        both, ulow,
     ):
         me = lax.axis_index("band")
         row_id = lax.axis_index("rows")
@@ -683,21 +700,7 @@
         def store(index, value):
             y_out[index] = value
 
-        lifted([x_row(r) for r in (-2, -1, hc, hc + 1)], table_ref, store)
-
-        top, end = (tiles(rest, low, range(at_low, at_low + 4)) for low in (True, False))
-        low = joined_low(fe_ref[...], top, end)
-        diff = jnp.concatenate([pan_ref[:, : 2 * LANES], pan_ref[:, w - 2 * LANES :]], axis=1) - low
-        adjoint = adjoint_of(table_ref, low)
-        psum = acc_ref[turns + 1] + tile_sum(low)
-        outer_tiles = (0, 1, fine_tiles - 2, fine_tiles - 1)
-        for i, k in enumerate(outer_tiles):
-            at = slice(LANES * i, LANES * (i + 1))
-            diff_out[k] = diff[:, at]
-            q_ref[k] = adjoint[:, at]
-        for k in range(inner_fine):
-            diff_out[k + 2] = diff_ref[k]
-            q_ref[k + 2] = qmid_ref[k]
+        lifted([x_row(m - 2) for m in around], table_ref, store)
 
         zero = jnp.zeros((8, LANES), F32)
 
@@ -705,7 +708,7 @@
             accs = list(carry[:turns])
             accp, accv = carry[turns], carry[turns + 1]
             ys = {m: y_ref[k, pl.ds(8 * (m - 2), 8), :] for m in own_rows}
-            for i, m in enumerate(halo_rows):
+            for i, m in enumerate(around):
                 ys[m] = y_out[k, pl.ds(8 * i, 8), :]
             for m in halo_rows:
                 near = weighted((gram[m, other], ys[other]) for other in own_rows)
@@ -714,11 +717,11 @@
                 for i in range(1, turns):
                     accs[i] = accs[i] + whole * pltpu.roll(ys[m], i, 0) + ys[m] * pltpu.roll(near, i, 0)
                 accv = accv + float(rise[m]) * ys[m]
-            for m in range(hc + 4):
-                accp = accp + ys[m] * q_ref[k, pl.ds(m, 1), :]
+            for m in around:
+                accp = accp + ys[m] * q_ref[k, pl.ds(m + 2, 1), :]
             return tuple(accs) + (accp, accv)
 
-        start = tuple(acc_ref[i] for i in range(turns)) + (zero, acc_ref[turns])
+        start = tuple(acc_ref[i] for i in range(turns)) + (acc_ref[turns + 1], acc_ref[turns])
         first = lax.fori_loop(0, fine_tiles, tile_step, start)
 
         below = jnp.where(row_id > 0, 1.0, 0.0).astype(F32)
@@ -834,17 +837,16 @@
         singles += [(40, first[turns]), (41, first[turns + 1])]
         for index, acc in singles:
             table = jnp.where(lane == index, column_of(acc), table)
-        total = jnp.sum(jnp.sum(psum, axis=0, keepdims=True), axis=1, keepdims=True)
+        total = jnp.sum(jnp.sum(acc_ref[turns + 2], axis=0, keepdims=True), axis=1, keepdims=True)
         table = jnp.where(lane == 43, total, table)
         turned = pltpu.roll(table, HALF, 1)
         mom_out[...] = jnp.where(lane[0:4] < HALF, table[0:4], turned[4:8])
 
-    mom, y_halo, diff, ugap, dgap, s_up = call(
+    mom, y_halo, ugap, dgap, s_up = call(
         moments,
         (
             shape(4, LANES),
-            shape(fine_tiles, 32, LANES),
-            shape(fine_tiles, h, LANES),
+            shape(fine_tiles, 8 * len(around), LANES),
             shape(8 * hc, wc),
             shape(pad, wc),
             shape(hc, BANDS, wc),
@@ -852,20 +854,19 @@
         [
             pltpu.VMEM((pad, wf), F32),
             pltpu.VMEM((8 * hc, wc), F32),
-            pltpu.VMEM((fine_tiles, hc + 4, LANES), F32),
         ],
         cost=(1_000_000_000, 8_000_000),
     )(
-        pan_held, x_loc, y_own, acc_own, s_own, diff_mid, q_mid,
-        rest_in, rest_out, coarse_mid, coarse_edge, fine_edge, table_held,
+        x_loc, y_own, acc_own, s_own, q_own, rest_in, rest_out, coarse_mid, coarse_edge, table_held,
     )
     devices = groups * strips
+    mom, low_in, low_out = lax.optimization_barrier((mom, low_in, low_out))
     spread = jnp.broadcast_to(mom[None], (devices,) + mom.shape)
     sums = lax.all_to_all(spread, ("rows", "band"), split_axis=0, concat_axis=0, tiled=True)
 
     def finish(
-        sums_ref, y_ref, yh_ref, v_ref, diff_ref, ugap_ref, dgap_ref, s_ref,
-        vnir_out, swir_out, tiles, swir, sems,
+        sums_ref, y_ref, yh_ref, v_ref, diff_ref, low_in_ref, low_out_ref, ugap_ref, dgap_ref, s_ref,
+        vnir_out, swir_out, tiles, swir, ends, sems,
     ):
         lane = lax.broadcasted_iota(jnp.int32, (8, LANES), 1)
         sub = lax.broadcasted_iota(jnp.int32, (8, LANES), 0)
@@ -930,8 +931,12 @@
             work = work - jnp.where(here, 0.0, col * pivot) * row
 
             ys = {m: y_ref[k, pl.ds(8 * (m - 2), 8), :] for m in own_rows}
-            for i, m in enumerate(halo_rows):
-                ys[m] = yh_ref[k, pl.ds(8 * i, 8), :]
+            for i, m in enumerate(around):
+                if m in halo_rows:
+                    ys[m] = yh_ref[k, pl.ds(8 * i, 8), :]
+            lows = (low_in_ref, low_out_ref)
+            ends[k, 0:HALO, :] = diff_ref[k, 0:HALO, :] - arrived(lows, k, True)
+            ends[k, HALO:, :] = diff_ref[k, h - HALO :, :] - arrived(lows, k, False)
             for m in range(hc):
                 for p in range(RATIO_V):
                     r = RATIO_V * m + p
@@ -939,7 +944,13 @@
                         value = v_ref[k, pl.ds(8 * (r - first_whole), 8), :]
                     else:
                         value = weighted((C4[t, p], ys[m + t]) for t in range(5) if C4[t, p] != 0.0)
-                    value = value + gain * diff_ref[k, pl.ds(r, 1), :]
+                    if r < HALO:
+                        detail = ends[k, pl.ds(r, 1), :]
+                    elif r >= h - HALO:
+                        detail = ends[k, pl.ds(r - h + 2 * HALO, 1), :]
+                    else:
+                        detail = diff_ref[k, pl.ds(r, 1), :]
+                    value = value + gain * detail
                     tiles[k, pl.ds(r, 8, stride=h), :] = value
             sent_tile(k).start()
             return work, inverse
@@ -972,11 +983,12 @@
         [
             pltpu.VMEM((fine_tiles, BANDS * h, LANES), F32),
             pltpu.VMEM((hc, BANDS, wc), F32),
+            pltpu.VMEM((fine_tiles, 2 * HALO, LANES), F32),
             pltpu.SemaphoreType.DMA((fine_tiles + 1,)),
         ],
         cost=(100_000_000, 8_000_000),
         out_specs=(ANY, ANY),
-    )(sums, y_own, y_halo, v_own, diff, ugap, dgap, s_up)
+    )(sums, y_own, y_halo, v_own, diff, low_in, low_out, ugap, dgap, s_up)
     return joined_vnir.reshape(BANDS, h, w), jnp.transpose(joined_swir, (1, 0, 2))
 
 

time: 47.7 us -> 45.6 us (0.956)
  blocking collectives: 17.3 us -> 15.5 us
  starting transfers between devices: 13.7 us -> 12.4 us
  waiting for transfers between devices: 1.85 us -> 2.63 us
    all_to_all x1, blocking collectives: 17.3 us -> 15.5 us  [local(): lax.all_to_all(spread, ('rows', 'band'), split_axis=0, concat_axis=0, til...]
    ppermute x3, waiting for transfers between devices: 1.25 us -> 2.62 us  [local(): lax.ppermute(chunks[d], 'band', [(i, (i + d) % groups) for i in range(gro...]
    ppermute x4, starting transfers between devices: 5.79 us -> 4.44 us  [the longest x2 3.11 us: trade(): return (lax.ppermute(inner, 'rows', pairs_in), outer)]
    ppermute x4, waiting for transfers between devices: 0.6 us -> 0.01 us  [the longest x2 0.01 us: trade(): outer = lax.ppermute(outer, 'rows', pairs_out)]
  transfers between devices with their start and end apart: 7 -> 7, of which waited for: 3 -> 3; matrix products, arithmetic and copies ran while one was open for 0% -> 0% of each run, Pallas kernels for 8% -> 16%
where the time goes in v4:
time: 45.6 us; the launch traced here: 45.4 us
  blocking collectives  15.5 us (34%)
  Pallas kernels  14.2 us (31%)
  starting transfers between devices  12.4 us (27%)
  waiting for transfers between devices  2.63 us (6%)
  between operations  0.71 us (2%)
    all_to_all x1, blocking collectives, local(): lax.all_to_all(spread, ('rows', 'band'), split_axis=0, concat_axis=0, til...  15.5 us
    ppermute x3, starting transfers between devices, local(): lax.ppermute(chunks[d], 'band', [(i, (i + d) % groups) for i in range(gro...  7.93 us
    pallas_call x1, Pallas kernels, local(): call(finish, (shape(BANDS * h, w), shape(hc, BANDS, wc)), [pltpu.VMEM((fi...  3.92 us
    ppermute x2, starting transfers between devices, trade(): return (lax.ppermute(inner, 'rows', pairs_in), outer)  3.11 us
    pallas_call x1, Pallas kernels, local(): call(moments, (shape(4, LANES), shape(fine_tiles, 8 * len(around), LANES)...  2.78 us
    pallas_call x1, Pallas kernels, local(): call(inside, (shape(fine_tiles, 8 * hc, LANES), shape(fine_tiles, 8 * who...  2.76 us
    ppermute x3, waiting for transfers between devices, local(): lax.ppermute(chunks[d], 'band', [(i, (i + d) % groups) for i in range(gro...  2.62 us
    pallas_call x1, Pallas kernels, local(): call(pack, tuple((shape(chunk_rows[d], nb, wc) for d in range(groups))) +...  2.45 us
  transfers between devices with their start and end apart: 7, of which 3 were waited for; matrix products, arithmetic and copies ran while one was open for 0% of the time, Pallas kernels for 16%

profile of v4, /device:TPU:0, one launch (start us, length us, event | category | flops | bytes accessed | tf_op | source)
XLA Modules:
  0.0 45.4 jit_solution(17752312969080103864)
XLA Ops:
  0.6 2.5 %shard_map.59 = (f32[14,2,768]{2,1,0:T(2,128)S(1)}, f32[15,2,768]{2,1,0:T(2,128)S(1)}, f32[14,2,768]{2,1,0:T(2,128)S(1)}, f32[15,2,768]{2,1,0:T(2,128)S(1)}, f32...) custom-call(f32[48,3072]{1,0:T(8,128)} %pan_ref.1, f32[12,2,3072]{2,1,0:T(2,128)} %bitcast.3, f32[2,4,1024]{2,1,0:T(4,128)} %swir_ref.1, ...), custom_call_target="tpu_custom_call" | custom-call | bytes 8000000 | tf_op jit(solution)/shard_map/pallas_call | solution.py:370
  3.1 4.1 %collective-permute-start.1 = (f32[14,2,768]{2,1,0:T(2,128)S(1)}, f32[14,2,768]{2,1,0:T(2,128)S(1)}, u32[]{:S(2)}, u32[]{:S(2)}) collective-permute-start(f32[14,2,768]{2,1,0:T(2,128)S(1)} %get-tuple-element.41), channel_id=1, source_target_pairs={{0,2},{1,3},{2,0},{3,1},{4,6},{5,7},{6,4},{7,5},{8,10},{9,11},{10,... | collective-permute-start | bytes 258056 | tf_op jit(solution)/shard_map/ppermute | solution.py:385
  7.2 1.6 %collective-permute-start = (f32[15,2,768]{2,1,0:T(2,128)S(1)}, f32[15,2,768]{2,1,0:T(2,128)S(1)}, u32[]{:S(2)}, u32[]{:S(2)}) collective-permute-start(f32[15,2,768]{2,1,0:T(2,128)S(1)} %get-tuple-element.40), channel_id=1, source_target_pairs={{0,1},{1,2},{2,3},{3,0},{4,5},{5,6},{6,7},{7,4},{8,9},{9,10},{10,1... | collective-permute-start | bytes 276488 | tf_op jit(solution)/shard_map/ppermute | solution.py:385
  8.8 2.2 %collective-permute-start.2 = (f32[15,2,768]{2,1,0:T(2,128)S(1)}, f32[15,2,768]{2,1,0:T(2,128)S(1)}, u32[]{:S(2)}, u32[]{:S(2)}) collective-permute-start(f32[15,2,768]{2,1,0:T(2,128)S(1)} %get-tuple-element.42), channel_id=1, source_target_pairs={{0,3},{1,0},{2,1},{3,2},{4,7},{5,4},{6,5},{7,6},{8,11},{9,8},{10,9... | collective-permute-start | bytes 276488 | tf_op jit(solution)/shard_map/ppermute | solution.py:385
  11.0 1.5 %shard_map.60 = (f32[64,640]{1,0:T(8,128)S(1)}, f32[64,2560]{1,0:T(8,128)S(1)}, f32[48,2560]{1,0:T(8,128)S(1)}) custom-call(f32[48,3072]{1,0:T(8,128)S(1)} %get-tuple-element.36.pan_ref, bf16[7296,256]{1,0:T(8,128)(2,1)S(1)} %get-tuple-element.37.table_ref), custom_call_target="tpu_custom_call" | custom-call | flops 2000000000 | bytes 8000000 | tf_op jit(solution)/shard_map/pallas_call | solution.py:464
  12.5 1.0 %collective-permute-done.1.rest_2_ = f32[14,2,768]{2,1,0:T(2,128)S(1)} collective-permute-done((f32[14,2,768]{2,1,0:T(2,128)S(1)}, f32[14,2,768]{2,1,0:T(2,128)S(1)}, u32[]{:S(2)}, u32[]{:S(2)}) %collective-permute-start.1) | collective-permute-done | bytes 86048 | tf_op jit(solution)/shard_map/ppermute | solution.py:385
  13.5 0.7 %collective-permute-done.rest_1_ = f32[15,2,768]{2,1,0:T(2,128)S(1)} collective-permute-done((f32[15,2,768]{2,1,0:T(2,128)S(1)}, f32[15,2,768]{2,1,0:T(2,128)S(1)}, u32[]{:S(2)}, u32[]{:S(2)}) %collective-permute-start) | collective-permute-done | bytes 92192 | tf_op jit(solution)/shard_map/ppermute | solution.py:385
  14.3 0.9 %collective-permute-done.2.rest_3_ = f32[15,2,768]{2,1,0:T(2,128)S(1)} collective-permute-done((f32[15,2,768]{2,1,0:T(2,128)S(1)}, f32[15,2,768]{2,1,0:T(2,128)S(1)}, u32[]{:S(2)}, u32[]{:S(2)}) %collective-permute-start.2) | collective-permute-done | bytes 92192 | tf_op jit(solution)/shard_map/ppermute | solution.py:385
  15.2 0.8 %shard_map.61 = (f32[12,8,896]{2,1,0:T(8,128)S(1)}, f32[4,8,384]{2,1,0:T(8,128)S(1)}, f32[32,256]{1,0:T(8,128)S(1)}, f32[64,512]{1,0:T(8,128)S(1)}, f32[48,512]{...) custom-call(f32[48,3072]{1,0:T(8,128)S(1)} %get-tuple-element.36.pan_ref, ...), custom_call_target="tpu_custom_call" | custom-call | flops 200000000 | bytes 3000000 | tf_op jit(solution)/shard_map/pallas_call | solution.py:555
  16.0 0.1 collective-permute-start.3
  16.0 0.7 %collective-permute-start.4 = (f32[63,8,128]{2,1,0:T(8,128)S(1)}, f32[63,8,128]{2,1,0:T(8,128)S(1)}, u32[]{:S(2)}, u32[]{:S(2)}) collective-permute-start(f32[63,8,128]{2,1,0:T(8,128)S(1)} %get-tuple-element.54), channel_id=1, source_target_pairs={{4,8},{12,16},{20,24},{8,4},{16,12},{24,20},{5,9},{13,17},{21,25},... | collective-permute-start | bytes 774152 | tf_op jit(solution)/shard_map/ppermute | solution.py:437
  16.7 2.8 %shard_map.62 = (f32[24,96,128]{2,1,0:T(8,128)S(1)}, f32[24,256,128]{2,1,0:T(8,128)S(1)}, f32[8,8,128]{2,1,0:T(8,128)S(1)}, f32[32,768]{1,0:T(8,128)S(1)}, f32[2...) custom-call(f32[48,3072]{1,0:T(8,128)S(1)} %get-tuple-element.36.pan_, ...), custom_call_target="tpu_custom_call" | custom-call | flops 2000000000 | bytes 8000000 | tf_op jit(solution)/shard_map/pallas_call | solution.py:652
  19.5 3.0 %collective-permute-start.5 = (f32[24,8,128]{2,1,0:T(8,128)S(1)}, f32[24,8,128]{2,1,0:T(8,128)S(1)}, u32[]{:S(2)}, u32[]{:S(2)}) collective-permute-start(f32[24,8,128]{2,1,0:T(8,128)S(1)} %get-tuple-element.57), channel_id=1, source_target_pairs={{0,4},{4,0},{8,12},{12,8},{16,20},{20,16},{24,28},{28,24},{1,5},{5... | collective-permute-start | bytes 294920 | tf_op jit(solution)/shard_map/ppermute | solution.py:438
  22.5 0.7 %collective-permute-start.6 = (f32[24,8,128]{2,1,0:T(8,128)S(1)}, f32[24,8,128]{2,1,0:T(8,128)S(1)}, u32[]{:S(2)}, u32[]{:S(2)}) collective-permute-start(f32[24,8,128]{2,1,0:T(8,128)S(1)} %get-tuple-element.58), channel_id=1, source_target_pairs={{4,8},{12,16},{20,24},{8,4},{16,12},{24,20},{5,9},{13,17},{21,25},... | collective-permute-start | bytes 294920 | tf_op jit(solution)/shard_map/ppermute | solution.py:437
  23.2 0.0 collective-permute-done.3.rest_in_ref
  23.2 0.0 collective-permute-done.4.rest_out_ref
  23.2 2.8 %shard_map.63 = (f32[4,128]{1,0:T(4,128)S(1)}, f32[24,64,128]{2,1,0:T(8,128)S(1)}, f32[96,768]{1,0:T(8,128)S(1)}, f32[16,768]{1,0:T(8,128)S(1)}, f32[12,8,768]{2,1,0:T(8,128)S(1)}) custom-call(f32[12,8,896]{2,1,0:T(8,128)S(1)} %get-tuple-element.43.x_ref, f32[24,96,128]{2,1,0:T(8,128)S(1)} %get-tuple-element.49.y_ref, ...), custom_call_target="tpu_custom_call" | custom-call | flops 1000000000 | bytes 8000000 | tf_op jit(solution)/shard_map/pallas_call | solution.py:845
  26.0 0.0 collective-permute-done.5.low_in_ref
  26.0 0.0 collective-permute-done.6.low_out_ref
  26.0 15.5 %all_to_all.5.sums_ref = f32[32,4,128]{2,1,0:T(4,128)S(1)} all-to-all(f32[32,4,128]{2,1,0:T(4,128)S(1)} %broadcast_in_dim.2), channel_id=1, replica_groups=mesh['rows'=8,'band'=4] {'rows','band'}, dimensions={0} | all-to-all | bytes 131072 | tf_op jit(solution)/shard_map/all_to_all | solution.py:865
  41.5 3.9 %shard_map.64 = (f32[384,3072]{1,0:T(8,128)}, f32[12,8,768]{2,1,0:T(8,128)}) custom-call(f32[32,4,128]{2,1,0:T(4,128)S(1)} %all_to_all.5.sums_ref, f32[24,96,128]{2,1,0:T(8,128)S(1)} %get-tuple-element.49.y_ref, f32[24,64,128]{2,1,0:T(8,128)S(1)} %get-tuple-element.60.yh_ref, f32[24,256,128]{2,1,0:T(8,128)S(1)} %get-tuple-element.61.v_ref, ...), custom_call_target="tpu_custom_call" | custom-call | flops 100000000 | bytes 8000000 | tf_op jit(solution)/shard_map/pallas_call | solution.py:980
  (1 shorter events, 0.0 us)
Async XLA Ops:
  3.1 10.4 %collective-permute-start.1 = (f32[14,2,768]{2,1,0:T(2,128)S(1)}, f32[14,2,768]{2,1,0:T(2,128)S(1)}, u32[]{:S(2)}, u32[]{:S(2)}) collective-permute-start(f32[14,2,768]{2,1,0:T(2,128)S(1)} %get-tuple-element.41), channel_id=1, source_target_pairs={{0,2},{1,3},{2,0},{3,1},{4,6},{5,7},{6,4},{7,5},{8,10},{9,11},{10,... | collective-permute-start | bytes 258056 | tf_op jit(solution)/shard_map/ppermute | solution.py:385
  7.2 7.1 %collective-permute-start = (f32[15,2,768]{2,1,0:T(2,128)S(1)}, f32[15,2,768]{2,1,0:T(2,128)S(1)}, u32[]{:S(2)}, u32[]{:S(2)}) collective-permute-start(f32[15,2,768]{2,1,0:T(2,128)S(1)} %get-tuple-element.40), channel_id=1, source_target_pairs={{0,1},{1,2},{2,3},{3,0},{4,5},{5,6},{6,7},{7,4},{8,9},{9,10},{10,1... | collective-permute-start | bytes 276488 | tf_op jit(solution)/shard_map/ppermute | solution.py:385
  8.8 6.4 %collective-permute-start.2 = (f32[15,2,768]{2,1,0:T(2,128)S(1)}, f32[15,2,768]{2,1,0:T(2,128)S(1)}, u32[]{:S(2)}, u32[]{:S(2)}) collective-permute-start(f32[15,2,768]{2,1,0:T(2,128)S(1)} %get-tuple-element.42), channel_id=1, source_target_pairs={{0,3},{1,0},{2,1},{3,2},{4,7},{5,4},{6,5},{7,6},{8,11},{9,8},{10,9... | collective-permute-start | bytes 276488 | tf_op jit(solution)/shard_map/ppermute | solution.py:385
  16.0 7.2 %collective-permute-start.3 = (f32[63,8,128]{2,1,0:T(8,128)S(1)}, f32[63,8,128]{2,1,0:T(8,128)S(1)}, u32[]{:S(2)}, u32[]{:S(2)}) collective-permute-start(f32[63,8,128]{2,1,0:T(8,128)S(1)} %get-tuple-element.53), channel_id=1, source_target_pairs={{0,4},{4,0},{8,12},{12,8},{16,20},{20,16},{24,28},{28,24},{1,5},{5... | collective-permute-start | bytes 774152 | tf_op jit(solution)/shard_map/ppermute | solution.py:438
  16.0 7.2 %collective-permute-start.4 = (f32[63,8,128]{2,1,0:T(8,128)S(1)}, f32[63,8,128]{2,1,0:T(8,128)S(1)}, u32[]{:S(2)}, u32[]{:S(2)}) collective-permute-start(f32[63,8,128]{2,1,0:T(8,128)S(1)} %get-tuple-element.54), channel_id=1, source_target_pairs={{4,8},{12,16},{20,24},{8,4},{16,12},{24,20},{5,9},{13,17},{21,25},... | collective-permute-start | bytes 774152 | tf_op jit(solution)/shard_map/ppermute | solution.py:437
  19.5 6.5 %collective-permute-start.5 = (f32[24,8,128]{2,1,0:T(8,128)S(1)}, f32[24,8,128]{2,1,0:T(8,128)S(1)}, u32[]{:S(2)}, u32[]{:S(2)}) collective-permute-start(f32[24,8,128]{2,1,0:T(8,128)S(1)} %get-tuple-element.57), channel_id=1, source_target_pairs={{0,4},{4,0},{8,12},{12,8},{16,20},{20,16},{24,28},{28,24},{1,5},{5... | collective-permute-start | bytes 294920 | tf_op jit(solution)/shard_map/ppermute | solution.py:438
  22.5 3.5 %collective-permute-start.6 = (f32[24,8,128]{2,1,0:T(8,128)S(1)}, f32[24,8,128]{2,1,0:T(8,128)S(1)}, u32[]{:S(2)}, u32[]{:S(2)}) collective-permute-start(f32[24,8,128]{2,1,0:T(8,128)S(1)} %get-tuple-element.58), channel_id=1, source_target_pairs={{4,8},{12,16},{20,24},{8,4},{16,12},{24,20},{5,9},{13,17},{21,25},... | collective-permute-start | bytes 294920 | tf_op jit(solution)/shard_map/ppermute | solution.py:437

commit v5 on v4

--- a/solution.py
+++ b/solution.py
@@ -58,6 +58,7 @@
 C4 = cubic_table(RATIO_V)
 C3 = cubic_table(RATIO_S)
 MEAN4 = C4.mean(axis=1)
+WIDE = np.convolve(KC, MEAN4)
 
 
 def split(table):
@@ -317,18 +318,17 @@
         )
     )
 
-    sources = (pan_image, jnp.transpose(vnir_bands, (1, 0, 2)), swir_bands, jnp.asarray(table))
-
-    def pack(pan_ref, vnir_ref, swir_ref, table_ref, *rest):
-        outs, (pan_out, table_out, wide, swide, edges, sems) = rest[:groups], rest[groups:]
+    def far(x):
+        return pltpu.with_memory_space_constraint(x, pltpu.HBM)
+
+    def pack(pan_ref, vnir_ref, swir_ref, *rest):
+        outs, (wide, swide, edges, sems) = rest[:groups], rest[groups:]
         me = lax.axis_index("band")
         copies = [
             pltpu.make_async_copy(vnir_ref, wide.at[:, :, pl.ds(LANES, full)], sems.at[0]),
             pltpu.make_async_copy(swir_ref, swide.at[:, :, pl.ds(LANES, sfull)], sems.at[1]),
             pltpu.make_async_copy(pan_ref.at[:, pl.ds(0, LANES)], edges.at[0], sems.at[2]),
             pltpu.make_async_copy(pan_ref.at[:, pl.ds(w - LANES, LANES)], edges.at[1], sems.at[3]),
-            pltpu.make_async_copy(pan_ref, pan_out, sems.at[4]),
-            pltpu.make_async_copy(table_ref, table_out, sems.at[5]),
         ]
         for copy in copies:
             copy.start()
@@ -336,7 +336,7 @@
         wide[:, :, LANES + full : 2 * LANES + full] = jnp.zeros((hc, nb, LANES), F32)
         swide[:, :, 0:LANES] = jnp.zeros((nb, hs, LANES), F32)
         swide[:, :, LANES + sfull : 2 * LANES + sfull] = jnp.zeros((nb, hs, LANES), F32)
-        for copy in copies[:4]:
+        for copy in copies:
             copy.wait()
         for d in range(groups):
             peer = lax.rem(me + d, groups)
@@ -364,23 +364,20 @@
                 for i in range(8 // nb):
                     lane = piece * (i % per_row)
                     out[first + i // per_row, :, lane : lane + piece] = flat[nb * i : nb * (i + 1)]
-        for copy in copies[4:]:
-            copy.wait()
-
-    staged = call(
+
+    chunks = call(
         pack,
-        tuple(shape(chunk_rows[d], nb, wc) for d in range(groups))
-        + (shape(h, w), jax.ShapeDtypeStruct(table.shape, BF16)),
+        tuple(shape(chunk_rows[d], nb, wc) for d in range(groups)),
         [
             pltpu.VMEM((hc, nb, full + 2 * LANES), F32),
             pltpu.VMEM((nb, hs, sfull + 2 * LANES), F32),
             pltpu.VMEM((2, h, LANES), F32),
-            pltpu.SemaphoreType.DMA((6,)),
+            pltpu.SemaphoreType.DMA((4,)),
         ],
         cost=(0, 8_000_000),
-        in_specs=[ANY] * 4,
-    )(*(pltpu.with_memory_space_constraint(x, pltpu.HBM) for x in sources))
-    chunks, pan_held, table_held = staged[:groups], staged[groups], staged[groups + 1]
+        in_specs=[ANY] * 3,
+    )(*(far(x) for x in (pan_image, jnp.transpose(vnir_bands, (1, 0, 2)), swir_bands)))
+    *chunks, pan_late, table_late = lax.optimization_barrier((*chunks, pan_image, jnp.asarray(table)))
     got = [chunks[0]] + [
         lax.ppermute(chunks[d], "band", [(i, (i + d) % groups) for i in range(groups)])
         for d in range(1, groups)
@@ -448,8 +445,19 @@
 
     inner_fine = fine_tiles - 4
 
-    def early(pan_ref, table_ref, coarse_out, fine_out, col_out):
+    def early(pan_far, table_far, pan_ref, table_ref, coarse_out, fine_out, col_out, sems):
+        now = pl.ds(0, place["low"][0][0][0])
+        later = pl.ds(now.size, table.shape[0] - now.size)
+        copies = [
+            pltpu.make_async_copy(pan_far, pan_ref, sems.at[0]),
+            pltpu.make_async_copy(table_far.at[now], table_ref.at[now], sems.at[1]),
+            pltpu.make_async_copy(table_far.at[later], table_ref.at[later], sems.at[2]),
+        ]
+        for copy in copies:
+            copy.start()
+        copies[0].wait()
         panes = parts2(pan_ref[...])
+        copies[1].wait()
         starts = [margin * k - 3 * LANES for k in range(1, frame_tiles - 1)]
         means, fines = shrink(
             windows(panes, starts, 6 * LANES), take(table_ref, "tall"), take(table_ref, "tall_low")
@@ -460,16 +468,21 @@
         col = blocks(dot3(windows(panes, starts, 4 * LANES), both_parts(table_ref, "fine")), pairs - 2)
         col_out[...] = col
         fine_out[...] = filter_rows(take(table_ref, "rows_fine"), col)
-
-    coarse_mid, fine_mid, col_mid = call(
+        copies[2].wait()
+
+    pan_held, table_held, coarse_mid, fine_mid, col_mid = call(
         early,
         (
+            shape(h, w),
+            jax.ShapeDtypeStruct(table.shape, BF16),
             shape(2 * pad + 32, LANES * middle),
             shape(h + 2 * HALO, LANES * inner_fine),
             shape(h, LANES * inner_fine),
         ),
+        [pltpu.SemaphoreType.DMA((3,))],
         cost=(2_000_000_000, 8_000_000),
-    )(pan_held, table_held)
+        in_specs=[ANY] * 2,
+    )(far(pan_late), far(table_late))
 
     border_tiles = -(-edge_size // LANES)
     at_s = HALO * coarse_tiles
@@ -602,7 +615,7 @@
 
     def inside(
         pan_ref, x_ref, s_ref, fm_ref, fe_ref, colm_ref, cole_ref, table_ref,
-        y_out, v_out, acc_out, s_out, diff_out, q_out, *outs,
+        y_out, v_out, acc_out, s_out, diff_out, q_out, edge_out, mean_out, lows_out, *outs,
     ):
         def store(index, value):
             y_out[index] = value
@@ -625,6 +638,22 @@
             q_out[k] = adjoint[:, at]
             total = total + adjoint[hc + 8 : hc + 9, at]
             put(outs, k, low[h : h + HALO, at], low[h + HALO : h + 2 * HALO, at])
+
+        row_id = lax.axis_index("rows")
+        below = jnp.where(row_id > 0, 1.0, 0.0).astype(F32)
+        above = jnp.where(row_id < strips - 1, 1.0, 0.0).astype(F32)
+        means = {}
+        for r in range(-2, hc + 2):
+            value = weighted((MEAN4[t + 2], x_ref[r + t]) for t in range(-2, 3) if 0 <= r + t < hc)
+            means[r] = value * below if r < 0 else (value * above if r >= hc else value)
+        for i, r in enumerate((0, 1, hc - 2, hc - 1)):
+            edge_out[i] = means[r]
+        rows = parts2(jnp.concatenate([means[r] for r in range(2, hc - 2)], axis=0))
+        pair = tuple(x[:, :LANES] for x in both_parts(table_ref, "pair", 0, 3))
+        mean_out[...] = blocks(dot3(windows(rows, block_starts, 2 * LANES), pair), coarse_tiles)
+        reach = TAPS_S // 2
+        for r in range(hc):
+            lows_out[r] = weighted((KC[t + reach], means[r + t]) for t in range(-reach, reach + 1) if r + t in means)
         acc_out[turns + 2] = jnp.concatenate([total, jnp.zeros((7, LANES), F32)], axis=0)
 
         def tile_step(k, carry):
@@ -649,7 +678,7 @@
             acc_out[i] = first[i]
 
     q_rows = -(-(hc + 9) // 16) * 16
-    y_own, v_own, acc_own, s_own, diff, q_own, low_in, low_out = call(
+    y_own, v_own, acc_own, s_own, diff, q_own, mean_edge, mean_own, lows_own, low_in, low_out = call(
         inside,
         (
             shape(fine_tiles, 8 * hc, LANES),
@@ -658,6 +687,9 @@
             shape(8 * hs, wc),
             shape(fine_tiles, h, LANES),
             shape(fine_tiles, q_rows, LANES),
+            shape(4, BANDS, wf),
+            shape(8 * (hc - 4), wc),
+            shape(hc, BANDS, wf),
             shape(fine_tiles, 8, LANES),
             shape(fine_tiles, 8, LANES),
         ),
@@ -666,12 +698,12 @@
     low_in, low_out = trade(low_in, low_out)
 
     def moments(
-        x_ref, y_ref, acc_ref, scol_ref, q_ref, rest_in_ref, rest_out_ref, cm_ref, ce_ref, table_ref,
+        x_ref, y_ref, acc_ref, scol_ref, q_ref, edge_ref, mean_ref, lows_ref,
+        rest_in_ref, rest_out_ref, cm_ref, ce_ref, table_ref,
         mom_out, y_out, ugap_out, dgap_out, s_out,
         both, ulow,
     ):
         me = lax.axis_index("band")
-        row_id = lax.axis_index("rows")
         rest = (rest_in_ref, rest_out_ref)
 
         def tiles(refs, low, indices):
@@ -722,31 +754,23 @@
             return tuple(accs) + (accp, accv)
 
         start = tuple(acc_ref[i] for i in range(turns)) + (acc_ref[turns + 1], acc_ref[turns])
-        first = lax.fori_loop(0, fine_tiles, tile_step, start)
-
-        below = jnp.where(row_id > 0, 1.0, 0.0).astype(F32)
-        above = jnp.where(row_id < strips - 1, 1.0, 0.0).astype(F32)
-        reach = TAPS_S // 2
-        means = []
-        for r in range(-reach, hc + reach):
-            value = float(MEAN4[2]) * x_row(r)
-            for t in (1, 2):
-                value = value + float(MEAN4[2 + t]) * (x_row(r - t) + x_row(r + t))
-            if r < 0:
-                value = value * below
-            if r >= hc:
-                value = value * above
-            means.append(value)
+        def two_tiles(k, carry):
+            return tile_step(2 * k + 1, tile_step(2 * k, carry))
+
+        first = lax.fori_loop(0, fine_tiles // 2, two_tiles, start)
+
+        beyond = [r for r in range(-HALO, hc + HALO) if not 0 <= r < hc]
+        edges = []
+        for i, r in enumerate((0, 1, hc - 2, hc - 1)):
+            more = weighted((MEAN4[a - r + 2], x_row(a)) for a in beyond if abs(a - r) <= 2)
+            edges.append(edge_ref[i] + more)
         lows = []
         for r in range(hc):
-            centre = r + reach
-            value = float(KC[reach]) * means[centre]
-            for t in range(1, reach + 1):
-                value = value + float(KC[reach + t]) * (means[centre - t] + means[centre + t])
-            lows.append(value)
-        u_rows = windows(parts2(jnp.concatenate(means[reach : reach + hc], axis=0)), block_starts, 2 * LANES)
+            more = weighted((WIDE[a - r + HALO], x_row(a)) for a in beyond if abs(a - r) <= HALO)
+            lows.append(lows_ref[r] + more)
+        u_rows = windows(parts2(jnp.concatenate(edges, axis=0)), block_starts, 2 * LANES)
         l_rows = windows(parts2(jnp.concatenate(lows, axis=0)), block_starts, 2 * LANES)
-        u_all = dot3(u_rows, tuple(x[:, :LANES] for x in both_parts(table_ref, "pair", 0, 3)))
+        u_edge = dot3(u_rows, tuple(x[:, :LANES] for x in both_parts(table_ref, "pair", 0, 3)))
         left = jnp.where(me == 0, 1, 0)
         right = jnp.where(me == groups - 1, 2, 0)
         size = 8 * hc
@@ -760,7 +784,9 @@
                 at = slice(LANES * k, LANES * (k + 1))
                 low_k = part[size * (k - lo_k) : size * (k - lo_k + 1)]
                 ulow[:, at] = low_k
-                ugap_out[:, at] = u_all[size * k : size * (k + 1)] - low_k
+                around_k = u_edge[32 * k : 32 * (k + 1)]
+                u_k = jnp.concatenate([around_k[0:16], mean_ref[:, at], around_k[16:32]], axis=0)
+                ugap_out[:, at] = u_k - low_k
 
         column = lax.broadcasted_iota(jnp.int32, (1, wf), 1) - HALF + me * wc
         valid = jnp.where((column >= 0) & (column < groups * wc), 1.0, 0.0).astype(F32)
@@ -857,7 +883,8 @@
         ],
         cost=(1_000_000_000, 8_000_000),
     )(
-        x_loc, y_own, acc_own, s_own, q_own, rest_in, rest_out, coarse_mid, coarse_edge, table_held,
+        x_loc, y_own, acc_own, s_own, q_own, mean_edge, mean_own, lows_own,
+        rest_in, rest_out, coarse_mid, coarse_edge, table_held,
     )
     devices = groups * strips
     mom, low_in, low_out = lax.optimization_barrier((mom, low_in, low_out))
@@ -922,14 +949,6 @@
             return pltpu.make_async_copy(tiles.at[k], vnir_out.at[:, lanes], sems.at[k])
 
         def tile_step(k, carry):
-            work, inverse = carry
-            here = sub == k
-            row = down(jnp.where(here, work, 0.0))
-            col = jnp.sum(jnp.where(lane == k, work, 0.0), axis=1, keepdims=True)
-            pivot = 1.0 / jnp.where(k < BANDS, down(jnp.where(here[:, 0:1], col, 0.0)), 1.0)
-            inverse = jnp.where(here, pivot, inverse)
-            work = work - jnp.where(here, 0.0, col * pivot) * row
-
             ys = {m: y_ref[k, pl.ds(8 * (m - 2), 8), :] for m in own_rows}
             for i, m in enumerate(around):
                 if m in halo_rows:
@@ -953,10 +972,26 @@
                     value = value + gain * detail
                     tiles[k, pl.ds(r, 8, stride=h), :] = value
             sent_tile(k).start()
+            return carry
+
+        beside = fine_tiles // BANDS
+
+        def solve_step(k, carry):
+            work, inverse = carry
+            here = sub == k
+            row = down(jnp.where(here, work, 0.0))
+            col = jnp.sum(jnp.where(lane == k, work, 0.0), axis=1, keepdims=True)
+            pivot = 1.0 / down(jnp.where(here[:, 0:1], col, 0.0))
+            inverse = jnp.where(here, pivot, inverse)
+            work = work - jnp.where(here, 0.0, col * pivot) * row
+
+            for i in range(beside):
+                tile_step(beside * k + i, 0)
             return work, inverse
 
         start = (jnp.where(lane == BANDS, target, a2), jnp.zeros((8, LANES), F32))
-        work, inverse = lax.fori_loop(0, fine_tiles, tile_step, start)
+        work, inverse = lax.fori_loop(0, BANDS, solve_step, start)
+        lax.fori_loop(BANDS * beside, fine_tiles, tile_step, 0)
         fit2 = column(work, BANDS) * inverse
         numer = down(fit2 * b2)
         share_row = numer / down(fit2 * target)

time: 45.6 us -> 43.9 us (0.963)
  waiting for transfers between devices: 2.63 us -> 1 us
    ppermute x3, waiting for transfers between devices: 2.62 us -> 0.99 us  [local(): lax.ppermute(chunks[d], 'band', [(i, (i + d) % groups) for i in range(gro...]
    pallas_call x1, Pallas kernels: 3.92 us -> 3.38 us  [local(): call(finish, (shape(BANDS * h, w), shape(hc, BANDS, wc)), [pltpu.VMEM((fi...]
    pallas_call x2, Pallas kernels: 3.97 us -> 4.43 us  [the longest x1 3.13 us: local(): call(early, (shape(h, w), jax.ShapeDtypeStruct(table.shape, BF16), shape(...]
  transfers between devices with their start and end apart: 7 -> 7, of which waited for: 3 -> 2; matrix products, arithmetic and copies ran while one was open for 0% -> 0% of each run, Pallas kernels for 16% -> 20%
where the time goes in v5:
time: 43.9 us; the launch traced here: 43.8 us
  blocking collectives  15.6 us (36%)
  Pallas kernels  14.1 us (32%)
  starting transfers between devices  12.4 us (28%)
  waiting for transfers between devices  1 us (2%)
  between operations  0.72 us (2%)
    all_to_all x1, blocking collectives, local(): lax.all_to_all(spread, ('rows', 'band'), split_axis=0, concat_axis=0, til...  15.6 us
    ppermute x3, starting transfers between devices, local(): lax.ppermute(chunks[d], 'band', [(i, (i + d) % groups) for i in range(gro...  7.92 us
    pallas_call x1, Pallas kernels, local(): call(finish, (shape(BANDS * h, w), shape(hc, BANDS, wc)), [pltpu.VMEM((fi...  3.38 us
    pallas_call x1, Pallas kernels, local(): call(early, (shape(h, w), jax.ShapeDtypeStruct(table.shape, BF16), shape(...  3.13 us
    pallas_call x1, Pallas kernels, local(): call(inside, (shape(fine_tiles, 8 * hc, LANES), shape(fine_tiles, 8 * who...  3.13 us
    ppermute x2, starting transfers between devices, trade(): return (lax.ppermute(inner, 'rows', pairs_in), outer)  3.11 us
    pallas_call x1, Pallas kernels, local(): call(moments, (shape(4, LANES), shape(fine_tiles, 8 * len(around), LANES)...  2.35 us
    ppermute x2, starting transfers between devices, trade(): outer = lax.ppermute(outer, 'rows', pairs_out)  1.33 us
  transfers between devices with their start and end apart: 7, of which 2 were waited for; matrix products, arithmetic and copies ran while one was open for 0% of the time, Pallas kernels for 20%

profile of v5, /device:TPU:0, one launch (start us, length us, event | category | flops | bytes accessed | tf_op | source)
XLA Modules:
  0.0 43.8 jit_solution(4876463758314127299)
XLA Ops:
  0.6 1.3 %shard_map.59 = (f32[14,2,768]{2,1,0:T(2,128)S(1)}, f32[15,2,768]{2,1,0:T(2,128)S(1)}, f32[14,2,768]{2,1,0:T(2,128)S(1)}, f32[15,2,768]{2,1,0:T(2,128)S(1)}) custom-call(f32[48,3072]{1,0:T(8,128)} %pan_far, f32[12,2,3072]{2,1,0:T(2,128)} %bitcast.3, f32[2,4,1024]{2,1,0:T(4,128)} %swir_ref.1), custom_call_target="tpu_custom_call" | custom-call | bytes 8000000 | tf_op jit(solution)/shard_map/pallas_call | solution.py:368
  1.9 4.1 %collective-permute-start.1 = (f32[14,2,768]{2,1,0:T(2,128)S(1)}, f32[14,2,768]{2,1,0:T(2,128)S(1)}, u32[]{:S(2)}, u32[]{:S(2)}) collective-permute-start(f32[14,2,768]{2,1,0:T(2,128)S(1)} %get-tuple-element.56), channel_id=1, source_target_pairs={{0,2},{1,3},{2,0},{3,1},{4,6},{5,7},{6,4},{7,5},{8,10},{9,11},{10,... | collective-permute-start | bytes 258056 | tf_op jit(solution)/shard_map/ppermute | solution.py:382
  6.0 1.6 %collective-permute-start = (f32[15,2,768]{2,1,0:T(2,128)S(1)}, f32[15,2,768]{2,1,0:T(2,128)S(1)}, u32[]{:S(2)}, u32[]{:S(2)}) collective-permute-start(f32[15,2,768]{2,1,0:T(2,128)S(1)} %get-tuple-element.55), channel_id=1, source_target_pairs={{0,1},{1,2},{2,3},{3,0},{4,5},{5,6},{6,7},{7,4},{8,9},{9,10},{10,1... | collective-permute-start | bytes 276488 | tf_op jit(solution)/shard_map/ppermute | solution.py:382
  7.6 2.2 %collective-permute-start.2 = (f32[15,2,768]{2,1,0:T(2,128)S(1)}, f32[15,2,768]{2,1,0:T(2,128)S(1)}, u32[]{:S(2)}, u32[]{:S(2)}) collective-permute-start(f32[15,2,768]{2,1,0:T(2,128)S(1)} %get-tuple-element.57), channel_id=1, source_target_pairs={{0,3},{1,0},{2,1},{3,2},{4,7},{5,4},{6,5},{7,6},{8,11},{9,8},{10,9... | collective-permute-start | bytes 276488 | tf_op jit(solution)/shard_map/ppermute | solution.py:382
  9.9 3.1 %shard_map.60 = (f32[48,3072]{1,0:T(8,128)S(1)}, bf16[7296,256]{1,0:T(8,128)(2,1)S(1)}, f32[64,640]{1,0:T(8,128)S(1)}, f32[64,2560]{1,0:T(8,128)S(1)}, f32[48,2560]{1,0:T(8,128)S(1)}) custom-call(f32[48,3072]{1,0:T(8,128)} %pan_far, bf16[7296,256]{1,0:T(8,128)(2,1)} %constant.2.clone.table_far), custom_call_target="tpu_custom_call" | custom-call | flops 2000000000 | bytes 8000000 | tf_op jit(solution)/shard_map/pallas_call | solution.py:473
  13.0 0.0 collective-permute-done.1.rest_2_
  13.0 0.1 collective-permute-done.rest_1_
  13.1 0.9 %collective-permute-done.2.rest_3_ = f32[15,2,768]{2,1,0:T(2,128)S(1)} collective-permute-done((f32[15,2,768]{2,1,0:T(2,128)S(1)}, f32[15,2,768]{2,1,0:T(2,128)S(1)}, u32[]{:S(2)}, u32[]{:S(2)}) %collective-permute-start.2) | collective-permute-done | bytes 92192 | tf_op jit(solution)/shard_map/ppermute | solution.py:382
  14.0 0.8 %shard_map.61 = (f32[12,8,896]{2,1,0:T(8,128)S(1)}, f32[4,8,384]{2,1,0:T(8,128)S(1)}, f32[32,256]{1,0:T(8,128)S(1)}, f32[64,512]{1,0:T(8,128)S(1)}, f32[48,512]{...) custom-call(f32[48,3072]{1,0:T(8,128)S(1)} %get-tuple-element.51.pan_ref, ...), custom_call_target="tpu_custom_call" | custom-call | flops 200000000 | bytes 3000000 | tf_op jit(solution)/shard_map/pallas_call | solution.py:568
  14.8 0.1 collective-permute-start.3
  14.9 0.7 %collective-permute-start.4 = (f32[63,8,128]{2,1,0:T(8,128)S(1)}, f32[63,8,128]{2,1,0:T(8,128)S(1)}, u32[]{:S(2)}, u32[]{:S(2)}) collective-permute-start(f32[63,8,128]{2,1,0:T(8,128)S(1)} %get-tuple-element.72), channel_id=1, source_target_pairs={{4,8},{12,16},{20,24},{8,4},{16,12},{24,20},{5,9},{13,17},{21,25},... | collective-permute-start | bytes 774152 | tf_op jit(solution)/shard_map/ppermute | solution.py:434
  15.6 3.1 %shard_map.62 = (f32[24,96,128]{2,1,0:T(8,128)S(1)}, f32[24,256,128]{2,1,0:T(8,128)S(1)}, f32[8,8,128]{2,1,0:T(8,128)S(1)}, f32[32,768]{1,0:T(8,128)S(1)}, f32[2...) custom-call(f32[48,3072]{1,0:T(8,128)S(1)} %get-tuple-element.51.pan, ...), custom_call_target="tpu_custom_call" | custom-call | flops 2000000000 | bytes 8000000 | tf_op jit(solution)/shard_map/pallas_call | solution.py:681
  18.7 3.0 %collective-permute-start.5 = (f32[24,8,128]{2,1,0:T(8,128)S(1)}, f32[24,8,128]{2,1,0:T(8,128)S(1)}, u32[]{:S(2)}, u32[]{:S(2)}) collective-permute-start(f32[24,8,128]{2,1,0:T(8,128)S(1)} %get-tuple-element.75), channel_id=1, source_target_pairs={{0,4},{4,0},{8,12},{12,8},{16,20},{20,16},{24,28},{28,24},{1,5},{5... | collective-permute-start | bytes 294920 | tf_op jit(solution)/shard_map/ppermute | solution.py:435
  21.8 0.7 %collective-permute-start.6 = (f32[24,8,128]{2,1,0:T(8,128)S(1)}, f32[24,8,128]{2,1,0:T(8,128)S(1)}, u32[]{:S(2)}, u32[]{:S(2)}) collective-permute-start(f32[24,8,128]{2,1,0:T(8,128)S(1)} %get-tuple-element.76), channel_id=1, source_target_pairs={{4,8},{12,16},{20,24},{8,4},{16,12},{24,20},{5,9},{13,17},{21,25},... | collective-permute-start | bytes 294920 | tf_op jit(solution)/shard_map/ppermute | solution.py:434
  22.4 0.0 collective-permute-done.3.rest_in_ref
  22.4 0.0 collective-permute-done.4.rest_out_ref
  22.4 2.4 %shard_map.63 = (f32[4,128]{1,0:T(4,128)S(1)}, f32[24,64,128]{2,1,0:T(8,128)S(1)}, f32[96,768]{1,0:T(8,128)S(1)}, f32[16,768]{1,0:T(8,128)S(1)}, f32[12,8,768]{2,1,0:T(8,128)S(1)}) custom-call(f32[12,8,896]{2,1,0:T(8,128)S(1)} %get-tuple-element.58.x_ref, f32[24,96,128]{2,1,0:T(8,128)S(1)} %get-tuple-element.64.y_ref, ...), custom_call_target="tpu_custom_call" | custom-call | flops 1000000000 | bytes 8000000 | tf_op jit(solution)/shard_map/pallas_call | solution.py:871
  24.8 0.0 collective-permute-done.5.low_in_ref
  24.8 0.0 collective-permute-done.6.low_out_ref
  24.8 15.6 %all_to_all.5.sums_ref = f32[32,4,128]{2,1,0:T(4,128)S(1)} all-to-all(f32[32,4,128]{2,1,0:T(4,128)S(1)} %broadcast_in_dim.2), channel_id=1, replica_groups=mesh['rows'=8,'band'=4] {'rows','band'}, dimensions={0} | all-to-all | bytes 131072 | tf_op jit(solution)/shard_map/all_to_all | solution.py:892
  40.4 3.4 %shard_map.64 = (f32[384,3072]{1,0:T(8,128)}, f32[12,8,768]{2,1,0:T(8,128)}) custom-call(f32[32,4,128]{2,1,0:T(4,128)S(1)} %all_to_all.5.sums_ref, f32[24,96,128]{2,1,0:T(8,128)S(1)} %get-tuple-element.64.y_ref, f32[24,64,128]{2,1,0:T(8,128)S(1)} %get-tuple-element.78.yh_ref, f32[24,256,128]{2,1,0:T(8,128)S(1)} %get-tuple-element.79.v_ref, ...), custom_call_target="tpu_custom_call" | custom-call | flops 100000000 | bytes 8000000 | tf_op jit(solution)/shard_map/pallas_call | solution.py:1015
  (1 shorter events, 0.0 us)
Async XLA Ops:
  1.9 11.1 %collective-permute-start.1 = (f32[14,2,768]{2,1,0:T(2,128)S(1)}, f32[14,2,768]{2,1,0:T(2,128)S(1)}, u32[]{:S(2)}, u32[]{:S(2)}) collective-permute-start(f32[14,2,768]{2,1,0:T(2,128)S(1)} %get-tuple-element.56), channel_id=1, source_target_pairs={{0,2},{1,3},{2,0},{3,1},{4,6},{5,7},{6,4},{7,5},{8,10},{9,11},{10,... | collective-permute-start | bytes 258056 | tf_op jit(solution)/shard_map/ppermute | solution.py:382
  6.0 7.1 %collective-permute-start = (f32[15,2,768]{2,1,0:T(2,128)S(1)}, f32[15,2,768]{2,1,0:T(2,128)S(1)}, u32[]{:S(2)}, u32[]{:S(2)}) collective-permute-start(f32[15,2,768]{2,1,0:T(2,128)S(1)} %get-tuple-element.55), channel_id=1, source_target_pairs={{0,1},{1,2},{2,3},{3,0},{4,5},{5,6},{6,7},{7,4},{8,9},{9,10},{10,1... | collective-permute-start | bytes 276488 | tf_op jit(solution)/shard_map/ppermute | solution.py:382
  7.6 6.4 %collective-permute-start.2 = (f32[15,2,768]{2,1,0:T(2,128)S(1)}, f32[15,2,768]{2,1,0:T(2,128)S(1)}, u32[]{:S(2)}, u32[]{:S(2)}) collective-permute-start(f32[15,2,768]{2,1,0:T(2,128)S(1)} %get-tuple-element.57), channel_id=1, source_target_pairs={{0,3},{1,0},{2,1},{3,2},{4,7},{5,4},{6,5},{7,6},{8,11},{9,8},{10,9... | collective-permute-start | bytes 276488 | tf_op jit(solution)/shard_map/ppermute | solution.py:382
  14.8 7.6 %collective-permute-start.3 = (f32[63,8,128]{2,1,0:T(8,128)S(1)}, f32[63,8,128]{2,1,0:T(8,128)S(1)}, u32[]{:S(2)}, u32[]{:S(2)}) collective-permute-start(f32[63,8,128]{2,1,0:T(8,128)S(1)} %get-tuple-element.71), channel_id=1, source_target_pairs={{0,4},{4,0},{8,12},{12,8},{16,20},{20,16},{24,28},{28,24},{1,5},{5... | collective-permute-start | bytes 774152 | tf_op jit(solution)/shard_map/ppermute | solution.py:435
  14.9 7.5 %collective-permute-start.4 = (f32[63,8,128]{2,1,0:T(8,128)S(1)}, f32[63,8,128]{2,1,0:T(8,128)S(1)}, u32[]{:S(2)}, u32[]{:S(2)}) collective-permute-start(f32[63,8,128]{2,1,0:T(8,128)S(1)} %get-tuple-element.72), channel_id=1, source_target_pairs={{4,8},{12,16},{20,24},{8,4},{16,12},{24,20},{5,9},{13,17},{21,25},... | collective-permute-start | bytes 774152 | tf_op jit(solution)/shard_map/ppermute | solution.py:434
  18.7 6.1 %collective-permute-start.5 = (f32[24,8,128]{2,1,0:T(8,128)S(1)}, f32[24,8,128]{2,1,0:T(8,128)S(1)}, u32[]{:S(2)}, u32[]{:S(2)}) collective-permute-start(f32[24,8,128]{2,1,0:T(8,128)S(1)} %get-tuple-element.75), channel_id=1, source_target_pairs={{0,4},{4,0},{8,12},{12,8},{16,20},{20,16},{24,28},{28,24},{1,5},{5... | collective-permute-start | bytes 294920 | tf_op jit(solution)/shard_map/ppermute | solution.py:435
  21.8 3.0 %collective-permute-start.6 = (f32[24,8,128]{2,1,0:T(8,128)S(1)}, f32[24,8,128]{2,1,0:T(8,128)S(1)}, u32[]{:S(2)}, u32[]{:S(2)}) collective-permute-start(f32[24,8,128]{2,1,0:T(8,128)S(1)} %get-tuple-element.76), channel_id=1, source_target_pairs={{4,8},{12,16},{20,24},{8,4},{16,12},{24,20},{5,9},{13,17},{21,25},... | collective-permute-start | bytes 294920 | tf_op jit(solution)/shard_map/ppermute | solution.py:434

commit v6 on v5

--- a/solution.py
+++ b/solution.py
@@ -586,9 +586,6 @@
     own_rows = range(2, hc + 2)
     halo_rows = (0, 1, hc + 2, hc + 3)
     around = (-2, -1) + halo_rows + (hc + 4, hc + 5)
-    whole_rows = range(2, hc - 2)
-    first_whole = RATIO_V * whole_rows[0]
-    whole_count = RATIO_V * len(whole_rows)
 
     def lifted(rows, table_ref, store):
         stack = windows(parts2(jnp.concatenate(rows, axis=0)), block_starts, 2 * LANES)
@@ -597,6 +594,14 @@
         for k in range(coarse_tiles):
             for q in range(RATIO_V):
                 store(RATIO_V * k + q, up[size * k : size * (k + 1), LANES * q : LANES * (q + 1)])
+
+    def grouped(step, size):
+        def body(k, carry):
+            for i in range(size):
+                carry = step(size * k + i, carry)
+            return carry
+
+        return body
 
     def weighted(pairs):
         value = None
@@ -666,14 +671,14 @@
                     accs[i] = accs[i] + z * pltpu.roll(ys[m], i, 0)
                 accv = accv + float(rise[m]) * ys[m]
                 accp = accp + ys[m] * q_out[k, pl.ds(m + 2, 1), :]
-            for m in whole_rows:
+            for m in range(hc):
                 for p in range(RATIO_V):
-                    r = RATIO_V * m + p - first_whole
-                    v_out[k, pl.ds(8 * r, 8), :] = weighted((C4[t, p], ys[m + t]) for t in range(5) if C4[t, p] != 0.0)
+                    r = RATIO_V * m + p
+                    v_out[k, pl.ds(8 * r, 8), :] = weighted((C4[t, p], ys[m + t]) for t in range(5) if m + t in ys)
             return tuple(accs) + (accv, accp)
 
         zero = jnp.zeros((8, LANES), F32)
-        first = lax.fori_loop(0, fine_tiles, tile_step, (zero,) * (turns + 2))
+        first = lax.fori_loop(0, fine_tiles // 2, grouped(tile_step, 2), (zero,) * (turns + 2))
         for i in range(turns + 2):
             acc_out[i] = first[i]
 
@@ -682,7 +687,7 @@
         inside,
         (
             shape(fine_tiles, 8 * hc, LANES),
-            shape(fine_tiles, 8 * whole_count, LANES),
+            shape(fine_tiles, 8 * h, LANES),
             shape(turns + 3, 8, LANES),
             shape(8 * hs, wc),
             shape(fine_tiles, h, LANES),
@@ -754,10 +759,7 @@
             return tuple(accs) + (accp, accv)
 
         start = tuple(acc_ref[i] for i in range(turns)) + (acc_ref[turns + 1], acc_ref[turns])
-        def two_tiles(k, carry):
-            return tile_step(2 * k + 1, tile_step(2 * k, carry))
-
-        first = lax.fori_loop(0, fine_tiles // 2, two_tiles, start)
+        first = lax.fori_loop(0, fine_tiles // 2, grouped(tile_step, 2), start)
 
         beyond = [r for r in range(-HALO, hc + HALO) if not 0 <= r < hc]
         edges = []
@@ -891,8 +893,10 @@
     spread = jnp.broadcast_to(mom[None], (devices,) + mom.shape)
     sums = lax.all_to_all(spread, ("rows", "band"), split_axis=0, concat_axis=0, tiled=True)
 
+    apart_rows = h + 8
+
     def finish(
-        sums_ref, y_ref, yh_ref, v_ref, diff_ref, low_in_ref, low_out_ref, ugap_ref, dgap_ref, s_ref,
+        sums_ref, yh_ref, v_ref, diff_ref, low_in_ref, low_out_ref, ugap_ref, dgap_ref, s_ref,
         vnir_out, swir_out, tiles, swir, ends, sems,
     ):
         lane = lax.broadcasted_iota(jnp.int32, (8, LANES), 1)
@@ -946,23 +950,21 @@
 
         def sent_tile(k):
             lanes = pl.ds(pl.multiple_of(LANES * k, LANES), LANES)
-            return pltpu.make_async_copy(tiles.at[k], vnir_out.at[:, lanes], sems.at[k])
+            held = tiles.reshape(fine_tiles, BANDS, apart_rows, LANES).at[k, :, pl.ds(0, h), :]
+            return pltpu.make_async_copy(held, vnir_out.at[:, :, lanes], sems.at[k])
 
         def tile_step(k, carry):
-            ys = {m: y_ref[k, pl.ds(8 * (m - 2), 8), :] for m in own_rows}
-            for i, m in enumerate(around):
-                if m in halo_rows:
-                    ys[m] = yh_ref[k, pl.ds(8 * i, 8), :]
+            ys = {m: yh_ref[k, pl.ds(8 * i, 8), :] for i, m in enumerate(around) if m in halo_rows}
             lows = (low_in_ref, low_out_ref)
             ends[k, 0:HALO, :] = diff_ref[k, 0:HALO, :] - arrived(lows, k, True)
             ends[k, HALO:, :] = diff_ref[k, h - HALO :, :] - arrived(lows, k, False)
             for m in range(hc):
                 for p in range(RATIO_V):
                     r = RATIO_V * m + p
-                    if m in whole_rows:
-                        value = v_ref[k, pl.ds(8 * (r - first_whole), 8), :]
-                    else:
-                        value = weighted((C4[t, p], ys[m + t]) for t in range(5) if C4[t, p] != 0.0)
+                    value = v_ref[k, pl.ds(8 * r, 8), :]
+                    more = weighted((C4[t, p], ys[m + t]) for t in range(5) if m + t in ys)
+                    if more is not None:
+                        value = value + more
                     if r < HALO:
                         detail = ends[k, pl.ds(r, 1), :]
                     elif r >= h - HALO:
@@ -970,7 +972,7 @@
                     else:
                         detail = diff_ref[k, pl.ds(r, 1), :]
                     value = value + gain * detail
-                    tiles[k, pl.ds(r, 8, stride=h), :] = value
+                    tiles[k, pl.ds(r, 8, stride=apart_rows), :] = value
             sent_tile(k).start()
             return carry
 
@@ -1014,17 +1016,17 @@
 
     joined_vnir, joined_swir = call(
         finish,
-        (shape(BANDS * h, w), shape(hc, BANDS, wc)),
+        (shape(BANDS, h, w), shape(hc, BANDS, wc)),
         [
-            pltpu.VMEM((fine_tiles, BANDS * h, LANES), F32),
+            pltpu.VMEM((fine_tiles, BANDS * apart_rows, LANES), F32),
             pltpu.VMEM((hc, BANDS, wc), F32),
             pltpu.VMEM((fine_tiles, 2 * HALO, LANES), F32),
             pltpu.SemaphoreType.DMA((fine_tiles + 1,)),
         ],
         cost=(100_000_000, 8_000_000),
         out_specs=(ANY, ANY),
-    )(sums, y_own, y_halo, v_own, diff, low_in, low_out, ugap, dgap, s_up)
-    return joined_vnir.reshape(BANDS, h, w), jnp.transpose(joined_swir, (1, 0, 2))
+    )(sums, y_halo, v_own, diff, low_in, low_out, ugap, dgap, s_up)
+    return joined_vnir, jnp.transpose(joined_swir, (1, 0, 2))
 
 
 def solution(mesh):

time: 43.9 us -> 43.6 us (level)
  no operation moved by 1% of the time
where the time goes in v6:
time: 43.6 us; the launch traced here: 43.4 us
  blocking collectives  15.6 us (36%)
  Pallas kernels  13.7 us (31%)
  starting transfers between devices  12.4 us (28%)
  waiting for transfers between devices  1 us (2%)
  between operations  0.72 us (2%)
    all_to_all x1, blocking collectives, local(): lax.all_to_all(spread, ('rows', 'band'), split_axis=0, concat_axis=0, til...  15.6 us
    ppermute x3, starting transfers between devices, local(): lax.ppermute(chunks[d], 'band', [(i, (i + d) % groups) for i in range(gro...  7.92 us
    pallas_call x1, Pallas kernels, local(): call(inside, (shape(fine_tiles, 8 * hc, LANES), shape(fine_tiles, 8 * h,...  3.21 us
    pallas_call x1, Pallas kernels, local(): call(early, (shape(h, w), jax.ShapeDtypeStruct(table.shape, BF16), shape(...  3.13 us
    ppermute x2, starting transfers between devices, trade(): return (lax.ppermute(inner, 'rows', pairs_in), outer)  3.11 us
    pallas_call x1, Pallas kernels, local(): call(finish, (shape(BANDS, h, w), shape(hc, BANDS, wc)), [pltpu.VMEM((fin...  2.94 us
    pallas_call x1, Pallas kernels, local(): call(moments, (shape(4, LANES), shape(fine_tiles, 8 * len(around), LANES)...  2.3 us
    ppermute x2, starting transfers between devices, trade(): outer = lax.ppermute(outer, 'rows', pairs_out)  1.33 us
  transfers between devices with their start and end apart: 7, of which 2 were waited for; matrix products, arithmetic and copies ran while one was open for 0% of the time, Pallas kernels for 20%

profile of v6, /device:TPU:0, one launch (start us, length us, event | category | flops | bytes accessed | tf_op | source)
XLA Modules:
  0.0 43.4 jit_solution(8089654454062760525)
XLA Ops:
  0.6 1.3 %shard_map.59 = (f32[14,2,768]{2,1,0:T(2,128)S(1)}, f32[15,2,768]{2,1,0:T(2,128)S(1)}, f32[14,2,768]{2,1,0:T(2,128)S(1)}, f32[15,2,768]{2,1,0:T(2,128)S(1)}) custom-call(f32[48,3072]{1,0:T(8,128)} %pan_far, f32[12,2,3072]{2,1,0:T(2,128)} %bitcast.2, f32[2,4,1024]{2,1,0:T(4,128)} %swir_ref.1), custom_call_target="tpu_custom_call" | custom-call | bytes 8000000 | tf_op jit(solution)/shard_map/pallas_call | solution.py:368
  1.9 4.1 %collective-permute-start.1 = (f32[14,2,768]{2,1,0:T(2,128)S(1)}, f32[14,2,768]{2,1,0:T(2,128)S(1)}, u32[]{:S(2)}, u32[]{:S(2)}) collective-permute-start(f32[14,2,768]{2,1,0:T(2,128)S(1)} %get-tuple-element.56), channel_id=1, source_target_pairs={{0,2},{1,3},{2,0},{3,1},{4,6},{5,7},{6,4},{7,5},{8,10},{9,11},{10,... | collective-permute-start | bytes 258056 | tf_op jit(solution)/shard_map/ppermute | solution.py:382
  6.0 1.6 %collective-permute-start = (f32[15,2,768]{2,1,0:T(2,128)S(1)}, f32[15,2,768]{2,1,0:T(2,128)S(1)}, u32[]{:S(2)}, u32[]{:S(2)}) collective-permute-start(f32[15,2,768]{2,1,0:T(2,128)S(1)} %get-tuple-element.55), channel_id=1, source_target_pairs={{0,1},{1,2},{2,3},{3,0},{4,5},{5,6},{6,7},{7,4},{8,9},{9,10},{10,1... | collective-permute-start | bytes 276488 | tf_op jit(solution)/shard_map/ppermute | solution.py:382
  7.6 2.2 %collective-permute-start.2 = (f32[15,2,768]{2,1,0:T(2,128)S(1)}, f32[15,2,768]{2,1,0:T(2,128)S(1)}, u32[]{:S(2)}, u32[]{:S(2)}) collective-permute-start(f32[15,2,768]{2,1,0:T(2,128)S(1)} %get-tuple-element.57), channel_id=1, source_target_pairs={{0,3},{1,0},{2,1},{3,2},{4,7},{5,4},{6,5},{7,6},{8,11},{9,8},{10,9... | collective-permute-start | bytes 276488 | tf_op jit(solution)/shard_map/ppermute | solution.py:382
  9.9 3.1 %shard_map.60 = (f32[48,3072]{1,0:T(8,128)S(1)}, bf16[7296,256]{1,0:T(8,128)(2,1)S(1)}, f32[64,640]{1,0:T(8,128)S(1)}, f32[64,2560]{1,0:T(8,128)S(1)}, f32[48,2560]{1,0:T(8,128)S(1)}) custom-call(f32[48,3072]{1,0:T(8,128)} %pan_far, bf16[7296,256]{1,0:T(8,128)(2,1)} %constant.2.clone.table_far), custom_call_target="tpu_custom_call" | custom-call | flops 2000000000 | bytes 8000000 | tf_op jit(solution)/shard_map/pallas_call | solution.py:473
  13.0 0.0 collective-permute-done.1.rest_2_
  13.0 0.1 collective-permute-done.rest_1_
  13.1 0.9 %collective-permute-done.2.rest_3_ = f32[15,2,768]{2,1,0:T(2,128)S(1)} collective-permute-done((f32[15,2,768]{2,1,0:T(2,128)S(1)}, f32[15,2,768]{2,1,0:T(2,128)S(1)}, u32[]{:S(2)}, u32[]{:S(2)}) %collective-permute-start.2) | collective-permute-done | bytes 92192 | tf_op jit(solution)/shard_map/ppermute | solution.py:382
  14.0 0.8 %shard_map.61 = (f32[12,8,896]{2,1,0:T(8,128)S(1)}, f32[4,8,384]{2,1,0:T(8,128)S(1)}, f32[32,256]{1,0:T(8,128)S(1)}, f32[64,512]{1,0:T(8,128)S(1)}, f32[48,512]{...) custom-call(f32[48,3072]{1,0:T(8,128)S(1)} %get-tuple-element.51.pan_ref, ...), custom_call_target="tpu_custom_call" | custom-call | flops 200000000 | bytes 3000000 | tf_op jit(solution)/shard_map/pallas_call | solution.py:568
  14.8 0.1 collective-permute-start.3
  14.9 0.7 %collective-permute-start.4 = (f32[63,8,128]{2,1,0:T(8,128)S(1)}, f32[63,8,128]{2,1,0:T(8,128)S(1)}, u32[]{:S(2)}, u32[]{:S(2)}) collective-permute-start(f32[63,8,128]{2,1,0:T(8,128)S(1)} %get-tuple-element.72), channel_id=1, source_target_pairs={{4,8},{12,16},{20,24},{8,4},{16,12},{24,20},{5,9},{13,17},{21,25},... | collective-permute-start | bytes 774152 | tf_op jit(solution)/shard_map/ppermute | solution.py:434
  15.6 3.2 %shard_map.62 = (f32[24,96,128]{2,1,0:T(8,128)S(1)}, f32[24,384,128]{2,1,0:T(8,128)S(1)}, f32[8,8,128]{2,1,0:T(8,128)S(1)}, f32[32,768]{1,0:T(8,128)S(1)}, f32[2...) custom-call(f32[48,3072]{1,0:T(8,128)S(1)} %get-tuple-element.51.pan, ...), custom_call_target="tpu_custom_call" | custom-call | flops 2000000000 | bytes 8000000 | tf_op jit(solution)/shard_map/pallas_call | solution.py:686
  18.8 3.0 %collective-permute-start.5 = (f32[24,8,128]{2,1,0:T(8,128)S(1)}, f32[24,8,128]{2,1,0:T(8,128)S(1)}, u32[]{:S(2)}, u32[]{:S(2)}) collective-permute-start(f32[24,8,128]{2,1,0:T(8,128)S(1)} %get-tuple-element.75), channel_id=1, source_target_pairs={{0,4},{4,0},{8,12},{12,8},{16,20},{20,16},{24,28},{28,24},{1,5},{5... | collective-permute-start | bytes 294920 | tf_op jit(solution)/shard_map/ppermute | solution.py:435
  21.8 0.7 %collective-permute-start.6 = (f32[24,8,128]{2,1,0:T(8,128)S(1)}, f32[24,8,128]{2,1,0:T(8,128)S(1)}, u32[]{:S(2)}, u32[]{:S(2)}) collective-permute-start(f32[24,8,128]{2,1,0:T(8,128)S(1)} %get-tuple-element.76), channel_id=1, source_target_pairs={{4,8},{12,16},{20,24},{8,4},{16,12},{24,20},{5,9},{13,17},{21,25},... | collective-permute-start | bytes 294920 | tf_op jit(solution)/shard_map/ppermute | solution.py:434
  22.5 0.0 collective-permute-done.3.rest_in_ref
  22.5 0.0 collective-permute-done.4.rest_out_ref
  22.5 2.3 %shard_map.63 = (f32[4,128]{1,0:T(4,128)S(1)}, f32[24,64,128]{2,1,0:T(8,128)S(1)}, f32[96,768]{1,0:T(8,128)S(1)}, f32[16,768]{1,0:T(8,128)S(1)}, f32[12,8,768]{2,1,0:T(8,128)S(1)}) custom-call(f32[12,8,896]{2,1,0:T(8,128)S(1)} %get-tuple-element.58.x_ref, f32[24,96,128]{2,1,0:T(8,128)S(1)} %get-tuple-element.64.y_ref, ...), custom_call_target="tpu_custom_call" | custom-call | flops 1000000000 | bytes 8000000 | tf_op jit(solution)/shard_map/pallas_call | solution.py:873
  24.8 0.0 collective-permute-done.5.low_in_ref
  24.8 0.0 collective-permute-done.6.low_out_ref
  24.8 15.6 %all_to_all.5.sums_ref = f32[32,4,128]{2,1,0:T(4,128)S(1)} all-to-all(f32[32,4,128]{2,1,0:T(4,128)S(1)} %broadcast_in_dim.2), channel_id=1, replica_groups=mesh['rows'=8,'band'=4] {'rows','band'}, dimensions={0} | all-to-all | bytes 131072 | tf_op jit(solution)/shard_map/all_to_all | solution.py:894
  40.5 2.9 %shard_map.64 = (f32[8,48,3072]{2,1,0:T(8,128)}, f32[12,8,768]{2,1,0:T(8,128)}) custom-call(f32[32,4,128]{2,1,0:T(4,128)S(1)} %all_to_all.5.sums_ref, f32[24,64,128]{2,1,0:T(8,128)S(1)} %get-tuple-element.78.yh_ref, f32[24,384,128]{2,1,0:T(8,128)S(1)} %get-tuple-element.79.v_ref, f32[24,48,128]{2,1,0:T(8,128)S(1)} %get-tuple-element.80.diff_ref, ...), custom_call_target="tpu_custom_call" | custom-call | flops 100000000 | bytes 8000000 | tf_op jit(solution)/shard_map/pallas_call | solution.py:1017
  (1 shorter events, 0.0 us)
Async XLA Ops:
  1.9 11.1 %collective-permute-start.1 = (f32[14,2,768]{2,1,0:T(2,128)S(1)}, f32[14,2,768]{2,1,0:T(2,128)S(1)}, u32[]{:S(2)}, u32[]{:S(2)}) collective-permute-start(f32[14,2,768]{2,1,0:T(2,128)S(1)} %get-tuple-element.56), channel_id=1, source_target_pairs={{0,2},{1,3},{2,0},{3,1},{4,6},{5,7},{6,4},{7,5},{8,10},{9,11},{10,... | collective-permute-start | bytes 258056 | tf_op jit(solution)/shard_map/ppermute | solution.py:382
  6.0 7.1 %collective-permute-start = (f32[15,2,768]{2,1,0:T(2,128)S(1)}, f32[15,2,768]{2,1,0:T(2,128)S(1)}, u32[]{:S(2)}, u32[]{:S(2)}) collective-permute-start(f32[15,2,768]{2,1,0:T(2,128)S(1)} %get-tuple-element.55), channel_id=1, source_target_pairs={{0,1},{1,2},{2,3},{3,0},{4,5},{5,6},{6,7},{7,4},{8,9},{9,10},{10,1... | collective-permute-start | bytes 276488 | tf_op jit(solution)/shard_map/ppermute | solution.py:382
  7.6 6.4 %collective-permute-start.2 = (f32[15,2,768]{2,1,0:T(2,128)S(1)}, f32[15,2,768]{2,1,0:T(2,128)S(1)}, u32[]{:S(2)}, u32[]{:S(2)}) collective-permute-start(f32[15,2,768]{2,1,0:T(2,128)S(1)} %get-tuple-element.57), channel_id=1, source_target_pairs={{0,3},{1,0},{2,1},{3,2},{4,7},{5,4},{6,5},{7,6},{8,11},{9,8},{10,9... | collective-permute-start | bytes 276488 | tf_op jit(solution)/shard_map/ppermute | solution.py:382
  14.8 7.7 %collective-permute-start.3 = (f32[63,8,128]{2,1,0:T(8,128)S(1)}, f32[63,8,128]{2,1,0:T(8,128)S(1)}, u32[]{:S(2)}, u32[]{:S(2)}) collective-permute-start(f32[63,8,128]{2,1,0:T(8,128)S(1)} %get-tuple-element.71), channel_id=1, source_target_pairs={{0,4},{4,0},{8,12},{12,8},{16,20},{20,16},{24,28},{28,24},{1,5},{5... | collective-permute-start | bytes 774152 | tf_op jit(solution)/shard_map/ppermute | solution.py:435
  14.9 7.6 %collective-permute-start.4 = (f32[63,8,128]{2,1,0:T(8,128)S(1)}, f32[63,8,128]{2,1,0:T(8,128)S(1)}, u32[]{:S(2)}, u32[]{:S(2)}) collective-permute-start(f32[63,8,128]{2,1,0:T(8,128)S(1)} %get-tuple-element.72), channel_id=1, source_target_pairs={{4,8},{12,16},{20,24},{8,4},{16,12},{24,20},{5,9},{13,17},{21,25},... | collective-permute-start | bytes 774152 | tf_op jit(solution)/shard_map/ppermute | solution.py:434
  18.8 6.0 %collective-permute-start.5 = (f32[24,8,128]{2,1,0:T(8,128)S(1)}, f32[24,8,128]{2,1,0:T(8,128)S(1)}, u32[]{:S(2)}, u32[]{:S(2)}) collective-permute-start(f32[24,8,128]{2,1,0:T(8,128)S(1)} %get-tuple-element.75), channel_id=1, source_target_pairs={{0,4},{4,0},{8,12},{12,8},{16,20},{20,16},{24,28},{28,24},{1,5},{5... | collective-permute-start | bytes 294920 | tf_op jit(solution)/shard_map/ppermute | solution.py:435
  21.8 3.0 %collective-permute-start.6 = (f32[24,8,128]{2,1,0:T(8,128)S(1)}, f32[24,8,128]{2,1,0:T(8,128)S(1)}, u32[]{:S(2)}, u32[]{:S(2)}) collective-permute-start(f32[24,8,128]{2,1,0:T(8,128)S(1)} %get-tuple-element.76), channel_id=1, source_target_pairs={{4,8},{12,16},{20,24},{8,4},{16,12},{24,20},{5,9},{13,17},{21,25},... | collective-permute-start | bytes 294920 | tf_op jit(solution)/shard_map/ppermute | solution.py:434

commit v7 on v6

--- a/solution.py
+++ b/solution.py
@@ -443,9 +443,17 @@
             down = downs[i : i + 4] + [blank] * (4 - len(downs[i : i + 4]))
             put(outs, first + i // 4, jnp.concatenate(up, axis=0), jnp.concatenate(down, axis=0))
 
+    def adjoint_of(table_ref, col):
+        p1 = col.astype(BF16)
+        over = col - p1.astype(F32)
+        p2 = over.astype(BF16)
+        p3 = (over - p2.astype(F32)).astype(BF16)
+        weights = take(table_ref, "adjoint", row_variant())
+        return dot(weights, jnp.concatenate([p1, p2, p3, p1, p2, p1], axis=0))
+
     inner_fine = fine_tiles - 4
 
-    def early(pan_far, table_far, pan_ref, table_ref, coarse_out, fine_out, col_out, sems):
+    def early(pan_far, table_far, pan_ref, table_ref, coarse_out, fine_out, diff_out, q_out, sems):
         now = pl.ds(0, place["low"][0][0][0])
         later = pl.ds(now.size, table.shape[0] - now.size)
         copies = [
@@ -466,18 +474,26 @@
         coarse_out[...] = along_rows(rc, blocks(means, middle), blocks(fines, middle))
         starts = [2 * LANES * k - LANES for k in range(1, pairs - 1)]
         col = blocks(dot3(windows(panes, starts, 4 * LANES), both_parts(table_ref, "fine")), pairs - 2)
-        col_out[...] = col
-        fine_out[...] = filter_rows(take(table_ref, "rows_fine"), col)
+        rows = filter_rows(take(table_ref, "rows_fine"), col)
+        fine_out[...] = rows[h:]
+        diff = pan_ref[:, 2 * LANES : w - 2 * LANES] - rows[0:h]
         copies[2].wait()
-
-    pan_held, table_held, coarse_mid, fine_mid, col_mid = call(
+        adjoint = adjoint_of(table_ref, col)
+        for k in range(inner_fine):
+            at = slice(LANES * k, LANES * (k + 1))
+            diff_out[k + 2] = diff[:, at]
+            q_out[k + 2] = adjoint[:, at]
+
+    q_rows = -(-(hc + 9) // 16) * 16
+    pan_held, table_held, coarse_mid, fine_mid, diff_mid, q_mid = call(
         early,
         (
             shape(h, w),
             jax.ShapeDtypeStruct(table.shape, BF16),
             shape(2 * pad + 32, LANES * middle),
-            shape(h + 2 * HALO, LANES * inner_fine),
-            shape(h, LANES * inner_fine),
+            shape(2 * HALO, LANES * inner_fine),
+            shape(fine_tiles, h, LANES),
+            shape(fine_tiles, q_rows, LANES),
         ),
         [pltpu.SemaphoreType.DMA((3,))],
         cost=(2_000_000_000, 8_000_000),
@@ -610,16 +626,8 @@
                 value = float(weight) * x if value is None else value + float(weight) * x
         return value
 
-    def adjoint_of(table_ref, col):
-        p1 = col.astype(BF16)
-        over = col - p1.astype(F32)
-        p2 = over.astype(BF16)
-        p3 = (over - p2.astype(F32)).astype(BF16)
-        weights = take(table_ref, "adjoint", row_variant())
-        return dot(weights, jnp.concatenate([p1, p2, p3, p1, p2, p1], axis=0))
-
     def inside(
-        pan_ref, x_ref, s_ref, fm_ref, fe_ref, colm_ref, cole_ref, table_ref,
+        pan_ref, x_ref, s_ref, fm_ref, fe_ref, col_ref, table_ref, diff_in, q_in,
         y_out, v_out, acc_out, s_out, diff_out, q_out, edge_out, mean_out, lows_out, *outs,
     ):
         def store(index, value):
@@ -630,19 +638,22 @@
         s_cols = dot3(windows(rows, block_starts[:swir_tiles], 2 * LANES), both_parts(table_ref, "up3"))
         s_out[...] = blocks(s_cols, swir_tiles)
 
-        def joined(outer, inner):
-            return jnp.concatenate([outer[:, : 2 * LANES], inner, outer[:, 2 * LANES :]], axis=1)
-
-        low = joined(fe_ref[...], fm_ref[...])
-        diff = pan_ref[...] - low[0:h]
-        adjoint = adjoint_of(table_ref, joined(cole_ref[...], colm_ref[...]))
+        diff = jnp.concatenate([pan_ref[:, : 2 * LANES], pan_ref[:, w - 2 * LANES :]], axis=1) - fe_ref[0:h, :]
+        adjoint = adjoint_of(table_ref, col_ref[...])
         total = jnp.zeros((1, LANES), F32)
         for k in range(fine_tiles):
-            at = slice(LANES * k, LANES * (k + 1))
-            diff_out[k] = diff[:, at]
-            q_out[k] = adjoint[:, at]
-            total = total + adjoint[hc + 8 : hc + 9, at]
-            put(outs, k, low[h : h + HALO, at], low[h + HALO : h + 2 * HALO, at])
+            if 2 <= k < fine_tiles - 2:
+                at = slice(LANES * (k - 2), LANES * (k - 1))
+                up, down = fm_ref[0:HALO, at], fm_ref[HALO:, at]
+                total = total + q_in[k, hc + 8 : hc + 9, :]
+            else:
+                lane = LANES * (k % (fine_tiles - 4))
+                at = slice(lane, lane + LANES)
+                up, down = fe_ref[h : h + HALO, at], fe_ref[h + HALO :, at]
+                diff_out[k] = diff[:, at]
+                q_out[k] = adjoint[:, at]
+                total = total + adjoint[hc + 8 : hc + 9, at]
+            put(outs, k, up, down)
 
         row_id = lax.axis_index("rows")
         below = jnp.where(row_id > 0, 1.0, 0.0).astype(F32)
@@ -682,7 +693,6 @@
         for i in range(turns + 2):
             acc_out[i] = first[i]
 
-    q_rows = -(-(hc + 9) // 16) * 16
     y_own, v_own, acc_own, s_own, diff, q_own, mean_edge, mean_own, lows_own, low_in, low_out = call(
         inside,
         (
@@ -699,7 +709,8 @@
             shape(fine_tiles, 8, LANES),
         ),
         cost=(2_000_000_000, 8_000_000),
-    )(pan_held, x_loc, s_loc, fine_mid, fine_edge, col_mid, col_edge, table_held)
+        input_output_aliases={7: 4, 8: 5},
+    )(pan_held, x_loc, s_loc, fine_mid, fine_edge, col_edge, table_held, diff_mid, q_mid)
     low_in, low_out = trade(low_in, low_out)
 
     def moments(
@@ -759,7 +770,9 @@
             return tuple(accs) + (accp, accv)
 
         start = tuple(acc_ref[i] for i in range(turns)) + (acc_ref[turns + 1], acc_ref[turns])
-        first = lax.fori_loop(0, fine_tiles // 2, grouped(tile_step, 2), start)
+        first = start
+        for k in range(fine_tiles):
+            first = tile_step(k, first)
 
         beyond = [r for r in range(-HALO, hc + HALO) if not 0 <= r < hc]
         edges = []
@@ -927,22 +940,22 @@
                     cols[j] = cols[j] - factor * jnp.broadcast_to(cols[j][k : k + 1], (8, LANES))
             return cols[BANDS] * inverse
 
-        n1 = float(fine_pixels)
-        mean_v = column(total, 41) / n1
-        mean_p = column(total, 43) / n1
-        cov_v = pltpu.roll(total, LANES - 32, 1) / n1 - mean_v * across(mean_v)
-        cov_p = column(total, 40) / n1 - mean_v * mean_p
+        n1 = 1.0 / fine_pixels
+        mean_v = column(total, 41) * n1
+        mean_p = column(total, 43) * n1
+        cov_v = pltpu.roll(total, LANES - 32, 1) * n1 - mean_v * across(mean_v)
+        cov_p = column(total, 40) * n1 - mean_v * mean_p
         gain = cov_p / down(cov_p * solve(cov_v, cov_p))
 
-        n2 = float(fine_pixels // (RATIO_V * RATIO_V))
-        mean_l = column(total, 17) / n2
-        mean_s = column(total, 19) / n2
-        mean_d = column(total, 21) / n2
-        cov_ll = total / n2 - mean_l * across(mean_l)
-        cov_ls = pltpu.roll(total, LANES - 8, 1) / n2 - mean_l * across(mean_s)
-        cov_ld = column(total, 16) / n2 - mean_l * mean_d
-        cov_sd = column(total, 18) / n2 - mean_s * mean_d
-        cov_dd = column(total, 20) / n2 - mean_d * mean_d
+        n2 = RATIO_V * RATIO_V / fine_pixels
+        mean_l = column(total, 17) * n2
+        mean_s = column(total, 19) * n2
+        mean_d = column(total, 21) * n2
+        cov_ll = total * n2 - mean_l * across(mean_l)
+        cov_ls = pltpu.roll(total, LANES - 8, 1) * n2 - mean_l * across(mean_s)
+        cov_ld = column(total, 16) * n2 - mean_l * mean_d
+        cov_sd = column(total, 18) * n2 - mean_s * mean_d
+        cov_dd = column(total, 20) * n2 - mean_d * mean_d
         gain_row = across(gain)
         a2 = cov_ll + gain * across(cov_ld) + cov_ld * gain_row + gain * gain_row * cov_dd
         b2 = jnp.where(lane < BANDS, cov_ls + gain * across(cov_sd), 0.0)
@@ -976,7 +989,7 @@
             sent_tile(k).start()
             return carry
 
-        beside = fine_tiles // BANDS
+        beside = max(1, fine_tiles // (BANDS + BANDS // 2))
 
         def solve_step(k, carry):
             work, inverse = carry
@@ -993,7 +1006,6 @@
 
         start = (jnp.where(lane == BANDS, target, a2), jnp.zeros((8, LANES), F32))
         work, inverse = lax.fori_loop(0, BANDS, solve_step, start)
-        lax.fori_loop(BANDS * beside, fine_tiles, tile_step, 0)
         fit2 = column(work, BANDS) * inverse
         numer = down(fit2 * b2)
         share_row = numer / down(fit2 * target)
@@ -1006,6 +1018,8 @@
             swir[r] = s_ref[r] + share * seen
         last = pltpu.make_async_copy(swir, swir_out, sems.at[fine_tiles])
         last.start()
+
+        lax.fori_loop(BANDS * beside, fine_tiles, tile_step, 0)
 
         def drain(k, carry):
             sent_tile(k).wait()

time: 43.6 us -> 43.3 us (level)
  waiting for transfers between devices: 1 us -> 0.18 us
    ppermute x3, waiting for transfers between devices: 0.99 us -> 0.17 us  [local(): lax.ppermute(chunks[d], 'band', [(i, (i + d) % groups) for i in range(gro...]
    pallas_call x1, Pallas kernels: 3.13 us -> 3.94 us  [local(): call(early, (shape(h, w), jax.ShapeDtypeStruct(table.shape, BF16), shape(...]
  transfers between devices with their start and end apart: 7 -> 7, of which waited for: 2 -> 1; matrix products, arithmetic and copies ran while one was open for 0% -> 0% of each run, Pallas kernels for 20% -> 21%
where the time goes in v7:
time: 43.3 us; the launch traced here: 43.1 us
  blocking collectives  15.8 us (36%)
  Pallas kernels  14 us (32%)
  starting transfers between devices  12.4 us (29%)
  between operations  0.73 us (2%)
    all_to_all x1, blocking collectives, local(): lax.all_to_all(spread, ('rows', 'band'), split_axis=0, concat_axis=0, til...  15.8 us
    ppermute x3, starting transfers between devices, local(): lax.ppermute(chunks[d], 'band', [(i, (i + d) % groups) for i in range(gro...  7.92 us
    pallas_call x1, Pallas kernels, local(): call(early, (shape(h, w), jax.ShapeDtypeStruct(table.shape, BF16), shape(...  3.94 us
    ppermute x2, starting transfers between devices, trade(): return (lax.ppermute(inner, 'rows', pairs_in), outer)  3.12 us
    pallas_call x1, Pallas kernels, local(): call(finish, (shape(BANDS, h, w), shape(hc, BANDS, wc)), [pltpu.VMEM((fin...  2.94 us
    pallas_call x1, Pallas kernels, local(): call(inside, (shape(fine_tiles, 8 * hc, LANES), shape(fine_tiles, 8 * h,...  2.91 us
    pallas_call x1, Pallas kernels, local(): call(moments, (shape(4, LANES), shape(fine_tiles, 8 * len(around), LANES)...  2.12 us
    ppermute x2, starting transfers between devices, trade(): outer = lax.ppermute(outer, 'rows', pairs_out)  1.33 us
  transfers between devices with their start and end apart: 7, of which 1 were waited for; matrix products, arithmetic and copies ran while one was open for 0% of the time, Pallas kernels for 21%

profile of v7, /device:TPU:0, one launch (start us, length us, event | category | flops | bytes accessed | tf_op | source)
XLA Modules:
  0.0 43.1 jit_solution(5014851817246327334)
XLA Ops:
  0.6 1.3 %shard_map.59 = (f32[14,2,768]{2,1,0:T(2,128)S(1)}, f32[15,2,768]{2,1,0:T(2,128)S(1)}, f32[14,2,768]{2,1,0:T(2,128)S(1)}, f32[15,2,768]{2,1,0:T(2,128)S(1)}) custom-call(f32[48,3072]{1,0:T(8,128)} %pan_far, f32[12,2,3072]{2,1,0:T(2,128)} %bitcast.2, f32[2,4,1024]{2,1,0:T(4,128)} %swir_ref.1), custom_call_target="tpu_custom_call" | custom-call | bytes 8000000 | tf_op jit(solution)/shard_map/pallas_call | solution.py:368
  1.9 4.1 %collective-permute-start.1 = (f32[14,2,768]{2,1,0:T(2,128)S(1)}, f32[14,2,768]{2,1,0:T(2,128)S(1)}, u32[]{:S(2)}, u32[]{:S(2)}) collective-permute-start(f32[14,2,768]{2,1,0:T(2,128)S(1)} %get-tuple-element.57), channel_id=1, source_target_pairs={{0,2},{1,3},{2,0},{3,1},{4,6},{5,7},{6,4},{7,5},{8,10},{9,11},{10,... | collective-permute-start | bytes 258056 | tf_op jit(solution)/shard_map/ppermute | solution.py:382
  6.0 1.6 %collective-permute-start = (f32[15,2,768]{2,1,0:T(2,128)S(1)}, f32[15,2,768]{2,1,0:T(2,128)S(1)}, u32[]{:S(2)}, u32[]{:S(2)}) collective-permute-start(f32[15,2,768]{2,1,0:T(2,128)S(1)} %get-tuple-element.56), channel_id=1, source_target_pairs={{0,1},{1,2},{2,3},{3,0},{4,5},{5,6},{6,7},{7,4},{8,9},{9,10},{10,1... | collective-permute-start | bytes 276488 | tf_op jit(solution)/shard_map/ppermute | solution.py:382
  7.6 2.2 %collective-permute-start.2 = (f32[15,2,768]{2,1,0:T(2,128)S(1)}, f32[15,2,768]{2,1,0:T(2,128)S(1)}, u32[]{:S(2)}, u32[]{:S(2)}) collective-permute-start(f32[15,2,768]{2,1,0:T(2,128)S(1)} %get-tuple-element.58), channel_id=1, source_target_pairs={{0,3},{1,0},{2,1},{3,2},{4,7},{5,4},{6,5},{7,6},{8,11},{9,8},{10,9... | collective-permute-start | bytes 276488 | tf_op jit(solution)/shard_map/ppermute | solution.py:382
  9.9 3.9 %shard_map.60 = (f32[48,3072]{1,0:T(8,128)S(1)}, bf16[7296,256]{1,0:T(8,128)(2,1)S(1)}, f32[64,640]{1,0:T(8,128)S(1)}, f32[16,2560]{1,0:T(8,128)S(1)}, f32[24,48...) custom-call(f32[48,3072]{1,0:T(8,128)} %pan_far, bf16[7296,256]{1,0:T(8,128)(2,1)} %constant.2.clone.table_far), custom_call_target="tpu_custom_call" | custom-call | flops 2000000000 | bytes 8000000 | tf_op jit(solution)/shard_map/pallas_call | solution.py:488
  13.8 0.0 collective-permute-done.1.rest_2_
  13.8 0.0 collective-permute-done.rest_1_
  13.8 0.2 collective-permute-done.2.rest_3_
  14.0 0.8 %shard_map.61 = (f32[12,8,896]{2,1,0:T(8,128)S(1)}, f32[4,8,384]{2,1,0:T(8,128)S(1)}, f32[32,256]{1,0:T(8,128)S(1)}, f32[64,512]{1,0:T(8,128)S(1)}, f32[48,512]{...) custom-call(f32[48,3072]{1,0:T(8,128)S(1)} %get-tuple-element.52.pan_ref, ...), custom_call_target="tpu_custom_call" | custom-call | flops 200000000 | bytes 3000000 | tf_op jit(solution)/shard_map/pallas_call | solution.py:584
  14.8 0.1 collective-permute-start.3
  14.9 0.7 %collective-permute-start.4 = (f32[63,8,128]{2,1,0:T(8,128)S(1)}, f32[63,8,128]{2,1,0:T(8,128)S(1)}, u32[]{:S(2)}, u32[]{:S(2)}) collective-permute-start(f32[63,8,128]{2,1,0:T(8,128)S(1)} %get-tuple-element.74), channel_id=1, source_target_pairs={{4,8},{12,16},{20,24},{8,4},{16,12},{24,20},{5,9},{13,17},{21,25},... | collective-permute-start | bytes 774152 | tf_op jit(solution)/shard_map/ppermute | solution.py:434
  15.6 2.9 %shard_map.62 = (f32[24,96,128]{2,1,0:T(8,128)S(1)}, f32[24,384,128]{2,1,0:T(8,128)S(1)}, f32[8,8,128]{2,1,0:T(8,128)S(1)}, f32[32,768]{1,0:T(8,128)S(1)}, f32[2...) custom-call(f32[48,3072]{1,0:T(8,128)S(1)} %get-tuple-element.52.pan, ...), custom_call_target="tpu_custom_call", output_to_operand_aliasing={{4}: (7, {}), {5}: (8, {})} | custom-call | flops 2000000000 | bytes 8000000 | tf_op jit(solution)/shard_map/pallas_call | solution.py:696
  18.5 3.0 %collective-permute-start.5 = (f32[24,8,128]{2,1,0:T(8,128)S(1)}, f32[24,8,128]{2,1,0:T(8,128)S(1)}, u32[]{:S(2)}, u32[]{:S(2)}) collective-permute-start(f32[24,8,128]{2,1,0:T(8,128)S(1)} %get-tuple-element.77), channel_id=1, source_target_pairs={{0,4},{4,0},{8,12},{12,8},{16,20},{20,16},{24,28},{28,24},{1,5},{5... | collective-permute-start | bytes 294920 | tf_op jit(solution)/shard_map/ppermute | solution.py:435
  21.5 0.7 %collective-permute-start.6 = (f32[24,8,128]{2,1,0:T(8,128)S(1)}, f32[24,8,128]{2,1,0:T(8,128)S(1)}, u32[]{:S(2)}, u32[]{:S(2)}) collective-permute-start(f32[24,8,128]{2,1,0:T(8,128)S(1)} %get-tuple-element.78), channel_id=1, source_target_pairs={{4,8},{12,16},{20,24},{8,4},{16,12},{24,20},{5,9},{13,17},{21,25},... | collective-permute-start | bytes 294920 | tf_op jit(solution)/shard_map/ppermute | solution.py:434
  22.2 0.0 collective-permute-done.3.rest_in_ref
  22.2 0.0 collective-permute-done.4.rest_out_ref
  22.2 2.1 %shard_map.63 = (f32[4,128]{1,0:T(4,128)S(1)}, f32[24,64,128]{2,1,0:T(8,128)S(1)}, f32[96,768]{1,0:T(8,128)S(1)}, f32[16,768]{1,0:T(8,128)S(1)}, f32[12,8,768]{2,1,0:T(8,128)S(1)}) custom-call(f32[12,8,896]{2,1,0:T(8,128)S(1)} %get-tuple-element.59.x_ref, f32[24,96,128]{2,1,0:T(8,128)S(1)} %get-tuple-element.66.y_ref, ...), custom_call_target="tpu_custom_call" | custom-call | flops 1000000000 | bytes 8000000 | tf_op jit(solution)/shard_map/pallas_call | solution.py:886
  24.3 0.0 collective-permute-done.5.low_in_ref
  24.3 0.0 collective-permute-done.6.low_out_ref
  24.4 15.8 %all_to_all.5.sums_ref = f32[32,4,128]{2,1,0:T(4,128)S(1)} all-to-all(f32[32,4,128]{2,1,0:T(4,128)S(1)} %broadcast_in_dim.2), channel_id=1, replica_groups=mesh['rows'=8,'band'=4] {'rows','band'}, dimensions={0} | all-to-all | bytes 131072 | tf_op jit(solution)/shard_map/all_to_all | solution.py:907
  40.2 2.9 %shard_map.64 = (f32[8,48,3072]{2,1,0:T(8,128)}, f32[12,8,768]{2,1,0:T(8,128)}) custom-call(f32[32,4,128]{2,1,0:T(4,128)S(1)} %all_to_all.5.sums_ref, f32[24,64,128]{2,1,0:T(8,128)S(1)} %get-tuple-element.80.yh_ref, f32[24,384,128]{2,1,0:T(8,128)S(1)} %get-tuple-element.81.v_ref, f32[24,48,128]{2,1,0:T(8,128)S(1)} %get-tuple-element.82.diff_ref, ...), custom_call_target="tpu_custom_call" | custom-call | flops 100000000 | bytes 8000000 | tf_op jit(solution)/shard_map/pallas_call | solution.py:1031
  (1 shorter events, 0.0 us)
Async XLA Ops:
  1.9 11.9 %collective-permute-start.1 = (f32[14,2,768]{2,1,0:T(2,128)S(1)}, f32[14,2,768]{2,1,0:T(2,128)S(1)}, u32[]{:S(2)}, u32[]{:S(2)}) collective-permute-start(f32[14,2,768]{2,1,0:T(2,128)S(1)} %get-tuple-element.57), channel_id=1, source_target_pairs={{0,2},{1,3},{2,0},{3,1},{4,6},{5,7},{6,4},{7,5},{8,10},{9,11},{10,... | collective-permute-start | bytes 258056 | tf_op jit(solution)/shard_map/ppermute | solution.py:382
  6.0 7.8 %collective-permute-start = (f32[15,2,768]{2,1,0:T(2,128)S(1)}, f32[15,2,768]{2,1,0:T(2,128)S(1)}, u32[]{:S(2)}, u32[]{:S(2)}) collective-permute-start(f32[15,2,768]{2,1,0:T(2,128)S(1)} %get-tuple-element.56), channel_id=1, source_target_pairs={{0,1},{1,2},{2,3},{3,0},{4,5},{5,6},{6,7},{7,4},{8,9},{9,10},{10,1... | collective-permute-start | bytes 276488 | tf_op jit(solution)/shard_map/ppermute | solution.py:382
  7.6 6.4 %collective-permute-start.2 = (f32[15,2,768]{2,1,0:T(2,128)S(1)}, f32[15,2,768]{2,1,0:T(2,128)S(1)}, u32[]{:S(2)}, u32[]{:S(2)}) collective-permute-start(f32[15,2,768]{2,1,0:T(2,128)S(1)} %get-tuple-element.58), channel_id=1, source_target_pairs={{0,3},{1,0},{2,1},{3,2},{4,7},{5,4},{6,5},{7,6},{8,11},{9,8},{10,9... | collective-permute-start | bytes 276488 | tf_op jit(solution)/shard_map/ppermute | solution.py:382
  14.8 7.4 %collective-permute-start.3 = (f32[63,8,128]{2,1,0:T(8,128)S(1)}, f32[63,8,128]{2,1,0:T(8,128)S(1)}, u32[]{:S(2)}, u32[]{:S(2)}) collective-permute-start(f32[63,8,128]{2,1,0:T(8,128)S(1)} %get-tuple-element.73), channel_id=1, source_target_pairs={{0,4},{4,0},{8,12},{12,8},{16,20},{20,16},{24,28},{28,24},{1,5},{5... | collective-permute-start | bytes 774152 | tf_op jit(solution)/shard_map/ppermute | solution.py:435
  14.9 7.3 %collective-permute-start.4 = (f32[63,8,128]{2,1,0:T(8,128)S(1)}, f32[63,8,128]{2,1,0:T(8,128)S(1)}, u32[]{:S(2)}, u32[]{:S(2)}) collective-permute-start(f32[63,8,128]{2,1,0:T(8,128)S(1)} %get-tuple-element.74), channel_id=1, source_target_pairs={{4,8},{12,16},{20,24},{8,4},{16,12},{24,20},{5,9},{13,17},{21,25},... | collective-permute-start | bytes 774152 | tf_op jit(solution)/shard_map/ppermute | solution.py:434
  18.5 5.9 %collective-permute-start.5 = (f32[24,8,128]{2,1,0:T(8,128)S(1)}, f32[24,8,128]{2,1,0:T(8,128)S(1)}, u32[]{:S(2)}, u32[]{:S(2)}) collective-permute-start(f32[24,8,128]{2,1,0:T(8,128)S(1)} %get-tuple-element.77), channel_id=1, source_target_pairs={{0,4},{4,0},{8,12},{12,8},{16,20},{20,16},{24,28},{28,24},{1,5},{5... | collective-permute-start | bytes 294920 | tf_op jit(solution)/shard_map/ppermute | solution.py:435
  21.5 2.8 %collective-permute-start.6 = (f32[24,8,128]{2,1,0:T(8,128)S(1)}, f32[24,8,128]{2,1,0:T(8,128)S(1)}, u32[]{:S(2)}, u32[]{:S(2)}) collective-permute-start(f32[24,8,128]{2,1,0:T(8,128)S(1)} %get-tuple-element.78), channel_id=1, source_target_pairs={{4,8},{12,16},{20,24},{8,4},{16,12},{24,20},{5,9},{13,17},{21,25},... | collective-permute-start | bytes 294920 | tf_op jit(solution)/shard_map/ppermute | solution.py:434

commit v8 on v7

--- a/solution.py
+++ b/solution.py
@@ -963,7 +963,7 @@
 
         def sent_tile(k):
             lanes = pl.ds(pl.multiple_of(LANES * k, LANES), LANES)
-            held = tiles.reshape(fine_tiles, BANDS, apart_rows, LANES).at[k, :, pl.ds(0, h), :]
+            held = tiles.reshape(fine_tiles, BANDS + 1, apart_rows, LANES).at[k, pl.ds(0, BANDS), pl.ds(0, h), :]
             return pltpu.make_async_copy(held, vnir_out.at[:, :, lanes], sems.at[k])
 
         def tile_step(k, carry):
@@ -1032,7 +1032,7 @@
         finish,
         (shape(BANDS, h, w), shape(hc, BANDS, wc)),
         [
-            pltpu.VMEM((fine_tiles, BANDS * apart_rows, LANES), F32),
+            pltpu.VMEM((fine_tiles, (BANDS + 1) * apart_rows, LANES), F32),
             pltpu.VMEM((hc, BANDS, wc), F32),
             pltpu.VMEM((fine_tiles, 2 * HALO, LANES), F32),
             pltpu.SemaphoreType.DMA((fine_tiles + 1,)),

time: 43.3 us -> 43.3 us (level)
  no operation moved by 1% of the time
where the time goes in v8:
time: 43.3 us; the launch traced here: 43.1 us
  blocking collectives  15.8 us (36%)
  Pallas kernels  14 us (32%)
  starting transfers between devices  12.4 us (29%)
  between operations  0.73 us (2%)
    all_to_all x1, blocking collectives, local(): lax.all_to_all(spread, ('rows', 'band'), split_axis=0, concat_axis=0, til...  15.8 us
    ppermute x3, starting transfers between devices, local(): lax.ppermute(chunks[d], 'band', [(i, (i + d) % groups) for i in range(gro...  7.92 us
    pallas_call x1, Pallas kernels, local(): call(early, (shape(h, w), jax.ShapeDtypeStruct(table.shape, BF16), shape(...  3.94 us
    ppermute x2, starting transfers between devices, trade(): return (lax.ppermute(inner, 'rows', pairs_in), outer)  3.12 us
    pallas_call x1, Pallas kernels, local(): call(finish, (shape(BANDS, h, w), shape(hc, BANDS, wc)), [pltpu.VMEM((fin...  2.94 us
    pallas_call x1, Pallas kernels, local(): call(inside, (shape(fine_tiles, 8 * hc, LANES), shape(fine_tiles, 8 * h,...  2.91 us
    pallas_call x1, Pallas kernels, local(): call(moments, (shape(4, LANES), shape(fine_tiles, 8 * len(around), LANES)...  2.12 us
    ppermute x2, starting transfers between devices, trade(): outer = lax.ppermute(outer, 'rows', pairs_out)  1.33 us
  transfers between devices with their start and end apart: 7, of which 1 were waited for; matrix products, arithmetic and copies ran while one was open for 0% of the time, Pallas kernels for 21%

profile of v8, /device:TPU:0, one launch (start us, length us, event | category | flops | bytes accessed | tf_op | source)
XLA Modules:
  0.0 43.1 jit_solution(9452635663956228980)
XLA Ops:
  0.6 1.3 %shard_map.59 = (f32[14,2,768]{2,1,0:T(2,128)S(1)}, f32[15,2,768]{2,1,0:T(2,128)S(1)}, f32[14,2,768]{2,1,0:T(2,128)S(1)}, f32[15,2,768]{2,1,0:T(2,128)S(1)}) custom-call(f32[48,3072]{1,0:T(8,128)} %pan_far, f32[12,2,3072]{2,1,0:T(2,128)} %bitcast.2, f32[2,4,1024]{2,1,0:T(4,128)} %swir_ref.1), custom_call_target="tpu_custom_call" | custom-call | bytes 8000000 | tf_op jit(solution)/shard_map/pallas_call | solution.py:368
  1.9 4.1 %collective-permute-start.1 = (f32[14,2,768]{2,1,0:T(2,128)S(1)}, f32[14,2,768]{2,1,0:T(2,128)S(1)}, u32[]{:S(2)}, u32[]{:S(2)}) collective-permute-start(f32[14,2,768]{2,1,0:T(2,128)S(1)} %get-tuple-element.57), channel_id=1, source_target_pairs={{0,2},{1,3},{2,0},{3,1},{4,6},{5,7},{6,4},{7,5},{8,10},{9,11},{10,... | collective-permute-start | bytes 258056 | tf_op jit(solution)/shard_map/ppermute | solution.py:382
  6.0 1.6 %collective-permute-start = (f32[15,2,768]{2,1,0:T(2,128)S(1)}, f32[15,2,768]{2,1,0:T(2,128)S(1)}, u32[]{:S(2)}, u32[]{:S(2)}) collective-permute-start(f32[15,2,768]{2,1,0:T(2,128)S(1)} %get-tuple-element.56), channel_id=1, source_target_pairs={{0,1},{1,2},{2,3},{3,0},{4,5},{5,6},{6,7},{7,4},{8,9},{9,10},{10,1... | collective-permute-start | bytes 276488 | tf_op jit(solution)/shard_map/ppermute | solution.py:382
  7.6 2.2 %collective-permute-start.2 = (f32[15,2,768]{2,1,0:T(2,128)S(1)}, f32[15,2,768]{2,1,0:T(2,128)S(1)}, u32[]{:S(2)}, u32[]{:S(2)}) collective-permute-start(f32[15,2,768]{2,1,0:T(2,128)S(1)} %get-tuple-element.58), channel_id=1, source_target_pairs={{0,3},{1,0},{2,1},{3,2},{4,7},{5,4},{6,5},{7,6},{8,11},{9,8},{10,9... | collective-permute-start | bytes 276488 | tf_op jit(solution)/shard_map/ppermute | solution.py:382
  9.9 3.9 %shard_map.60 = (f32[48,3072]{1,0:T(8,128)S(1)}, bf16[7296,256]{1,0:T(8,128)(2,1)S(1)}, f32[64,640]{1,0:T(8,128)S(1)}, f32[16,2560]{1,0:T(8,128)S(1)}, f32[24,48...) custom-call(f32[48,3072]{1,0:T(8,128)} %pan_far, bf16[7296,256]{1,0:T(8,128)(2,1)} %constant.2.clone.table_far), custom_call_target="tpu_custom_call" | custom-call | flops 2000000000 | bytes 8000000 | tf_op jit(solution)/shard_map/pallas_call | solution.py:488
  13.8 0.0 collective-permute-done.1.rest_2_
  13.8 0.0 collective-permute-done.rest_1_
  13.8 0.2 collective-permute-done.2.rest_3_
  14.0 0.8 %shard_map.61 = (f32[12,8,896]{2,1,0:T(8,128)S(1)}, f32[4,8,384]{2,1,0:T(8,128)S(1)}, f32[32,256]{1,0:T(8,128)S(1)}, f32[64,512]{1,0:T(8,128)S(1)}, f32[48,512]{...) custom-call(f32[48,3072]{1,0:T(8,128)S(1)} %get-tuple-element.52.pan_ref, ...), custom_call_target="tpu_custom_call" | custom-call | flops 200000000 | bytes 3000000 | tf_op jit(solution)/shard_map/pallas_call | solution.py:584
  14.8 0.1 collective-permute-start.3
  14.9 0.7 %collective-permute-start.4 = (f32[63,8,128]{2,1,0:T(8,128)S(1)}, f32[63,8,128]{2,1,0:T(8,128)S(1)}, u32[]{:S(2)}, u32[]{:S(2)}) collective-permute-start(f32[63,8,128]{2,1,0:T(8,128)S(1)} %get-tuple-element.74), channel_id=1, source_target_pairs={{4,8},{12,16},{20,24},{8,4},{16,12},{24,20},{5,9},{13,17},{21,25},... | collective-permute-start | bytes 774152 | tf_op jit(solution)/shard_map/ppermute | solution.py:434
  15.6 2.9 %shard_map.62 = (f32[24,96,128]{2,1,0:T(8,128)S(1)}, f32[24,384,128]{2,1,0:T(8,128)S(1)}, f32[8,8,128]{2,1,0:T(8,128)S(1)}, f32[32,768]{1,0:T(8,128)S(1)}, f32[2...) custom-call(f32[48,3072]{1,0:T(8,128)S(1)} %get-tuple-element.52.pan, ...), custom_call_target="tpu_custom_call", output_to_operand_aliasing={{4}: (7, {}), {5}: (8, {})} | custom-call | flops 2000000000 | bytes 8000000 | tf_op jit(solution)/shard_map/pallas_call | solution.py:696
  18.5 3.0 %collective-permute-start.5 = (f32[24,8,128]{2,1,0:T(8,128)S(1)}, f32[24,8,128]{2,1,0:T(8,128)S(1)}, u32[]{:S(2)}, u32[]{:S(2)}) collective-permute-start(f32[24,8,128]{2,1,0:T(8,128)S(1)} %get-tuple-element.77), channel_id=1, source_target_pairs={{0,4},{4,0},{8,12},{12,8},{16,20},{20,16},{24,28},{28,24},{1,5},{5... | collective-permute-start | bytes 294920 | tf_op jit(solution)/shard_map/ppermute | solution.py:435
  21.5 0.7 %collective-permute-start.6 = (f32[24,8,128]{2,1,0:T(8,128)S(1)}, f32[24,8,128]{2,1,0:T(8,128)S(1)}, u32[]{:S(2)}, u32[]{:S(2)}) collective-permute-start(f32[24,8,128]{2,1,0:T(8,128)S(1)} %get-tuple-element.78), channel_id=1, source_target_pairs={{4,8},{12,16},{20,24},{8,4},{16,12},{24,20},{5,9},{13,17},{21,25},... | collective-permute-start | bytes 294920 | tf_op jit(solution)/shard_map/ppermute | solution.py:434
  22.2 0.0 collective-permute-done.3.rest_in_ref
  22.2 0.0 collective-permute-done.4.rest_out_ref
  22.2 2.1 %shard_map.63 = (f32[4,128]{1,0:T(4,128)S(1)}, f32[24,64,128]{2,1,0:T(8,128)S(1)}, f32[96,768]{1,0:T(8,128)S(1)}, f32[16,768]{1,0:T(8,128)S(1)}, f32[12,8,768]{2,1,0:T(8,128)S(1)}) custom-call(f32[12,8,896]{2,1,0:T(8,128)S(1)} %get-tuple-element.59.x_ref, f32[24,96,128]{2,1,0:T(8,128)S(1)} %get-tuple-element.66.y_ref, ...), custom_call_target="tpu_custom_call" | custom-call | flops 1000000000 | bytes 8000000 | tf_op jit(solution)/shard_map/pallas_call | solution.py:886
  24.3 0.0 collective-permute-done.5.low_in_ref
  24.3 0.0 collective-permute-done.6.low_out_ref
  24.4 15.8 %all_to_all.5.sums_ref = f32[32,4,128]{2,1,0:T(4,128)S(1)} all-to-all(f32[32,4,128]{2,1,0:T(4,128)S(1)} %broadcast_in_dim.2), channel_id=1, replica_groups=mesh['rows'=8,'band'=4] {'rows','band'}, dimensions={0} | all-to-all | bytes 131072 | tf_op jit(solution)/shard_map/all_to_all | solution.py:907
  40.2 2.9 %shard_map.64 = (f32[8,48,3072]{2,1,0:T(8,128)}, f32[12,8,768]{2,1,0:T(8,128)}) custom-call(f32[32,4,128]{2,1,0:T(4,128)S(1)} %all_to_all.5.sums_ref, f32[24,64,128]{2,1,0:T(8,128)S(1)} %get-tuple-element.80.yh_ref, f32[24,384,128]{2,1,0:T(8,128)S(1)} %get-tuple-element.81.v_ref, f32[24,48,128]{2,1,0:T(8,128)S(1)} %get-tuple-element.82.diff_ref, ...), custom_call_target="tpu_custom_call" | custom-call | flops 100000000 | bytes 8000000 | tf_op jit(solution)/shard_map/pallas_call | solution.py:1031
  (1 shorter events, 0.0 us)
Async XLA Ops:
  1.9 11.9 %collective-permute-start.1 = (f32[14,2,768]{2,1,0:T(2,128)S(1)}, f32[14,2,768]{2,1,0:T(2,128)S(1)}, u32[]{:S(2)}, u32[]{:S(2)}) collective-permute-start(f32[14,2,768]{2,1,0:T(2,128)S(1)} %get-tuple-element.57), channel_id=1, source_target_pairs={{0,2},{1,3},{2,0},{3,1},{4,6},{5,7},{6,4},{7,5},{8,10},{9,11},{10,... | collective-permute-start | bytes 258056 | tf_op jit(solution)/shard_map/ppermute | solution.py:382
  6.0 7.8 %collective-permute-start = (f32[15,2,768]{2,1,0:T(2,128)S(1)}, f32[15,2,768]{2,1,0:T(2,128)S(1)}, u32[]{:S(2)}, u32[]{:S(2)}) collective-permute-start(f32[15,2,768]{2,1,0:T(2,128)S(1)} %get-tuple-element.56), channel_id=1, source_target_pairs={{0,1},{1,2},{2,3},{3,0},{4,5},{5,6},{6,7},{7,4},{8,9},{9,10},{10,1... | collective-permute-start | bytes 276488 | tf_op jit(solution)/shard_map/ppermute | solution.py:382
  7.6 6.4 %collective-permute-start.2 = (f32[15,2,768]{2,1,0:T(2,128)S(1)}, f32[15,2,768]{2,1,0:T(2,128)S(1)}, u32[]{:S(2)}, u32[]{:S(2)}) collective-permute-start(f32[15,2,768]{2,1,0:T(2,128)S(1)} %get-tuple-element.58), channel_id=1, source_target_pairs={{0,3},{1,0},{2,1},{3,2},{4,7},{5,4},{6,5},{7,6},{8,11},{9,8},{10,9... | collective-permute-start | bytes 276488 | tf_op jit(solution)/shard_map/ppermute | solution.py:382
  14.8 7.4 %collective-permute-start.3 = (f32[63,8,128]{2,1,0:T(8,128)S(1)}, f32[63,8,128]{2,1,0:T(8,128)S(1)}, u32[]{:S(2)}, u32[]{:S(2)}) collective-permute-start(f32[63,8,128]{2,1,0:T(8,128)S(1)} %get-tuple-element.73), channel_id=1, source_target_pairs={{0,4},{4,0},{8,12},{12,8},{16,20},{20,16},{24,28},{28,24},{1,5},{5... | collective-permute-start | bytes 774152 | tf_op jit(solution)/shard_map/ppermute | solution.py:435
  14.9 7.3 %collective-permute-start.4 = (f32[63,8,128]{2,1,0:T(8,128)S(1)}, f32[63,8,128]{2,1,0:T(8,128)S(1)}, u32[]{:S(2)}, u32[]{:S(2)}) collective-permute-start(f32[63,8,128]{2,1,0:T(8,128)S(1)} %get-tuple-element.74), channel_id=1, source_target_pairs={{4,8},{12,16},{20,24},{8,4},{16,12},{24,20},{5,9},{13,17},{21,25},... | collective-permute-start | bytes 774152 | tf_op jit(solution)/shard_map/ppermute | solution.py:434
  18.5 5.9 %collective-permute-start.5 = (f32[24,8,128]{2,1,0:T(8,128)S(1)}, f32[24,8,128]{2,1,0:T(8,128)S(1)}, u32[]{:S(2)}, u32[]{:S(2)}) collective-permute-start(f32[24,8,128]{2,1,0:T(8,128)S(1)} %get-tuple-element.77), channel_id=1, source_target_pairs={{0,4},{4,0},{8,12},{12,8},{16,20},{20,16},{24,28},{28,24},{1,5},{5... | collective-permute-start | bytes 294920 | tf_op jit(solution)/shard_map/ppermute | solution.py:435
  21.5 2.8 %collective-permute-start.6 = (f32[24,8,128]{2,1,0:T(8,128)S(1)}, f32[24,8,128]{2,1,0:T(8,128)S(1)}, u32[]{:S(2)}, u32[]{:S(2)}) collective-permute-start(f32[24,8,128]{2,1,0:T(8,128)S(1)} %get-tuple-element.78), channel_id=1, source_target_pairs={{4,8},{12,16},{20,24},{8,4},{16,12},{24,20},{5,9},{13,17},{21,25},... | collective-permute-start | bytes 294920 | tf_op jit(solution)/shard_map/ppermute | solution.py:434

commit v9 on v8

--- a/solution.py
+++ b/solution.py
@@ -628,7 +628,7 @@
 
     def inside(
         pan_ref, x_ref, s_ref, fm_ref, fe_ref, col_ref, table_ref, diff_in, q_in,
-        y_out, v_out, acc_out, s_out, diff_out, q_out, edge_out, mean_out, lows_out, *outs,
+        y_out, v_out, acc_out, s_out, diff_out, q_out, *outs,
     ):
         def store(index, value):
             y_out[index] = value
@@ -655,6 +655,47 @@
                 total = total + adjoint[hc + 8 : hc + 9, at]
             put(outs, k, up, down)
 
+        acc_out[turns + 2] = jnp.concatenate([total, jnp.zeros((7, LANES), F32)], axis=0)
+
+        def tile_step(k, carry):
+            accs, accv, accp = list(carry[:turns]), carry[turns], carry[turns + 1]
+            ys = {m: y_out[k, pl.ds(8 * (m - 2), 8), :] for m in own_rows}
+            for m in own_rows:
+                z = weighted((gram[m, other], ys[other]) for other in own_rows)
+                accs[0] = accs[0] + z * ys[m]
+                for i in range(1, turns):
+                    accs[i] = accs[i] + z * pltpu.roll(ys[m], i, 0)
+                accv = accv + float(rise[m]) * ys[m]
+                accp = accp + ys[m] * q_out[k, pl.ds(m + 2, 1), :]
+            for m in range(hc):
+                for p in range(RATIO_V):
+                    r = RATIO_V * m + p
+                    v_out[k, pl.ds(8 * r, 8), :] = weighted((C4[t, p], ys[m + t]) for t in range(5) if m + t in ys)
+            return tuple(accs) + (accv, accp)
+
+        zero = jnp.zeros((8, LANES), F32)
+        first = lax.fori_loop(0, fine_tiles // 2, grouped(tile_step, 2), (zero,) * (turns + 2))
+        for i in range(turns + 2):
+            acc_out[i] = first[i]
+
+    y_own, v_own, acc_own, s_own, diff, q_own, low_in, low_out = call(
+        inside,
+        (
+            shape(fine_tiles, 8 * hc, LANES),
+            shape(fine_tiles, 8 * h, LANES),
+            shape(turns + 3, 8, LANES),
+            shape(8 * hs, wc),
+            shape(fine_tiles, h, LANES),
+            shape(fine_tiles, q_rows, LANES),
+            shape(fine_tiles, 8, LANES),
+            shape(fine_tiles, 8, LANES),
+        ),
+        cost=(2_000_000_000, 8_000_000),
+        input_output_aliases={7: 4, 8: 5},
+    )(pan_held, x_loc, s_loc, fine_mid, fine_edge, col_edge, table_held, diff_mid, q_mid)
+    low_in, low_out = trade(low_in, low_out)
+
+    def means_of(x_ref, table_ref, edge_out, mean_out, lows_out):
         row_id = lax.axis_index("rows")
         below = jnp.where(row_id > 0, 1.0, 0.0).astype(F32)
         above = jnp.where(row_id < strips - 1, 1.0, 0.0).astype(F32)
@@ -670,48 +711,12 @@
         reach = TAPS_S // 2
         for r in range(hc):
             lows_out[r] = weighted((KC[t + reach], means[r + t]) for t in range(-reach, reach + 1) if r + t in means)
-        acc_out[turns + 2] = jnp.concatenate([total, jnp.zeros((7, LANES), F32)], axis=0)
-
-        def tile_step(k, carry):
-            accs, accv, accp = list(carry[:turns]), carry[turns], carry[turns + 1]
-            ys = {m: y_out[k, pl.ds(8 * (m - 2), 8), :] for m in own_rows}
-            for m in own_rows:
-                z = weighted((gram[m, other], ys[other]) for other in own_rows)
-                accs[0] = accs[0] + z * ys[m]
-                for i in range(1, turns):
-                    accs[i] = accs[i] + z * pltpu.roll(ys[m], i, 0)
-                accv = accv + float(rise[m]) * ys[m]
-                accp = accp + ys[m] * q_out[k, pl.ds(m + 2, 1), :]
-            for m in range(hc):
-                for p in range(RATIO_V):
-                    r = RATIO_V * m + p
-                    v_out[k, pl.ds(8 * r, 8), :] = weighted((C4[t, p], ys[m + t]) for t in range(5) if m + t in ys)
-            return tuple(accs) + (accv, accp)
-
-        zero = jnp.zeros((8, LANES), F32)
-        first = lax.fori_loop(0, fine_tiles // 2, grouped(tile_step, 2), (zero,) * (turns + 2))
-        for i in range(turns + 2):
-            acc_out[i] = first[i]
-
-    y_own, v_own, acc_own, s_own, diff, q_own, mean_edge, mean_own, lows_own, low_in, low_out = call(
-        inside,
-        (
-            shape(fine_tiles, 8 * hc, LANES),
-            shape(fine_tiles, 8 * h, LANES),
-            shape(turns + 3, 8, LANES),
-            shape(8 * hs, wc),
-            shape(fine_tiles, h, LANES),
-            shape(fine_tiles, q_rows, LANES),
-            shape(4, BANDS, wf),
-            shape(8 * (hc - 4), wc),
-            shape(hc, BANDS, wf),
-            shape(fine_tiles, 8, LANES),
-            shape(fine_tiles, 8, LANES),
-        ),
-        cost=(2_000_000_000, 8_000_000),
-        input_output_aliases={7: 4, 8: 5},
-    )(pan_held, x_loc, s_loc, fine_mid, fine_edge, col_edge, table_held, diff_mid, q_mid)
-    low_in, low_out = trade(low_in, low_out)
+
+    mean_edge, mean_own, lows_own = call(
+        means_of,
+        (shape(4, BANDS, wf), shape(8 * (hc - 4), wc), shape(hc, BANDS, wf)),
+        cost=(200_000_000, 3_000_000),
+    )(x_loc, table_held)
 
     def moments(
         x_ref, y_ref, acc_ref, scol_ref, q_ref, edge_ref, mean_ref, lows_ref,
@@ -866,7 +871,7 @@
             return jnp.broadcast_to(jnp.sum(acc, axis=1, keepdims=True), (8, LANES))
 
         table = zero
-        for base, accs in ((0, ll), (32, first[:turns])):
+        for base, accs in ((0, ll), (16, first[:turns])):
             for i in range(turns):
                 col = column_of(accs[i])
                 table = jnp.where(lane == base + lax.rem(sub + BANDS - i, BANDS), col, table)
@@ -874,19 +879,22 @@
                     turned = pltpu.roll(col, BANDS - i, 0)
                     table = jnp.where(lane == base + lax.rem(sub + i, BANDS), turned, table)
         singles = [(8 + i, cross[i]) for i in range(BANDS)]
-        singles += [(16, ld), (17, ls), (18, sd), (19, ss), (20, dd), (21, ds)]
-        singles += [(40, first[turns]), (41, first[turns + 1])]
+        singles += [(24, ld), (25, ls), (26, sd), (27, ss), (28, first[turns]), (29, first[turns + 1])]
         for index, acc in singles:
             table = jnp.where(lane == index, column_of(acc), table)
         total = jnp.sum(jnp.sum(acc_ref[turns + 2], axis=0, keepdims=True), axis=1, keepdims=True)
-        table = jnp.where(lane == 43, total, table)
-        turned = pltpu.roll(table, HALF, 1)
-        mom_out[...] = jnp.where(lane[0:4] < HALF, table[0:4], turned[4:8])
+        rest_of = jnp.where(sub == 0, column_of(dd), jnp.where(sub == 1, column_of(ds), total))
+        table = jnp.where(lane == 30, rest_of, table)
+        packed = table[0:2]
+        for q in range(1, 4):
+            turned = pltpu.roll(table, 32 * q, 1)
+            packed = jnp.where(lane[0:2] >= 32 * q, turned[2 * q : 2 * q + 2], packed)
+        mom_out[...] = packed
 
     mom, y_halo, ugap, dgap, s_up = call(
         moments,
         (
-            shape(4, LANES),
+            shape(2, LANES),
             shape(fine_tiles, 8 * len(around), LANES),
             shape(8 * hc, wc),
             shape(pad, wc),
@@ -918,7 +926,14 @@
         terms = [sums_ref[index] for index in range(devices)]
         while len(terms) > 1:
             terms = [sum(terms[i : i + 2][1:], terms[i]) for i in range(0, len(terms), 2)]
-        total = jnp.concatenate([terms[0], pltpu.roll(terms[0], HALF, 1)], axis=0)
+        packed = jnp.concatenate([terms[0]] * 4, axis=0)
+        total = packed
+        for q in range(1, 4):
+            total = jnp.where(sub >= 2 * q, pltpu.roll(packed, LANES - 32 * q, 1), total)
+
+        def single(row):
+            return jnp.broadcast_to(total[row : row + 1, 30:31], (8, LANES))
+
 
         def column(x, index):
             return jnp.broadcast_to(x[:, index : index + 1], (8, LANES))
@@ -941,21 +956,21 @@
             return cols[BANDS] * inverse
 
         n1 = 1.0 / fine_pixels
-        mean_v = column(total, 41) * n1
-        mean_p = column(total, 43) * n1
-        cov_v = pltpu.roll(total, LANES - 32, 1) * n1 - mean_v * across(mean_v)
-        cov_p = column(total, 40) * n1 - mean_v * mean_p
+        mean_v = column(total, 29) * n1
+        mean_p = single(2) * n1
+        cov_v = pltpu.roll(total, LANES - 16, 1) * n1 - mean_v * across(mean_v)
+        cov_p = column(total, 28) * n1 - mean_v * mean_p
         gain = cov_p / down(cov_p * solve(cov_v, cov_p))
 
         n2 = RATIO_V * RATIO_V / fine_pixels
-        mean_l = column(total, 17) * n2
-        mean_s = column(total, 19) * n2
-        mean_d = column(total, 21) * n2
+        mean_l = column(total, 25) * n2
+        mean_s = column(total, 27) * n2
+        mean_d = single(1) * n2
         cov_ll = total * n2 - mean_l * across(mean_l)
         cov_ls = pltpu.roll(total, LANES - 8, 1) * n2 - mean_l * across(mean_s)
-        cov_ld = column(total, 16) * n2 - mean_l * mean_d
-        cov_sd = column(total, 18) * n2 - mean_s * mean_d
-        cov_dd = column(total, 20) * n2 - mean_d * mean_d
+        cov_ld = column(total, 24) * n2 - mean_l * mean_d
+        cov_sd = column(total, 26) * n2 - mean_s * mean_d
+        cov_dd = single(0) * n2 - mean_d * mean_d
         gain_row = across(gain)
         a2 = cov_ll + gain * across(cov_ld) + cov_ld * gain_row + gain * gain_row * cov_dd
         b2 = jnp.where(lane < BANDS, cov_ls + gain * across(cov_sd), 0.0)

time: 43.3 us -> 43 us (level)
  waiting for transfers between devices: 0.18 us -> 3.38 us
  starting transfers between devices: 12.4 us -> 10.4 us
  blocking collectives: 15.8 us -> 14 us
    ppermute x3, waiting for transfers between devices: 0.17 us -> 3.37 us  [local(): lax.ppermute(chunks[d], 'band', [(i, (i + d) % groups) for i in range(gro...]
    ppermute x3, starting transfers between devices: 7.92 us -> 6.11 us  [local(): lax.ppermute(chunks[d], 'band', [(i, (i + d) % groups) for i in range(gro...]
    all_to_all x1, blocking collectives: 15.8 us -> 14 us  [local(): lax.all_to_all(spread, ('rows', 'band'), split_axis=0, concat_axis=0, til...]
    pallas_call x1 -> x2, Pallas kernels: 2.12 us -> 2.7 us  [the longest x1 2.15 us: local(): call(moments, (shape(2, LANES), shape(fine_tiles, 8 * len(around), LANES)...]
  transfers between devices with their start and end apart: 7 -> 7, of which waited for: 1 -> 1; matrix products, arithmetic and copies ran while one was open for 0% -> 0% of each run, Pallas kernels for 21% -> 22%
where the time goes in v9:
time: 43 us; the launch traced here: 42.8 us
  Pallas kernels  14.3 us (33%)
  blocking collectives  14 us (33%)
  starting transfers between devices  10.4 us (24%)
  waiting for transfers between devices  3.38 us (8%)
  between operations  0.72 us (2%)
    all_to_all x1, blocking collectives, local(): lax.all_to_all(spread, ('rows', 'band'), split_axis=0, concat_axis=0, til...  14 us
    ppermute x3, starting transfers between devices, local(): lax.ppermute(chunks[d], 'band', [(i, (i + d) % groups) for i in range(gro...  6.11 us
    pallas_call x1, Pallas kernels, local(): call(early, (shape(h, w), jax.ShapeDtypeStruct(table.shape, BF16), shape(...  3.94 us
    ppermute x3, waiting for transfers between devices, local(): lax.ppermute(chunks[d], 'band', [(i, (i + d) % groups) for i in range(gro...  3.37 us
    ppermute x2, starting transfers between devices, trade(): return (lax.ppermute(inner, 'rows', pairs_in), outer)  2.97 us
    pallas_call x1, Pallas kernels, local(): call(finish, (shape(BANDS, h, w), shape(hc, BANDS, wc)), [pltpu.VMEM((fin...  2.94 us
    pallas_call x1, Pallas kernels, local(): call(inside, (shape(fine_tiles, 8 * hc, LANES), shape(fine_tiles, 8 * h,...  2.57 us
    pallas_call x1, Pallas kernels, local(): call(moments, (shape(2, LANES), shape(fine_tiles, 8 * len(around), LANES)...  2.15 us
  transfers between devices with their start and end apart: 7, of which 1 were waited for; matrix products, arithmetic and copies ran while one was open for 0% of the time, Pallas kernels for 22%

profile of v9, /device:TPU:0, one launch (start us, length us, event | category | flops | bytes accessed | tf_op | source)
XLA Modules:
  0.0 42.8 jit_solution(54353510925944911)
XLA Ops:
  0.6 1.3 %shard_map.59 = (f32[14,2,768]{2,1,0:T(2,128)S(1)}, f32[15,2,768]{2,1,0:T(2,128)S(1)}, f32[14,2,768]{2,1,0:T(2,128)S(1)}, f32[15,2,768]{2,1,0:T(2,128)S(1)}) custom-call(f32[48,3072]{1,0:T(8,128)} %pan_far, f32[12,2,3072]{2,1,0:T(2,128)} %bitcast.2, f32[2,4,1024]{2,1,0:T(4,128)} %swir_ref.1), custom_call_target="tpu_custom_call" | custom-call | bytes 8000000 | tf_op jit(solution)/shard_map/pallas_call | solution.py:368
  1.9 3.1 %collective-permute-start = (f32[15,2,768]{2,1,0:T(2,128)S(1)}, f32[15,2,768]{2,1,0:T(2,128)S(1)}, u32[]{:S(2)}, u32[]{:S(2)}) collective-permute-start(f32[15,2,768]{2,1,0:T(2,128)S(1)} %get-tuple-element.56), channel_id=1, source_target_pairs={{0,1},{1,2},{2,3},{3,0},{4,5},{5,6},{6,7},{7,4},{8,9},{9,10},{10,1... | collective-permute-start | bytes 276488 | tf_op jit(solution)/shard_map/ppermute | solution.py:382
  5.0 2.1 %collective-permute-start.2 = (f32[15,2,768]{2,1,0:T(2,128)S(1)}, f32[15,2,768]{2,1,0:T(2,128)S(1)}, u32[]{:S(2)}, u32[]{:S(2)}) collective-permute-start(f32[15,2,768]{2,1,0:T(2,128)S(1)} %get-tuple-element.58), channel_id=1, source_target_pairs={{0,3},{1,0},{2,1},{3,2},{4,7},{5,4},{6,5},{7,6},{8,11},{9,8},{10,9... | collective-permute-start | bytes 276488 | tf_op jit(solution)/shard_map/ppermute | solution.py:382
  7.1 0.9 %collective-permute-start.1 = (f32[14,2,768]{2,1,0:T(2,128)S(1)}, f32[14,2,768]{2,1,0:T(2,128)S(1)}, u32[]{:S(2)}, u32[]{:S(2)}) collective-permute-start(f32[14,2,768]{2,1,0:T(2,128)S(1)} %get-tuple-element.57), channel_id=1, source_target_pairs={{0,2},{1,3},{2,0},{3,1},{4,6},{5,7},{6,4},{7,5},{8,10},{9,11},{10,... | collective-permute-start | bytes 258056 | tf_op jit(solution)/shard_map/ppermute | solution.py:382
  8.1 3.9 %shard_map.60 = (f32[48,3072]{1,0:T(8,128)S(1)}, bf16[7296,256]{1,0:T(8,128)(2,1)S(1)}, f32[64,640]{1,0:T(8,128)S(1)}, f32[16,2560]{1,0:T(8,128)S(1)}, f32[24,48...) custom-call(f32[48,3072]{1,0:T(8,128)} %pan_far, bf16[7296,256]{1,0:T(8,128)(2,1)} %constant.2.clone.table_far), custom_call_target="tpu_custom_call" | custom-call | flops 2000000000 | bytes 8000000 | tf_op jit(solution)/shard_map/pallas_call | solution.py:488
  12.0 3.4 %collective-permute-done.1.rest_2_ = f32[14,2,768]{2,1,0:T(2,128)S(1)} collective-permute-done((f32[14,2,768]{2,1,0:T(2,128)S(1)}, f32[14,2,768]{2,1,0:T(2,128)S(1)}, u32[]{:S(2)}, u32[]{:S(2)}) %collective-permute-start.1) | collective-permute-done | bytes 86048 | tf_op jit(solution)/shard_map/ppermute | solution.py:382
  15.4 0.0 collective-permute-done.rest_1_
  15.4 0.0 collective-permute-done.2.rest_3_
  15.4 0.8 %shard_map.61 = (f32[12,8,896]{2,1,0:T(8,128)S(1)}, f32[4,8,384]{2,1,0:T(8,128)S(1)}, f32[32,256]{1,0:T(8,128)S(1)}, f32[64,512]{1,0:T(8,128)S(1)}, f32[48,512]{...) custom-call(f32[48,3072]{1,0:T(8,128)S(1)} %get-tuple-element.52.pan_ref, ...), custom_call_target="tpu_custom_call" | custom-call | flops 200000000 | bytes 3000000 | tf_op jit(solution)/shard_map/pallas_call | solution.py:584
  16.2 0.1 collective-permute-start.3
  16.3 0.7 %collective-permute-start.4 = (f32[63,8,128]{2,1,0:T(8,128)S(1)}, f32[63,8,128]{2,1,0:T(8,128)S(1)}, u32[]{:S(2)}, u32[]{:S(2)}) collective-permute-start(f32[63,8,128]{2,1,0:T(8,128)S(1)} %get-tuple-element.74), channel_id=1, source_target_pairs={{4,8},{12,16},{20,24},{8,4},{16,12},{24,20},{5,9},{13,17},{21,25},... | collective-permute-start | bytes 774152 | tf_op jit(solution)/shard_map/ppermute | solution.py:434
  16.9 2.6 %shard_map.62 = (f32[24,96,128]{2,1,0:T(8,128)S(1)}, f32[24,384,128]{2,1,0:T(8,128)S(1)}, f32[8,8,128]{2,1,0:T(8,128)S(1)}, f32[32,768]{1,0:T(8,128)S(1)}, f32[2...) custom-call(f32[48,3072]{1,0:T(8,128)S(1)} %get-tuple-element.52.pan, ...), custom_call_target="tpu_custom_call", output_to_operand_aliasing={{4}: (7, {}), {5}: (8, {})} | custom-call | flops 2000000000 | bytes 8000000 | tf_op jit(solution)/shard_map/pallas_call | solution.py:681
  19.5 2.9 %collective-permute-start.5 = (f32[24,8,128]{2,1,0:T(8,128)S(1)}, f32[24,8,128]{2,1,0:T(8,128)S(1)}, u32[]{:S(2)}, u32[]{:S(2)}) collective-permute-start(f32[24,8,128]{2,1,0:T(8,128)S(1)} %get-tuple-element.77), channel_id=1, source_target_pairs={{0,4},{4,0},{8,12},{12,8},{16,20},{20,16},{24,28},{28,24},{1,5},{5... | collective-permute-start | bytes 294920 | tf_op jit(solution)/shard_map/ppermute | solution.py:435
  22.4 0.7 %collective-permute-start.6 = (f32[24,8,128]{2,1,0:T(8,128)S(1)}, f32[24,8,128]{2,1,0:T(8,128)S(1)}, u32[]{:S(2)}, u32[]{:S(2)}) collective-permute-start(f32[24,8,128]{2,1,0:T(8,128)S(1)} %get-tuple-element.78), channel_id=1, source_target_pairs={{4,8},{12,16},{20,24},{8,4},{16,12},{24,20},{5,9},{13,17},{21,25},... | collective-permute-start | bytes 294920 | tf_op jit(solution)/shard_map/ppermute | solution.py:434
  23.1 0.6 %shard_map.63 = (f32[4,8,896]{2,1,0:T(8,128)S(1)}, f32[64,768]{1,0:T(8,128)S(1)}, f32[12,8,896]{2,1,0:T(8,128)S(1)}) custom-call(f32[12,8,896]{2,1,0:T(8,128)S(1)} %get-tuple-element.59.x_ref, bf16[7296,256]{1,0:T(8,128)(2,1)S(1)} %get-tuple-element.53.table_ref), custom_call_target="tpu_custom_call" | custom-call | flops 200000000 | bytes 3000000 | tf_op jit(solution)/shard_map/pallas_call | solution.py:715
  23.6 0.0 collective-permute-done.3.rest_in_ref
  23.6 0.0 collective-permute-done.4.rest_out_ref
  23.7 2.1 %shard_map.64 = (f32[2,128]{1,0:T(2,128)S(1)}, f32[24,64,128]{2,1,0:T(8,128)S(1)}, f32[96,768]{1,0:T(8,128)S(1)}, f32[16,768]{1,0:T(8,128)S(1)}, f32[12,8,768]{2,1,0:T(8,128)S(1)}) custom-call(f32[12,8,896]{2,1,0:T(8,128)S(1)} %get-tuple-element.59.x_ref, f32[24,96,128]{2,1,0:T(8,128)S(1)} %get-tuple-element.66.y_ref, ...), custom_call_target="tpu_custom_call" | custom-call | flops 1000000000 | bytes 8000000 | tf_op jit(solution)/shard_map/pallas_call | solution.py:894
  25.8 0.0 collective-permute-done.5.low_in_ref
  25.8 0.0 collective-permute-done.6.low_out_ref
  25.8 14.0 %all_to_all.5.sums_ref = f32[32,2,128]{2,1,0:T(2,128)S(1)} all-to-all(f32[32,2,128]{2,1,0:T(2,128)S(1)} %broadcast_in_dim.2), channel_id=1, replica_groups=mesh['rows'=8,'band'=4] {'rows','band'}, dimensions={0} | all-to-all | bytes 65536 | tf_op jit(solution)/shard_map/all_to_all | solution.py:915
  39.8 2.9 %shard_map.65 = (f32[8,48,3072]{2,1,0:T(8,128)}, f32[12,8,768]{2,1,0:T(8,128)}) custom-call(f32[32,2,128]{2,1,0:T(2,128)S(1)} %all_to_all.5.sums_ref, f32[24,64,128]{2,1,0:T(8,128)S(1)} %get-tuple-element.80.yh_ref, f32[24,384,128]{2,1,0:T(8,128)S(1)} %get-tuple-element.81.v_ref, f32[24,48,128]{2,1,0:T(8,128)S(1)} %get-tuple-element.82.diff_ref, ...), custom_call_target="tpu_custom_call" | custom-call | flops 100000000 | bytes 8000000 | tf_op jit(solution)/shard_map/pallas_call | solution.py:1046
  (1 shorter events, 0.0 us)
Async XLA Ops:
  1.9 13.4 %collective-permute-start = (f32[15,2,768]{2,1,0:T(2,128)S(1)}, f32[15,2,768]{2,1,0:T(2,128)S(1)}, u32[]{:S(2)}, u32[]{:S(2)}) collective-permute-start(f32[15,2,768]{2,1,0:T(2,128)S(1)} %get-tuple-element.56), channel_id=1, source_target_pairs={{0,1},{1,2},{2,3},{3,0},{4,5},{5,6},{6,7},{7,4},{8,9},{9,10},{10,1... | collective-permute-start | bytes 276488 | tf_op jit(solution)/shard_map/ppermute | solution.py:382
  5.0 10.4 %collective-permute-start.2 = (f32[15,2,768]{2,1,0:T(2,128)S(1)}, f32[15,2,768]{2,1,0:T(2,128)S(1)}, u32[]{:S(2)}, u32[]{:S(2)}) collective-permute-start(f32[15,2,768]{2,1,0:T(2,128)S(1)} %get-tuple-element.58), channel_id=1, source_target_pairs={{0,3},{1,0},{2,1},{3,2},{4,7},{5,4},{6,5},{7,6},{8,11},{9,8},{10,9... | collective-permute-start | bytes 276488 | tf_op jit(solution)/shard_map/ppermute | solution.py:382
  7.1 8.3 %collective-permute-start.1 = (f32[14,2,768]{2,1,0:T(2,128)S(1)}, f32[14,2,768]{2,1,0:T(2,128)S(1)}, u32[]{:S(2)}, u32[]{:S(2)}) collective-permute-start(f32[14,2,768]{2,1,0:T(2,128)S(1)} %get-tuple-element.57), channel_id=1, source_target_pairs={{0,2},{1,3},{2,0},{3,1},{4,6},{5,7},{6,4},{7,5},{8,10},{9,11},{10,... | collective-permute-start | bytes 258056 | tf_op jit(solution)/shard_map/ppermute | solution.py:382
  16.2 7.5 %collective-permute-start.3 = (f32[63,8,128]{2,1,0:T(8,128)S(1)}, f32[63,8,128]{2,1,0:T(8,128)S(1)}, u32[]{:S(2)}, u32[]{:S(2)}) collective-permute-start(f32[63,8,128]{2,1,0:T(8,128)S(1)} %get-tuple-element.73), channel_id=1, source_target_pairs={{0,4},{4,0},{8,12},{12,8},{16,20},{20,16},{24,28},{28,24},{1,5},{5... | collective-permute-start | bytes 774152 | tf_op jit(solution)/shard_map/ppermute | solution.py:435
  16.3 7.4 %collective-permute-start.4 = (f32[63,8,128]{2,1,0:T(8,128)S(1)}, f32[63,8,128]{2,1,0:T(8,128)S(1)}, u32[]{:S(2)}, u32[]{:S(2)}) collective-permute-start(f32[63,8,128]{2,1,0:T(8,128)S(1)} %get-tuple-element.74), channel_id=1, source_target_pairs={{4,8},{12,16},{20,24},{8,4},{16,12},{24,20},{5,9},{13,17},{21,25},... | collective-permute-start | bytes 774152 | tf_op jit(solution)/shard_map/ppermute | solution.py:434
  19.5 6.3 %collective-permute-start.5 = (f32[24,8,128]{2,1,0:T(8,128)S(1)}, f32[24,8,128]{2,1,0:T(8,128)S(1)}, u32[]{:S(2)}, u32[]{:S(2)}) collective-permute-start(f32[24,8,128]{2,1,0:T(8,128)S(1)} %get-tuple-element.77), channel_id=1, source_target_pairs={{0,4},{4,0},{8,12},{12,8},{16,20},{20,16},{24,28},{28,24},{1,5},{5... | collective-permute-start | bytes 294920 | tf_op jit(solution)/shard_map/ppermute | solution.py:435
  22.4 3.4 %collective-permute-start.6 = (f32[24,8,128]{2,1,0:T(8,128)S(1)}, f32[24,8,128]{2,1,0:T(8,128)S(1)}, u32[]{:S(2)}, u32[]{:S(2)}) collective-permute-start(f32[24,8,128]{2,1,0:T(8,128)S(1)} %get-tuple-element.78), channel_id=1, source_target_pairs={{4,8},{12,16},{20,24},{8,4},{16,12},{24,20},{5,9},{13,17},{21,25},... | collective-permute-start | bytes 294920 | tf_op jit(solution)/shard_map/ppermute | solution.py:434

commit v10 on v9

--- a/solution.py
+++ b/solution.py
@@ -674,7 +674,9 @@
             return tuple(accs) + (accv, accp)
 
         zero = jnp.zeros((8, LANES), F32)
-        first = lax.fori_loop(0, fine_tiles // 2, grouped(tile_step, 2), (zero,) * (turns + 2))
+        first = (zero,) * (turns + 2)
+        for k in range(fine_tiles):
+            first = tile_step(k, first)
         for i in range(turns + 2):
             acc_out[i] = first[i]
 

time: 43 us -> 43.1 us (level)
  no operation moved by 1% of the time
where the time goes in v10:
time: 43.1 us; the launch traced here: 42.9 us
  Pallas kernels  14.4 us (33%)
  blocking collectives  14 us (32%)
  starting transfers between devices  10.4 us (24%)
  waiting for transfers between devices  3.38 us (8%)
  between operations  0.72 us (2%)
    all_to_all x1, blocking collectives, local(): lax.all_to_all(spread, ('rows', 'band'), split_axis=0, concat_axis=0, til...  14 us
    ppermute x3, starting transfers between devices, local(): lax.ppermute(chunks[d], 'band', [(i, (i + d) % groups) for i in range(gro...  6.11 us
    pallas_call x1, Pallas kernels, local(): call(early, (shape(h, w), jax.ShapeDtypeStruct(table.shape, BF16), shape(...  3.94 us
    ppermute x3, waiting for transfers between devices, local(): lax.ppermute(chunks[d], 'band', [(i, (i + d) % groups) for i in range(gro...  3.37 us
    ppermute x2, starting transfers between devices, trade(): return (lax.ppermute(inner, 'rows', pairs_in), outer)  2.96 us
    pallas_call x1, Pallas kernels, local(): call(finish, (shape(BANDS, h, w), shape(hc, BANDS, wc)), [pltpu.VMEM((fin...  2.94 us
    pallas_call x1, Pallas kernels, local(): call(inside, (shape(fine_tiles, 8 * hc, LANES), shape(fine_tiles, 8 * h,...  2.69 us
    pallas_call x1, Pallas kernels, local(): call(moments, (shape(2, LANES), shape(fine_tiles, 8 * len(around), LANES)...  2.15 us
  transfers between devices with their start and end apart: 7, of which 1 were waited for; matrix products, arithmetic and copies ran while one was open for 0% of the time, Pallas kernels for 22%

profile of v10, /device:TPU:0, one launch (start us, length us, event | category | flops | bytes accessed | tf_op | source)
XLA Modules:
  0.0 42.9 jit_solution(15810143594614150732)
XLA Ops:
  0.6 1.3 %shard_map.59 = (f32[14,2,768]{2,1,0:T(2,128)S(1)}, f32[15,2,768]{2,1,0:T(2,128)S(1)}, f32[14,2,768]{2,1,0:T(2,128)S(1)}, f32[15,2,768]{2,1,0:T(2,128)S(1)}) custom-call(f32[48,3072]{1,0:T(8,128)} %pan_far, f32[12,2,3072]{2,1,0:T(2,128)} %bitcast.2, f32[2,4,1024]{2,1,0:T(4,128)} %swir_ref.1), custom_call_target="tpu_custom_call" | custom-call | bytes 8000000 | tf_op jit(solution)/shard_map/pallas_call | solution.py:368
  1.9 3.1 %collective-permute-start = (f32[15,2,768]{2,1,0:T(2,128)S(1)}, f32[15,2,768]{2,1,0:T(2,128)S(1)}, u32[]{:S(2)}, u32[]{:S(2)}) collective-permute-start(f32[15,2,768]{2,1,0:T(2,128)S(1)} %get-tuple-element.56), channel_id=1, source_target_pairs={{0,1},{1,2},{2,3},{3,0},{4,5},{5,6},{6,7},{7,4},{8,9},{9,10},{10,1... | collective-permute-start | bytes 276488 | tf_op jit(solution)/shard_map/ppermute | solution.py:382
  5.0 2.1 %collective-permute-start.2 = (f32[15,2,768]{2,1,0:T(2,128)S(1)}, f32[15,2,768]{2,1,0:T(2,128)S(1)}, u32[]{:S(2)}, u32[]{:S(2)}) collective-permute-start(f32[15,2,768]{2,1,0:T(2,128)S(1)} %get-tuple-element.58), channel_id=1, source_target_pairs={{0,3},{1,0},{2,1},{3,2},{4,7},{5,4},{6,5},{7,6},{8,11},{9,8},{10,9... | collective-permute-start | bytes 276488 | tf_op jit(solution)/shard_map/ppermute | solution.py:382
  7.1 0.9 %collective-permute-start.1 = (f32[14,2,768]{2,1,0:T(2,128)S(1)}, f32[14,2,768]{2,1,0:T(2,128)S(1)}, u32[]{:S(2)}, u32[]{:S(2)}) collective-permute-start(f32[14,2,768]{2,1,0:T(2,128)S(1)} %get-tuple-element.57), channel_id=1, source_target_pairs={{0,2},{1,3},{2,0},{3,1},{4,6},{5,7},{6,4},{7,5},{8,10},{9,11},{10,... | collective-permute-start | bytes 258056 | tf_op jit(solution)/shard_map/ppermute | solution.py:382
  8.1 3.9 %shard_map.60 = (f32[48,3072]{1,0:T(8,128)S(1)}, bf16[7296,256]{1,0:T(8,128)(2,1)S(1)}, f32[64,640]{1,0:T(8,128)S(1)}, f32[16,2560]{1,0:T(8,128)S(1)}, f32[24,48...) custom-call(f32[48,3072]{1,0:T(8,128)} %pan_far, bf16[7296,256]{1,0:T(8,128)(2,1)} %constant.2.clone.table_far), custom_call_target="tpu_custom_call" | custom-call | flops 2000000000 | bytes 8000000 | tf_op jit(solution)/shard_map/pallas_call | solution.py:488
  12.0 3.4 %collective-permute-done.1.rest_2_ = f32[14,2,768]{2,1,0:T(2,128)S(1)} collective-permute-done((f32[14,2,768]{2,1,0:T(2,128)S(1)}, f32[14,2,768]{2,1,0:T(2,128)S(1)}, u32[]{:S(2)}, u32[]{:S(2)}) %collective-permute-start.1) | collective-permute-done | bytes 86048 | tf_op jit(solution)/shard_map/ppermute | solution.py:382
  15.4 0.0 collective-permute-done.rest_1_
  15.4 0.0 collective-permute-done.2.rest_3_
  15.4 0.8 %shard_map.61 = (f32[12,8,896]{2,1,0:T(8,128)S(1)}, f32[4,8,384]{2,1,0:T(8,128)S(1)}, f32[32,256]{1,0:T(8,128)S(1)}, f32[64,512]{1,0:T(8,128)S(1)}, f32[48,512]{...) custom-call(f32[48,3072]{1,0:T(8,128)S(1)} %get-tuple-element.52.pan_ref, ...), custom_call_target="tpu_custom_call" | custom-call | flops 200000000 | bytes 3000000 | tf_op jit(solution)/shard_map/pallas_call | solution.py:584
  16.2 0.1 collective-permute-start.3
  16.3 0.7 %collective-permute-start.4 = (f32[63,8,128]{2,1,0:T(8,128)S(1)}, f32[63,8,128]{2,1,0:T(8,128)S(1)}, u32[]{:S(2)}, u32[]{:S(2)}) collective-permute-start(f32[63,8,128]{2,1,0:T(8,128)S(1)} %get-tuple-element.74), channel_id=1, source_target_pairs={{4,8},{12,16},{20,24},{8,4},{16,12},{24,20},{5,9},{13,17},{21,25},... | collective-permute-start | bytes 774152 | tf_op jit(solution)/shard_map/ppermute | solution.py:434
  16.9 2.7 %shard_map.62 = (f32[24,96,128]{2,1,0:T(8,128)S(1)}, f32[24,384,128]{2,1,0:T(8,128)S(1)}, f32[8,8,128]{2,1,0:T(8,128)S(1)}, f32[32,768]{1,0:T(8,128)S(1)}, f32[2...) custom-call(f32[48,3072]{1,0:T(8,128)S(1)} %get-tuple-element.52.pan, ...), custom_call_target="tpu_custom_call", output_to_operand_aliasing={{4}: (7, {}), {5}: (8, {})} | custom-call | flops 2000000000 | bytes 8000000 | tf_op jit(solution)/shard_map/pallas_call | solution.py:683
  19.6 2.9 %collective-permute-start.5 = (f32[24,8,128]{2,1,0:T(8,128)S(1)}, f32[24,8,128]{2,1,0:T(8,128)S(1)}, u32[]{:S(2)}, u32[]{:S(2)}) collective-permute-start(f32[24,8,128]{2,1,0:T(8,128)S(1)} %get-tuple-element.77), channel_id=1, source_target_pairs={{0,4},{4,0},{8,12},{12,8},{16,20},{20,16},{24,28},{28,24},{1,5},{5... | collective-permute-start | bytes 294920 | tf_op jit(solution)/shard_map/ppermute | solution.py:435
  22.5 0.7 %collective-permute-start.6 = (f32[24,8,128]{2,1,0:T(8,128)S(1)}, f32[24,8,128]{2,1,0:T(8,128)S(1)}, u32[]{:S(2)}, u32[]{:S(2)}) collective-permute-start(f32[24,8,128]{2,1,0:T(8,128)S(1)} %get-tuple-element.78), channel_id=1, source_target_pairs={{4,8},{12,16},{20,24},{8,4},{16,12},{24,20},{5,9},{13,17},{21,25},... | collective-permute-start | bytes 294920 | tf_op jit(solution)/shard_map/ppermute | solution.py:434
  23.2 0.6 %shard_map.63 = (f32[4,8,896]{2,1,0:T(8,128)S(1)}, f32[64,768]{1,0:T(8,128)S(1)}, f32[12,8,896]{2,1,0:T(8,128)S(1)}) custom-call(f32[12,8,896]{2,1,0:T(8,128)S(1)} %get-tuple-element.59.x_ref, bf16[7296,256]{1,0:T(8,128)(2,1)S(1)} %get-tuple-element.53.table_ref), custom_call_target="tpu_custom_call" | custom-call | flops 200000000 | bytes 3000000 | tf_op jit(solution)/shard_map/pallas_call | solution.py:717
  23.7 0.0 collective-permute-done.3.rest_in_ref
  23.8 0.0 collective-permute-done.4.rest_out_ref
  23.8 2.1 %shard_map.64 = (f32[2,128]{1,0:T(2,128)S(1)}, f32[24,64,128]{2,1,0:T(8,128)S(1)}, f32[96,768]{1,0:T(8,128)S(1)}, f32[16,768]{1,0:T(8,128)S(1)}, f32[12,8,768]{2,1,0:T(8,128)S(1)}) custom-call(f32[12,8,896]{2,1,0:T(8,128)S(1)} %get-tuple-element.59.x_ref, f32[24,96,128]{2,1,0:T(8,128)S(1)} %get-tuple-element.66.y_ref, ...), custom_call_target="tpu_custom_call" | custom-call | flops 1000000000 | bytes 8000000 | tf_op jit(solution)/shard_map/pallas_call | solution.py:896
  25.9 0.0 collective-permute-done.5.low_in_ref
  25.9 0.0 collective-permute-done.6.low_out_ref
  25.9 14.0 %all_to_all.5.sums_ref = f32[32,2,128]{2,1,0:T(2,128)S(1)} all-to-all(f32[32,2,128]{2,1,0:T(2,128)S(1)} %broadcast_in_dim.2), channel_id=1, replica_groups=mesh['rows'=8,'band'=4] {'rows','band'}, dimensions={0} | all-to-all | bytes 65536 | tf_op jit(solution)/shard_map/all_to_all | solution.py:917
  39.9 2.9 %shard_map.65 = (f32[8,48,3072]{2,1,0:T(8,128)}, f32[12,8,768]{2,1,0:T(8,128)}) custom-call(f32[32,2,128]{2,1,0:T(2,128)S(1)} %all_to_all.5.sums_ref, f32[24,64,128]{2,1,0:T(8,128)S(1)} %get-tuple-element.80.yh_ref, f32[24,384,128]{2,1,0:T(8,128)S(1)} %get-tuple-element.81.v_ref, f32[24,48,128]{2,1,0:T(8,128)S(1)} %get-tuple-element.82.diff_ref, ...), custom_call_target="tpu_custom_call" | custom-call | flops 100000000 | bytes 8000000 | tf_op jit(solution)/shard_map/pallas_call | solution.py:1048
  (1 shorter events, 0.0 us)
Async XLA Ops:
  1.9 13.4 %collective-permute-start = (f32[15,2,768]{2,1,0:T(2,128)S(1)}, f32[15,2,768]{2,1,0:T(2,128)S(1)}, u32[]{:S(2)}, u32[]{:S(2)}) collective-permute-start(f32[15,2,768]{2,1,0:T(2,128)S(1)} %get-tuple-element.56), channel_id=1, source_target_pairs={{0,1},{1,2},{2,3},{3,0},{4,5},{5,6},{6,7},{7,4},{8,9},{9,10},{10,1... | collective-permute-start | bytes 276488 | tf_op jit(solution)/shard_map/ppermute | solution.py:382
  5.0 10.4 %collective-permute-start.2 = (f32[15,2,768]{2,1,0:T(2,128)S(1)}, f32[15,2,768]{2,1,0:T(2,128)S(1)}, u32[]{:S(2)}, u32[]{:S(2)}) collective-permute-start(f32[15,2,768]{2,1,0:T(2,128)S(1)} %get-tuple-element.58), channel_id=1, source_target_pairs={{0,3},{1,0},{2,1},{3,2},{4,7},{5,4},{6,5},{7,6},{8,11},{9,8},{10,9... | collective-permute-start | bytes 276488 | tf_op jit(solution)/shard_map/ppermute | solution.py:382
  7.1 8.3 %collective-permute-start.1 = (f32[14,2,768]{2,1,0:T(2,128)S(1)}, f32[14,2,768]{2,1,0:T(2,128)S(1)}, u32[]{:S(2)}, u32[]{:S(2)}) collective-permute-start(f32[14,2,768]{2,1,0:T(2,128)S(1)} %get-tuple-element.57), channel_id=1, source_target_pairs={{0,2},{1,3},{2,0},{3,1},{4,6},{5,7},{6,4},{7,5},{8,10},{9,11},{10,... | collective-permute-start | bytes 258056 | tf_op jit(solution)/shard_map/ppermute | solution.py:382
  16.2 7.6 %collective-permute-start.3 = (f32[63,8,128]{2,1,0:T(8,128)S(1)}, f32[63,8,128]{2,1,0:T(8,128)S(1)}, u32[]{:S(2)}, u32[]{:S(2)}) collective-permute-start(f32[63,8,128]{2,1,0:T(8,128)S(1)} %get-tuple-element.73), channel_id=1, source_target_pairs={{0,4},{4,0},{8,12},{12,8},{16,20},{20,16},{24,28},{28,24},{1,5},{5... | collective-permute-start | bytes 774152 | tf_op jit(solution)/shard_map/ppermute | solution.py:435
  16.3 7.5 %collective-permute-start.4 = (f32[63,8,128]{2,1,0:T(8,128)S(1)}, f32[63,8,128]{2,1,0:T(8,128)S(1)}, u32[]{:S(2)}, u32[]{:S(2)}) collective-permute-start(f32[63,8,128]{2,1,0:T(8,128)S(1)} %get-tuple-element.74), channel_id=1, source_target_pairs={{4,8},{12,16},{20,24},{8,4},{16,12},{24,20},{5,9},{13,17},{21,25},... | collective-permute-start | bytes 774152 | tf_op jit(solution)/shard_map/ppermute | solution.py:434
  19.6 6.3 %collective-permute-start.5 = (f32[24,8,128]{2,1,0:T(8,128)S(1)}, f32[24,8,128]{2,1,0:T(8,128)S(1)}, u32[]{:S(2)}, u32[]{:S(2)}) collective-permute-start(f32[24,8,128]{2,1,0:T(8,128)S(1)} %get-tuple-element.77), channel_id=1, source_target_pairs={{0,4},{4,0},{8,12},{12,8},{16,20},{20,16},{24,28},{28,24},{1,5},{5... | collective-permute-start | bytes 294920 | tf_op jit(solution)/shard_map/ppermute | solution.py:435
  22.5 3.4 %collective-permute-start.6 = (f32[24,8,128]{2,1,0:T(8,128)S(1)}, f32[24,8,128]{2,1,0:T(8,128)S(1)}, u32[]{:S(2)}, u32[]{:S(2)}) collective-permute-start(f32[24,8,128]{2,1,0:T(8,128)S(1)} %get-tuple-element.78), channel_id=1, source_target_pairs={{4,8},{12,16},{20,24},{8,4},{16,12},{24,20},{5,9},{13,17},{21,25},... | collective-permute-start | bytes 294920 | tf_op jit(solution)/shard_map/ppermute | solution.py:434
